TPU v7x, 256 devices: a whole 4x4x8 slice. The times are simulated.
256 devices in a mesh: space: 64 (over y, z, core), dp: 4 (over x).
Axes of the slice: x: 4, y: 4, z: 8, core: 2. Of those that a mesh axis runs over, the one named last changes fastest.
Arguments:
- inputs: bfloat16 [4, 64, 2, 16, 64, 128], P('dp', 'space'), may hold values from -6 to 6
- depth_one: bfloat16 [3, 3, 3, 128], replicated, may hold values from -1.25 to 1.25
- point_one: bfloat16 [128, 128], replicated, may hold values from -0.5 to 0.5
- depth_two: bfloat16 [3, 3, 3, 128], replicated, may hold values from -1.25 to 1.25
- point_two: bfloat16 [128, 128], replicated, may hold values from -0.5 to 0.5
- cotangent: bfloat16 [4, 64, 2, 16, 64, 128], P('dp', 'space'), may hold values from -6 to 6
Outputs:
- grad_input: bfloat16 [4, 64, 2, 16, 64, 128], P('dp', 'space')
- grad_depth_one: float32 [3, 3, 3, 128], replicated
- grad_point_one: float32 [128, 128], replicated
- grad_depth_two: float32 [3, 3, 3, 128], replicated
- grad_point_two: float32 [128, 128], replicated
All inputs are finite; a program needn't handle non-finite values.
Results may differ from a plain program's by a relative error of at most 0.0068.
Values may be sent and summed in bfloat16 or wider, within the bound.
No kernel may reach another device: no remote copies, remote signals or barrier semaphores. Data moves between devices by JAX's collectives and lax.ppermute only.
A program may use at most 64 MiB of HBM per device.

v0:
```python
import math

import jax
import jax.numpy as jnp
from jax import lax
from jax.sharding import PartitionSpec as P


def passed_along(block, axis, distance):
    devices = range(lax.axis_size(axis))
    route = [(i - distance, i) for i in devices if i - distance in devices]
    return lax.ppermute(block, axis, route)


def cut_along(array, dim, count):
    before, after = (array.shape[:dim], array.shape[dim + 1 :])
    return jnp.moveaxis(array.reshape(*before, count, -1, *after), dim, 0)


def sent_and_summed(array, axis, dim):
    tiles = cut_along(array, dim, lax.axis_size(axis))
    arrived = lax.all_to_all(tiles, axis, split_axis=0, concat_axis=0, tiled=True)
    return arrived.sum(axis=0)


def from_everyone(array, axis):
    copies = jnp.broadcast_to(array, (lax.axis_size(axis), *array.shape))
    return lax.all_to_all(copies, axis, split_axis=0, concat_axis=0, tiled=True)


def taken_together(array, axis):
    return from_everyone(array, axis).sum(axis=0)


def in_order(tiles, dim):
    tiles = jnp.moveaxis(tiles, 0, dim)
    dims = tiles.shape
    return tiles.reshape(*dims[:dim], dims[dim] * dims[dim + 1], *dims[dim + 2 :])


def gather_directly(array, axis, dim):
    tiles = from_everyone(array, axis)
    return in_order(tiles, dim)


def depthwise(volume, kernel):
    count_x = volume.shape[1] - 2
    count_y = volume.shape[2] - 2
    wide_z = volume.shape[3]
    padded = jnp.pad(volume, ((0, 0), (0, 0), (0, 0), (1, 1), (0, 0)))
    weights = kernel.astype(jnp.float32)
    total = jnp.zeros((volume.shape[0], count_x, count_y, wide_z, volume.shape[4]), jnp.float32)
    for tap_x in range(3):
        for tap_y in range(3):
            for tap_z in range(3):
                total = (
                    total
                    + padded[
                        :, tap_x : tap_x + count_x, tap_y : tap_y + count_y, tap_z : tap_z + wide_z
                    ].astype(jnp.float32)
                    * weights[tap_x, tap_y, tap_z]
                )
    return total


def depthwise_t(volume, kernel):
    count_x = volume.shape[1] - 2
    count_y = volume.shape[2] - 2
    wide_z = volume.shape[3]
    padded = jnp.pad(volume, ((0, 0), (0, 0), (0, 0), (1, 1), (0, 0)))
    weights = kernel.astype(jnp.float32)
    total = jnp.zeros((volume.shape[0], count_x, count_y, wide_z, volume.shape[4]), jnp.float32)
    for tap_x in range(3):
        for tap_y in range(3):
            for tap_z in range(3):
                total = (
                    total
                    + padded[
                        :,
                        2 - tap_x : 2 - tap_x + count_x,
                        2 - tap_y : 2 - tap_y + count_y,
                        2 - tap_z : 2 - tap_z + wide_z,
                    ].astype(jnp.float32)
                    * weights[tap_x, tap_y, tap_z]
                )
    return total


def kernel_grad(volume, upstream):
    count_x = upstream.shape[1]
    count_y = upstream.shape[2]
    wide_z = upstream.shape[3]
    padded = jnp.pad(volume, ((0, 0), (0, 0), (0, 0), (1, 1), (0, 0)))
    rows = []
    for tap_x in range(3):
        for tap_y in range(3):
            for tap_z in range(3):
                window = padded[
                    :, tap_x : tap_x + count_x, tap_y : tap_y + count_y, tap_z : tap_z + wide_z
                ]
                rows.append(
                    jnp.einsum(
                        "sxyzc,sxyzc->c", window, upstream, preferred_element_type=jnp.float32
                    )
                )
    return jnp.stack(rows).reshape(3, 3, 3, upstream.shape[4])


def silu_slope(value):
    sigma = jax.nn.sigmoid(value)
    return sigma * (1.0 + value * (1.0 - sigma))


def channel_mix(volume, matrix):
    return jnp.einsum("sxyzc,cd->sxyzd", volume, matrix, preferred_element_type=jnp.float32)


def channel_back(volume, matrix):
    return jnp.einsum("sxyzd,cd->sxyzc", volume, matrix, preferred_element_type=jnp.float32)


def outer_sum(left, right):
    return jnp.einsum("sxyzc,sxyzd->cd", left, right, preferred_element_type=jnp.float32)


def frame_one(field):
    widened = jnp.pad(field, ((0, 0), (0, 0), (1, 1), (0, 0), (0, 0)))
    below = passed_along(widened[:, -1:], "space", 1)
    above = passed_along(widened[:, :1], "space", -1)
    return jnp.concatenate([below, widened, above], axis=1)


def on_device(inputs, depth_one, point_one, depth_two, point_two, cotangent):
    block_in = inputs[:, 0]
    block_up = cotangent[:, 0]
    size_x = block_in.shape[1]
    size_y = block_in.shape[2]
    channels = block_in.shape[4]
    x_framed = frame_one(block_in)
    mixed_one = depthwise(x_framed, depth_one).astype(jnp.bfloat16)
    pre_act = channel_mix(mixed_one, point_one)
    hidden = jax.nn.silu(pre_act).astype(jnp.bfloat16)
    hidden_framed = frame_one(hidden)
    mixed_two = depthwise(hidden_framed, depth_two).astype(jnp.bfloat16)
    g_point_two = outer_sum(mixed_two, block_up)
    back_two = channel_back(block_up, point_two).astype(jnp.bfloat16)
    g_depth_two = kernel_grad(hidden_framed, back_two)
    back_two_framed = frame_one(back_two)
    carried = depthwise_t(back_two_framed, depth_two)
    scaled = (carried * silu_slope(pre_act)).astype(jnp.bfloat16)
    g_point_one = outer_sum(mixed_one, scaled)
    back_one = channel_back(scaled, point_one).astype(jnp.bfloat16)
    g_depth_one = kernel_grad(x_framed, back_one)
    back_one_framed = frame_one(back_one)
    grad_block = depthwise_t(back_one_framed, depth_one).astype(jnp.bfloat16)
    total_cells = (
        block_in.shape[0]
        * lax.axis_size("dp")
        * lax.axis_size("space")
        * size_x
        * size_y
        * block_in.shape[3]
    )
    factor = 1.0 / math.sqrt(total_cells)
    depth_size = 27 * channels
    point_size = channels * channels
    flat_terms = jnp.concatenate(
        [
            g_depth_one.reshape(-1),
            g_point_one.reshape(-1),
            g_depth_two.reshape(-1),
            g_point_two.reshape(-1),
        ]
    )
    share = sent_and_summed(flat_terms, "space", 0)
    share = taken_together(share, "dp")
    flat_sums = gather_directly(share, "space", 0)
    g_depth_one = flat_sums[:depth_size].reshape(3, 3, 3, channels)
    g_point_one = flat_sums[depth_size : depth_size + point_size].reshape(channels, channels)
    g_depth_two = flat_sums[depth_size + point_size : 2 * depth_size + point_size].reshape(
        3, 3, 3, channels
    )
    g_point_two = flat_sums[2 * depth_size + point_size :].reshape(channels, channels)
    return (
        grad_block[:, None],
        g_depth_one * factor,
        g_point_one * factor,
        g_depth_two * factor,
        g_point_two * factor,
    )


def solution(mesh):
    placed = (
        P("dp", "space", None, None, None, None),
        P(),
        P(),
        P(),
        P(),
        P("dp", "space", None, None, None, None),
    )
    return jax.shard_map(
        on_device,
        mesh=mesh,
        in_specs=placed,
        out_specs=(P("dp", "space", None, None, None, None), P(), P(), P(), P()),
        check_vma=False,
    )
```

profile of v0, /device:TPU:1, one launch (start us, length us, event | category | flops | bytes accessed | tf_op | source)
XLA Modules:
  0.0 121.6 jit_solution(15774153613167835404)
XLA Ops:
  0.6 0.0 copy-start
  0.7 1.0 copy-done
  1.7 1.0 convolution_convert_fusion.1
  2.7 0.0 copy-start.5
  2.7 0.0 copy-start.6
  2.8 0.1 pad_slice_fusion.36
  2.8 5.1 %collective-permute-start.1 = (bf16[1,1,18,64,128]{4,3,2,1,0:T(8,128)(2,1)S(1)}, bf16[1,1,18,64,128]{4,3,2,1,0:T(8,128)(2,1)S(1)}, u32[]{:S(2)}, u32[]{:S(2)}) collective-permute-start(bf16[1,1,18,64,128]{4,3,2,1,0:T(8,128)(2,1)S(1)} %get-tuple-element.73), channel_id=1, source_target_pairs={{4,0},{8,4},{12,8},{16,12},{20,16},{24,20},{28,24},{32,28},{36,32}... | collective-permute-start | bytes 884744 | tf_op jit(solution)/shard_map/ppermute | solution.py:12
  8.0 1.9 %collective-permute-start = (bf16[1,1,18,64,128]{4,3,2,1,0:T(8,128)(2,1)S(1)}, bf16[1,1,18,64,128]{4,3,2,1,0:T(8,128)(2,1)S(1)}, u32[]{:S(2)}, u32[]{:S(2)}) collective-permute-start(bf16[1,1,18,64,128]{4,3,2,1,0:T(8,128)(2,1)S(1)} %get-tuple-element.74), channel_id=1, source_target_pairs={{0,4},{4,8},{8,12},{12,16},{16,20},{20,24},{24,28},{28,32},{32,36}... | collective-permute-start | bytes 884744 | tf_op jit(solution)/shard_map/ppermute | solution.py:12
  9.9 0.1 pad_slice_fusion.33
  10.0 2.2 %collective-permute-start.2 = (bf16[1,1,18,64,128]{4,3,2,1,0:T(8,128)(2,1)S(1)}, bf16[1,1,18,64,128]{4,3,2,1,0:T(8,128)(2,1)S(1)}, u32[]{:S(2)}, u32[]{:S(2)}) collective-permute-start(bf16[1,1,18,64,128]{4,3,2,1,0:T(8,128)(2,1)S(1)} %get-tuple-element.75), channel_id=1, source_target_pairs={{0,4},{4,8},{8,12},{12,16},{16,20},{20,24},{24,28},{28,32},{32,36}... | collective-permute-start | bytes 884744 | tf_op jit(solution)/shard_map/ppermute | solution.py:12
  12.2 2.1 %collective-permute-start.3 = (bf16[1,1,18,64,128]{4,3,2,1,0:T(8,128)(2,1)S(1)}, bf16[1,1,18,64,128]{4,3,2,1,0:T(8,128)(2,1)S(1)}, u32[]{:S(2)}, u32[]{:S(2)}) collective-permute-start(bf16[1,1,18,64,128]{4,3,2,1,0:T(8,128)(2,1)S(1)} %get-tuple-element.76), channel_id=1, source_target_pairs={{4,0},{8,4},{12,8},{16,12},{20,16},{24,20},{28,24},{32,28},{36,32}... | collective-permute-start | bytes 884744 | tf_op jit(solution)/shard_map/ppermute | solution.py:12
  14.5 0.0 copy-start.45
  14.8 0.6 slice_bitcast_fusion.52
  15.5 0.1 pad.30
  15.5 0.1 pad.28
  15.6 1.1 collective-permute-done.2
  16.7 3.5 %collective-permute-done.3 = bf16[1,1,18,64,128]{4,3,2,1,0:T(8,128)(2,1)S(1)} collective-permute-done((bf16[1,1,18,64,128]{4,3,2,1,0:T(8,128)(2,1)S(1)}, bf16[1,1,18,64,128]{4,3,2,1,0:T(8,128)(2,1)S(1)}, u32[]{:S(2)}, u32[]{:S(2)}) %collective-permute-start.3) | collective-permute-done | bytes 294944 | tf_op jit(solution)/shard_map/ppermute | solution.py:12
  20.2 0.5 fusion.10
  20.8 0.0 collective-permute-done.1
  20.8 0.0 collective-permute-done
  20.8 0.5 fusion.8
  21.5 0.0 copy-start.65
  21.5 4.2 %add_convert_fusion = bf16[1,2,16,64,128]{4,3,2,1,0:T(8,128)(2,1)S(1)} fusion(f32[128]{0:T(128)S(1)} %get-tuple-element.109, f32[128]{0:T(128)S(1)} %get-tuple-element.110, f32[128]{0:T(128)S(1)} %get-tuple-element.111, f32[128]{0:T(128)S(1)} %get-tuple-element.112, f32[128]{0:T(128)S(1)} %get-tuple-element.113, f32[128]{0:T(128)S(1)} %get-tuple-element.114, ...), kind=kLoop, calls=%fused_computation.191 | loop fusion | flops 22806528 | bytes 12727808 | tf_op jit(solution)/shard_map/convert_element_type | solution.py:140
  26.0 4.6 %fusion.91 = (bf16[1,2,16,64,128]{4,3,2,1,0:T(8,128)(2,1)S(1)}, f32[2,16,64,128]{3,2,1,0:T(8,128)S(1)}) fusion(bf16[2,16,64,128]{3,2,1,0:T(8,128)(2,1)S(1)} %convolution_convert_fusion.1, bf16[1,2,18,64,128]{4,3,2,1,0:T(8,128)(2,1)S(1)} %pad.28, bf16[1,1,18,64,128]{4,3,2,1,0:T(8,128)(2,1)S(1)} %collective-permute-done, ...), kind=kOutput, calls=%fused_computation.174 | convolution fusion | flops 92012544 | bytes 14333440 | tf_op jit(solution)/shard_map/sxyzc,cd->sxyzd/dot_general | solution.py:115
  30.6 3.4 %fusion.36 = (f32[128]{0:T(128)S(1)}, f32[128]{0:T(128)S(1)}, f32[128]{0:T(128)S(1)}, f32[128]{0:T(128)S(1)}, f32[128]{0:T(128)S(1)}, /*index=5*/f32[128]{0:T(12...) fusion(bf16[1,4,18,66,128]{4,3,2,1,0:T(8,128)(2,1)S(1)} %fusion, ...), kind=kOutput, calls=%fused_computation.116 | convolution fusion | flops 81786624 | bytes 10527744 | tf_op jit(solution)/shard_map/sxyzd,cd->sxyzc/dot_general | solution.py:119
  34.0 0.3 fusion.161
  34.3 1.0 pad_slice_fusion.35
  35.3 1.9 %collective-permute-start.7 = (bf16[1,1,18,64,128]{4,3,2,1,0:T(8,128)(2,1)}, bf16[1,1,18,64,128]{4,3,2,1,0:T(8,128)(2,1)}, u32[]{:S(2)}, u32[]{:S(2)}) collective-permute-start(bf16[1,1,18,64,128]{4,3,2,1,0:T(8,128)(2,1)} %get-tuple-element.138), channel_id=1, source_target_pairs={{4,0},{8,4},{12,8},{16,12},{20,16},{24,20},{28,24},{32,28},{36,32}... | collective-permute-start | bytes 884744 | tf_op jit(solution)/shard_map/ppermute | solution.py:12
  37.2 3.8 %collective-permute-start.6 = (bf16[1,1,18,64,128]{4,3,2,1,0:T(8,128)(2,1)S(1)}, bf16[1,1,18,64,128]{4,3,2,1,0:T(8,128)(2,1)}, u32[]{:S(2)}, u32[]{:S(2)}) collective-permute-start(bf16[1,1,18,64,128]{4,3,2,1,0:T(8,128)(2,1)S(1)} %get-tuple-element.139), channel_id=1, source_target_pairs={{0,4},{4,8},{8,12},{12,16},{16,20},{20,24},{24,28},{28,32},{32,36}... | collective-permute-start | bytes 884744 | tf_op jit(solution)/shard_map/ppermute | solution.py:12
  41.0 1.3 %fusion.35 = (f32[128]{0:T(128)S(1)}, f32[128]{0:T(128)S(1)}, f32[128]{0:T(128)S(1)}, f32[128]{0:T(128)S(1)}, f32[128]{0:T(128)S(1)}, /*index=5*/f32[128]{0:T(12...) fusion(bf16[2,16,64,128]{3,2,1,0:T(8,128)(2,1)S(1)} %get-tuple-element.137, ...), kind=kLoop, calls=%fused_computation.115 | loop fusion | flops 8911744 | bytes 2757120 | tf_op jit(solution)/shard_map/sxyzc,sxyzc->c/dot_general | solution.py:102
  42.3 0.9 pad.34
  43.2 1.5 %stack.195 = f32[27,128]{1,0:T(8,128)S(1)} concatenate(f32[1,128]{1,0:T(1,128)} %bitcast.705, f32[1,128]{1,0:T(1,128)S(1)} %bitcast.655, f32[1,128]{1,0:T(1,128)} %bitcast.704, f32[1,128]{1,0:T(1,128)} %bitcast.703, f32[1,128]{1,0:T(1,128)S(1)} %bitcast.656, f32[1,128]{1,0:T(1,128)} %bitcast.702, f32[1,128]{1,0:T(1,128)} %bitcast.701, f32[1,128]{1,0:T(1,128)S(1)} %bitcast.657, ...), dimensions={0} | concatenate | bytes 27648 | tf_op jit(solution)/shard_map/stack | solution.py:106
  44.7 0.3 convolution_bitcast_fusion.1
  45.0 0.0 collective-permute-done.7
  45.1 0.0 collective-permute-done.6
  45.1 0.7 copy-done.2
  45.8 1.6 %select_maximum_fusion = bf16[1,4,18,66,128]{4,3,2,1,0:T(8,128)(2,1)S(1)} fusion(bf16[1,1,18,64,128]{4,3,2,1,0:T(8,128)(2,1)} %collective-permute-done.7, bf16[1,2,18,64,128]{4,3,2,1,0:T(8,128)(2,1)S(1)} %copy-done.2, bf16[1,1,18,64,128]{4,3,2,1,0:T(8,128)(2,1)} %collective-permute-done.6), kind=kLoop, calls=%fused_computation.59 | loop fusion | flops 7299072 | bytes 2396160 | tf_op jit(solution)/shard_map/concatenate | solution.py:130
  47.4 3.6 %fusion.64 = (f32[128]{0:T(128)}, f32[128]{0:T(128)}, f32[128]{0:T(128)}, f32[128]{0:T(128)}, f32[128]{0:T(128)}, /*index=5*/f32[128]{0:T(128)}, f32[128]{0:T(12...) fusion(bf16[2,16,64,128]{3,2,1,0:T(8,128)(2,1)S(1)} %convolutio, ...), kind=kLoop, calls=%fused_computation.144 | loop fusion | flops 14415616 | bytes 9970688 | tf_op jit(solution)/shard_map/sxyzc,sxyzc->c/dot_general | solution.py:102
  51.0 3.0 %fusion.63 = (f32[128]{0:T(128)}, f32[128]{0:T(128)}, f32[128]{0:T(128)}, f32[128]{0:T(128)}, f32[128]{0:T(128)}, /*index=5*/f32[128]{0:T(128)}, f32[128]{0:T(128)}, f32[128]{0:T(128)}, f32[128]{0:T(128)}) fusion(bf16[2,16,64,128]{3,2,1,0:T(8,128)(2,1)S(1)} %convolution_convert_fusion.1, bf16[1,1,18,64,128]{4,3,2,1,0:T(8,128)(2,1)} %collective-permute-done.7, ...), kind=kLoop, calls=%fused_computation.143 | loop fusion | flops 10222464 | bytes 3281408 | tf_op jit(solution)/shard_map/sxyzc,sxyzc->c/dot_general | solution.py:102
  54.0 2.8 %stack.223 = f32[27,128]{1,0:T(8,128)S(1)} concatenate(f32[1,128]{1,0:T(1,128)} %bitcast.678, f32[1,128]{1,0:T(1,128)} %bitcast.682, f32[1,128]{1,0:T(1,128)} %bitcast.677, f32[1,128]{1,0:T(1,128)} %bitcast.676, f32[1,128]{1,0:T(1,128)} %bitcast.683, f32[1,128]{1,0:T(1,128)} %bitcast.675, f32[1,128]{1,0:T(1,128)} %bitcast.674, f32[1,128]{1,0:T(1,128)} %bitcast.684, ...), dimensions={0} | concatenate | bytes 27648 | tf_op jit(solution)/shard_map/stack | solution.py:106
  56.8 6.3 %convolution_bitcast_fusion = f32[16384]{0:T(1024)S(1)} fusion(bf16[1,1,2,16,64,128]{5,4,3,2,1,0:T(8,128)(2,1)S(1)} %copy-done, f32[128]{0:T(128)} %copy-done.46, f32[128]{0:T(128)} %copy-done.47, f32[128]{0:T(128)} %copy-done.48, f32[128]{0:T(128)} %copy-done.49, f32[128]{0:T(128)} %copy-done.50, f32[128]{0:T(128)} %copy-done.51, f32[128]{0:T(128)} %copy-done.52, ...), kind=kOutput, calls=%fused_computation.57 | convolution fusion | flops 91226112 | bytes 13317632 | tf_op jit(solution)/shard_map/sxyzc,sxyzd->cd/dot_general | solution.py:123
  63.1 1.0 all_to_all.14
  64.1 16.0 %all-to-all-start = ((f32[64,1,620]{2,1,0:T(1,128)}), f32[64,1,620]{2,1,0:T(1,128)S(1)}, u32[]{:S(2)}, u32[]{:S(2)}) async-start(f32[64,1,620]{2,1,0:T(1,128)} %all_to_all.14), calls=%async_computation | async-start | bytes 327680 | tf_op jit(solution)/shard_map/all_to_all | solution.py:22
  80.1 3.5 %collective-permute-start.4 = (bf16[1,1,18,64,128]{4,3,2,1,0:T(8,128)(2,1)}, bf16[1,1,18,64,128]{4,3,2,1,0:T(8,128)(2,1)S(1)}, u32[]{:S(2)}, u32[]{:S(2)}) collective-permute-start(bf16[1,1,18,64,128]{4,3,2,1,0:T(8,128)(2,1)} %get-tuple-element.71), channel_id=1, source_target_pairs={{0,4},{4,8},{8,12},{12,16},{16,20},{20,24},{24,28},{28,32},{32,36}... | collective-permute-start | bytes 884744 | tf_op jit(solution)/shard_map/ppermute | solution.py:12
  83.6 1.9 %collective-permute-start.5 = (bf16[1,1,18,64,128]{4,3,2,1,0:T(8,128)(2,1)}, bf16[1,1,18,64,128]{4,3,2,1,0:T(8,128)(2,1)}, u32[]{:S(2)}, u32[]{:S(2)}) collective-permute-start(bf16[1,1,18,64,128]{4,3,2,1,0:T(8,128)(2,1)} %get-tuple-element.72), channel_id=1, source_target_pairs={{4,0},{8,4},{12,8},{16,12},{20,16},{24,20},{28,24},{32,28},{36,32}... | collective-permute-start | bytes 884744 | tf_op jit(solution)/shard_map/ppermute | solution.py:12
  85.5 0.1 pad.32
  85.6 5.0 %all-to-all-done = f32[64,1,620]{2,1,0:T(1,128)S(1)} async-done(((f32[64,1,620]{2,1,0:T(1,128)}), f32[64,1,620]{2,1,0:T(1,128)S(1)}, u32[]{:S(2)}, u32[]{:S(2)}) %all-to-all-start) | async-done | bytes 158752 | tf_op jit(solution)/shard_map/all_to_all | solution.py:22
  90.7 0.1 reduce_sum.18
  90.8 0.6 broadcast_in_dim.10
  91.4 4.0 %all-to-all-start.1 = ((f32[4,1,620]{2,1,0:T(1,128)}), f32[4,1,620]{2,1,0:T(1,128)S(1)}, u32[]{:S(2)}, u32[]{:S(2)}) async-start(f32[4,1,620]{2,1,0:T(1,128)} %broadcast_in_dim.10), calls=%async_computation.1 | async-start | bytes 20480 | tf_op jit(solution)/shard_map/all_to_all | solution.py:28
  95.6 0.0 collective-permute-done.4
  95.6 0.0 collective-permute-done.5
  95.6 1.5 %select_maximum_fusion.2 = bf16[1,4,18,66,128]{4,3,2,1,0:T(8,128)(2,1)S(1)} fusion(bf16[1,1,18,64,128]{4,3,2,1,0:T(8,128)(2,1)} %collective-permute-done.5, bf16[1,2,18,64,128]{4,3,2,1,0:T(8,128)(2,1)S(1)} %pad.32, bf16[1,1,18,64,128]{4,3,2,1,0:T(8,128)(2,1)S(1)} %collective-permute-done.4), kind=kLoop, calls=%fused_computation.61 | loop fusion | flops 7299072 | bytes 2396160 | tf_op jit(solution)/shard_map/concatenate | solution.py:130
  97.1 2.5 %all-to-all-done.1 = f32[4,1,620]{2,1,0:T(1,128)S(1)} async-done(((f32[4,1,620]{2,1,0:T(1,128)}), f32[4,1,620]{2,1,0:T(1,128)S(1)}, u32[]{:S(2)}, u32[]{:S(2)}) %all-to-all-start.1) | async-done | bytes 9952 | tf_op jit(solution)/shard_map/all_to_all | solution.py:28
  99.6 0.8 broadcast_in_dim.11
  100.4 8.0 %all-to-all-start.2 = ((f32[64,1,620]{2,1,0:T(1,128)}), f32[64,1,620]{2,1,0:T(1,128)S(1)}, u32[]{:S(2)}, u32[]{:S(2)}) async-start(f32[64,1,620]{2,1,0:T(1,128)} %broadcast_in_dim.11), calls=%async_computation.2 | async-start | bytes 327680 | tf_op jit(solution)/shard_map/all_to_all | solution.py:28
  108.6 6.0 %fusion.132 = bf16[1,1,2,16,64,128]{5,4,3,2,1,0:T(8,128)(2,1)} fusion(f32[128]{0:T(128)S(1)} %get-tuple-element.109, bf16[1,4,18,66,128]{4,3,2,1,0:T(8,128)(2,1)S(1)} %select_maximum_fusion.2, f32[128]{0:T(128)S(1)} %get-tuple-element.110, bf16[1,2,18,64,128]{4,3,2,1,0:T(8,128)(2,1)S(1)} %pad.32, ...), kind=kLoop, calls=%fused_computation.242 | loop fusion | flops 22806528 | bytes 12727808 | tf_op jit(solution)/shard_map/broadcast_in_dim | solution.py:185
  114.6 4.4 %all-to-all-done.2 = f32[64,1,620]{2,1,0:T(1,128)S(1)} async-done(((f32[64,1,620]{2,1,0:T(1,128)}), f32[64,1,620]{2,1,0:T(1,128)S(1)}, u32[]{:S(2)}, u32[]{:S(2)}) %all-to-all-start.2) | async-done | bytes 158752 | tf_op jit(solution)/shard_map/all_to_all | solution.py:28
  119.0 0.4 reduce.56
  119.4 0.1 slice.865
  119.5 0.1 reshape.585
  119.7 0.7 slice_multiply_fusion
  120.4 0.6 mul.1146
  121.0 0.6 mul.1143
  (133 shorter events, 0.3 us)
Async XLA Ops:
  0.6 9.3 %copy-start.1 = (bf16[1,1,2,16,64,128]{5,4,3,2,1,0:T(8,128)(2,1)S(1)}, bf16[1,1,2,16,64,128]{5,4,3,2,1,0:T(8,128)(2,1)}, u32[]{:S(2)}) copy-start(bf16[1,1,2,16,64,128]{5,4,3,2,1,0:T(8,128)(2,1)} %param.6) | copy-start | bytes 1572868
  2.7 11.6 %copy-start.5 = (bf16[3,3,3,128]{3,2,1,0:T(4,128)(2,1)S(1)}, bf16[3,3,3,128]{3,2,1,0:T(4,128)(2,1)}, u32[]{:S(2)}) copy-start(bf16[3,3,3,128]{3,2,1,0:T(4,128)(2,1)} %param.7) | copy-start | bytes 20740
  2.7 11.7 %copy-start.6 = (bf16[3,3,3,128]{3,2,1,0:T(4,128)(2,1)S(1)}, bf16[3,3,3,128]{3,2,1,0:T(4,128)(2,1)}, u32[]{:S(2)}) copy-start(bf16[3,3,3,128]{3,2,1,0:T(4,128)(2,1)} %param.9) | copy-start | bytes 20740
  2.8 18.0 %collective-permute-start.1 = (bf16[1,1,18,64,128]{4,3,2,1,0:T(8,128)(2,1)S(1)}, bf16[1,1,18,64,128]{4,3,2,1,0:T(8,128)(2,1)S(1)}, u32[]{:S(2)}, u32[]{:S(2)}) collective-permute-start(bf16[1,1,18,64,128]{4,3,2,1,0:T(8,128)(2,1)S(1)} %get-tuple-element.73), channel_id=1, source_target_pairs={{4,0},{8,4},{12,8},{16,12},{20,16},{24,20},{28,24},{32,28},{36,32}... | collective-permute-start | bytes 884744 | tf_op jit(solution)/shard_map/ppermute | solution.py:12
  8.0 12.8 %collective-permute-start = (bf16[1,1,18,64,128]{4,3,2,1,0:T(8,128)(2,1)S(1)}, bf16[1,1,18,64,128]{4,3,2,1,0:T(8,128)(2,1)S(1)}, u32[]{:S(2)}, u32[]{:S(2)}) collective-permute-start(bf16[1,1,18,64,128]{4,3,2,1,0:T(8,128)(2,1)S(1)} %get-tuple-element.74), channel_id=1, source_target_pairs={{0,4},{4,8},{8,12},{12,16},{16,20},{20,24},{24,28},{28,32},{32,36}... | collective-permute-start | bytes 884744 | tf_op jit(solution)/shard_map/ppermute | solution.py:12
  10.0 6.7 %collective-permute-start.2 = (bf16[1,1,18,64,128]{4,3,2,1,0:T(8,128)(2,1)S(1)}, bf16[1,1,18,64,128]{4,3,2,1,0:T(8,128)(2,1)S(1)}, u32[]{:S(2)}, u32[]{:S(2)}) collective-permute-start(bf16[1,1,18,64,128]{4,3,2,1,0:T(8,128)(2,1)S(1)} %get-tuple-element.75), channel_id=1, source_target_pairs={{0,4},{4,8},{8,12},{12,16},{16,20},{20,24},{24,28},{28,32},{32,36}... | collective-permute-start | bytes 884744 | tf_op jit(solution)/shard_map/ppermute | solution.py:12
  12.2 8.0 %collective-permute-start.3 = (bf16[1,1,18,64,128]{4,3,2,1,0:T(8,128)(2,1)S(1)}, bf16[1,1,18,64,128]{4,3,2,1,0:T(8,128)(2,1)S(1)}, u32[]{:S(2)}, u32[]{:S(2)}) collective-permute-start(bf16[1,1,18,64,128]{4,3,2,1,0:T(8,128)(2,1)S(1)} %get-tuple-element.76), channel_id=1, source_target_pairs={{4,0},{8,4},{12,8},{16,12},{20,16},{24,20},{28,24},{32,28},{36,32}... | collective-permute-start | bytes 884744 | tf_op jit(solution)/shard_map/ppermute | solution.py:12
  14.4 6.9 %copy-start.7 = (f32[128]{0:T(128)}, f32[128]{0:T(128)S(1)}, u32[]{:S(2)}) copy-start(f32[128]{0:T(128)S(1)} %get-tuple-element.116) | copy-start | bytes 1540
  14.4 6.9 %copy-start.9 = (f32[128]{0:T(128)}, f32[128]{0:T(128)S(1)}, u32[]{:S(2)}) copy-start(f32[128]{0:T(128)S(1)} %get-tuple-element.117) | copy-start | bytes 1540
  14.4 6.9 %copy-start.11 = (f32[128]{0:T(128)}, f32[128]{0:T(128)S(1)}, u32[]{:S(2)}) copy-start(f32[128]{0:T(128)S(1)} %get-tuple-element.118) | copy-start | bytes 1540
  14.4 6.9 %copy-start.13 = (f32[128]{0:T(128)}, f32[128]{0:T(128)S(1)}, u32[]{:S(2)}) copy-start(f32[128]{0:T(128)S(1)} %get-tuple-element.119) | copy-start | bytes 1540
  14.4 6.9 %copy-start.15 = (f32[128]{0:T(128)}, f32[128]{0:T(128)S(1)}, u32[]{:S(2)}) copy-start(f32[128]{0:T(128)S(1)} %get-tuple-element.120) | copy-start | bytes 1540
  14.5 6.9 %copy-start.17 = (f32[128]{0:T(128)}, f32[128]{0:T(128)S(1)}, u32[]{:S(2)}) copy-start(f32[128]{0:T(128)S(1)} %get-tuple-element.121) | copy-start | bytes 1540
  14.5 6.9 %copy-start.19 = (f32[128]{0:T(128)}, f32[128]{0:T(128)S(1)}, u32[]{:S(2)}) copy-start(f32[128]{0:T(128)S(1)} %get-tuple-element.122) | copy-start | bytes 1540
  14.5 6.9 %copy-start.21 = (f32[128]{0:T(128)}, f32[128]{0:T(128)S(1)}, u32[]{:S(2)}) copy-start(f32[128]{0:T(128)S(1)} %get-tuple-element.123) | copy-start | bytes 1540
  14.5 6.9 %copy-start.23 = (f32[128]{0:T(128)}, f32[128]{0:T(128)S(1)}, u32[]{:S(2)}) copy-start(f32[128]{0:T(128)S(1)} %get-tuple-element.124) | copy-start | bytes 1540
  14.5 6.9 %copy-start.25 = (f32[128]{0:T(128)}, f32[128]{0:T(128)S(1)}, u32[]{:S(2)}) copy-start(f32[128]{0:T(128)S(1)} %get-tuple-element.125) | copy-start | bytes 1540
  14.5 6.9 %copy-start.27 = (f32[128]{0:T(128)}, f32[128]{0:T(128)S(1)}, u32[]{:S(2)}) copy-start(f32[128]{0:T(128)S(1)} %get-tuple-element.126) | copy-start | bytes 1540
  14.5 11.2 %copy-start.45 = (f32[128]{0:T(128)}, f32[128]{0:T(128)S(1)}, u32[]{:S(2)}) copy-start(f32[128]{0:T(128)S(1)} %get-tuple-element.81) | copy-start | bytes 1540
  14.6 11.2 %copy-start.46 = (f32[128]{0:T(128)}, f32[128]{0:T(128)S(1)}, u32[]{:S(2)}) copy-start(f32[128]{0:T(128)S(1)} %get-tuple-element.82) | copy-start | bytes 1540
  14.6 11.2 %copy-start.47 = (f32[128]{0:T(128)}, f32[128]{0:T(128)S(1)}, u32[]{:S(2)}) copy-start(f32[128]{0:T(128)S(1)} %get-tuple-element.83) | copy-start | bytes 1540
  14.6 11.2 %copy-start.48 = (f32[128]{0:T(128)}, f32[128]{0:T(128)S(1)}, u32[]{:S(2)}) copy-start(f32[128]{0:T(128)S(1)} %get-tuple-element.84) | copy-start | bytes 1540
  14.6 11.2 %copy-start.49 = (f32[128]{0:T(128)}, f32[128]{0:T(128)S(1)}, u32[]{:S(2)}) copy-start(f32[128]{0:T(128)S(1)} %get-tuple-element.85) | copy-start | bytes 1540
  14.6 11.2 %copy-start.50 = (f32[128]{0:T(128)}, f32[128]{0:T(128)S(1)}, u32[]{:S(2)}) copy-start(f32[128]{0:T(128)S(1)} %get-tuple-element.86) | copy-start | bytes 1540
  14.6 11.2 %copy-start.51 = (f32[128]{0:T(128)}, f32[128]{0:T(128)S(1)}, u32[]{:S(2)}) copy-start(f32[128]{0:T(128)S(1)} %get-tuple-element.87) | copy-start | bytes 1540
  14.6 11.2 %copy-start.52 = (f32[128]{0:T(128)}, f32[128]{0:T(128)S(1)}, u32[]{:S(2)}) copy-start(f32[128]{0:T(128)S(1)} %get-tuple-element.88) | copy-start | bytes 1540
  14.6 11.2 %copy-start.53 = (f32[128]{0:T(128)}, f32[128]{0:T(128)S(1)}, u32[]{:S(2)}) copy-start(f32[128]{0:T(128)S(1)} %get-tuple-element.89) | copy-start | bytes 1540
  14.6 11.2 %copy-start.54 = (f32[128]{0:T(128)}, f32[128]{0:T(128)S(1)}, u32[]{:S(2)}) copy-start(f32[128]{0:T(128)S(1)} %get-tuple-element.90) | copy-start | bytes 1540
  14.6 11.2 %copy-start.55 = (f32[128]{0:T(128)}, f32[128]{0:T(128)S(1)}, u32[]{:S(2)}) copy-start(f32[128]{0:T(128)S(1)} %get-tuple-element.91) | copy-start | bytes 1540
  14.7 11.2 %copy-start.56 = (f32[128]{0:T(128)}, f32[128]{0:T(128)S(1)}, u32[]{:S(2)}) copy-start(f32[128]{0:T(128)S(1)} %get-tuple-element.92) | copy-start | bytes 1540
  14.7 11.2 %copy-start.57 = (f32[128]{0:T(128)}, f32[128]{0:T(128)S(1)}, u32[]{:S(2)}) copy-start(f32[128]{0:T(128)S(1)} %get-tuple-element.93) | copy-start | bytes 1540
  14.7 11.2 %copy-start.58 = (f32[128]{0:T(128)}, f32[128]{0:T(128)S(1)}, u32[]{:S(2)}) copy-start(f32[128]{0:T(128)S(1)} %get-tuple-element.94) | copy-start | bytes 1540
  14.7 11.2 %copy-start.59 = (f32[128]{0:T(128)}, f32[128]{0:T(128)S(1)}, u32[]{:S(2)}) copy-start(f32[128]{0:T(128)S(1)} %get-tuple-element.95) | copy-start | bytes 1540
  14.7 11.2 %copy-start.60 = (f32[128]{0:T(128)}, f32[128]{0:T(128)S(1)}, u32[]{:S(2)}) copy-start(f32[128]{0:T(128)S(1)} %get-tuple-element.96) | copy-start | bytes 1540
  14.7 11.2 %copy-start.61 = (f32[128]{0:T(128)}, f32[128]{0:T(128)S(1)}, u32[]{:S(2)}) copy-start(f32[128]{0:T(128)S(1)} %get-tuple-element.97) | copy-start | bytes 1540
  14.7 11.2 %copy-start.62 = (f32[128]{0:T(128)}, f32[128]{0:T(128)S(1)}, u32[]{:S(2)}) copy-start(f32[128]{0:T(128)S(1)} %get-tuple-element.98) | copy-start | bytes 1540
  14.7 11.2 %copy-start.63 = (f32[128]{0:T(128)}, f32[128]{0:T(128)S(1)}, u32[]{:S(2)}) copy-start(f32[128]{0:T(128)S(1)} %get-tuple-element.99) | copy-start | bytes 1540
  15.5 10.5 %copy-start.64 = (f32[128]{0:T(128)}, f32[128]{0:T(128)S(1)}, u32[]{:S(2)}) copy-start(f32[128]{0:T(128)S(1)} %get-tuple-element.100) | copy-start | bytes 1540
  35.3 9.8 %collective-permute-start.7 = (bf16[1,1,18,64,128]{4,3,2,1,0:T(8,128)(2,1)}, bf16[1,1,18,64,128]{4,3,2,1,0:T(8,128)(2,1)}, u32[]{:S(2)}, u32[]{:S(2)}) collective-permute-start(bf16[1,1,18,64,128]{4,3,2,1,0:T(8,128)(2,1)} %get-tuple-element.138), channel_id=1, source_target_pairs={{4,0},{8,4},{12,8},{16,12},{20,16},{24,20},{28,24},{32,28},{36,32}... | collective-permute-start | bytes 884744 | tf_op jit(solution)/shard_map/ppermute | solution.py:12
  37.2 7.8 %collective-permute-start.6 = (bf16[1,1,18,64,128]{4,3,2,1,0:T(8,128)(2,1)S(1)}, bf16[1,1,18,64,128]{4,3,2,1,0:T(8,128)(2,1)}, u32[]{:S(2)}, u32[]{:S(2)}) collective-permute-start(bf16[1,1,18,64,128]{4,3,2,1,0:T(8,128)(2,1)S(1)} %get-tuple-element.139), channel_id=1, source_target_pairs={{0,4},{4,8},{8,12},{12,16},{16,20},{20,24},{24,28},{28,32},{32,36}... | collective-permute-start | bytes 884744 | tf_op jit(solution)/shard_map/ppermute | solution.py:12
  64.1 26.6 %all-to-all-start = ((f32[64,1,620]{2,1,0:T(1,128)}), f32[64,1,620]{2,1,0:T(1,128)S(1)}, u32[]{:S(2)}, u32[]{:S(2)}) async-start(f32[64,1,620]{2,1,0:T(1,128)} %all_to_all.14), calls=%async_computation | async-start | bytes 327680 | tf_op jit(solution)/shard_map/all_to_all | solution.py:22
  80.1 15.5 %collective-permute-start.4 = (bf16[1,1,18,64,128]{4,3,2,1,0:T(8,128)(2,1)}, bf16[1,1,18,64,128]{4,3,2,1,0:T(8,128)(2,1)S(1)}, u32[]{:S(2)}, u32[]{:S(2)}) collective-permute-start(bf16[1,1,18,64,128]{4,3,2,1,0:T(8,128)(2,1)} %get-tuple-element.71), channel_id=1, source_target_pairs={{0,4},{4,8},{8,12},{12,16},{16,20},{20,24},{24,28},{28,32},{32,36}... | collective-permute-start | bytes 884744 | tf_op jit(solution)/shard_map/ppermute | solution.py:12
  83.6 12.0 %collective-permute-start.5 = (bf16[1,1,18,64,128]{4,3,2,1,0:T(8,128)(2,1)}, bf16[1,1,18,64,128]{4,3,2,1,0:T(8,128)(2,1)}, u32[]{:S(2)}, u32[]{:S(2)}) collective-permute-start(bf16[1,1,18,64,128]{4,3,2,1,0:T(8,128)(2,1)} %get-tuple-element.72), channel_id=1, source_target_pairs={{4,0},{8,4},{12,8},{16,12},{20,16},{24,20},{28,24},{32,28},{36,32}... | collective-permute-start | bytes 884744 | tf_op jit(solution)/shard_map/ppermute | solution.py:12
  91.4 8.2 %all-to-all-start.1 = ((f32[4,1,620]{2,1,0:T(1,128)}), f32[4,1,620]{2,1,0:T(1,128)S(1)}, u32[]{:S(2)}, u32[]{:S(2)}) async-start(f32[4,1,620]{2,1,0:T(1,128)} %broadcast_in_dim.10), calls=%async_computation.1 | async-start | bytes 20480 | tf_op jit(solution)/shard_map/all_to_all | solution.py:28
  95.4 13.0 %copy-start.8 = (f32[128]{0:T(128)S(1)}, f32[128]{0:T(128)}, u32[]{:S(2)}) copy-start(f32[128]{0:T(128)} %copy-done.7) | copy-start | bytes 1540
  95.4 13.0 %copy-start.10 = (f32[128]{0:T(128)S(1)}, f32[128]{0:T(128)}, u32[]{:S(2)}) copy-start(f32[128]{0:T(128)} %copy-done.9) | copy-start | bytes 1540
  95.4 13.0 %copy-start.12 = (f32[128]{0:T(128)S(1)}, f32[128]{0:T(128)}, u32[]{:S(2)}) copy-start(f32[128]{0:T(128)} %copy-done.11) | copy-start | bytes 1540
  95.4 13.0 %copy-start.14 = (f32[128]{0:T(128)S(1)}, f32[128]{0:T(128)}, u32[]{:S(2)}) copy-start(f32[128]{0:T(128)} %copy-done.13) | copy-start | bytes 1540
  95.4 13.0 %copy-start.16 = (f32[128]{0:T(128)S(1)}, f32[128]{0:T(128)}, u32[]{:S(2)}) copy-start(f32[128]{0:T(128)} %copy-done.15) | copy-start | bytes 1540
  95.4 13.0 %copy-start.18 = (f32[128]{0:T(128)S(1)}, f32[128]{0:T(128)}, u32[]{:S(2)}) copy-start(f32[128]{0:T(128)} %copy-done.17) | copy-start | bytes 1540
  95.5 13.0 %copy-start.20 = (f32[128]{0:T(128)S(1)}, f32[128]{0:T(128)}, u32[]{:S(2)}) copy-start(f32[128]{0:T(128)} %copy-done.19) | copy-start | bytes 1540
  95.5 13.0 %copy-start.22 = (f32[128]{0:T(128)S(1)}, f32[128]{0:T(128)}, u32[]{:S(2)}) copy-start(f32[128]{0:T(128)} %copy-done.21) | copy-start | bytes 1540
  95.5 13.0 %copy-start.24 = (f32[128]{0:T(128)S(1)}, f32[128]{0:T(128)}, u32[]{:S(2)}) copy-start(f32[128]{0:T(128)} %copy-done.23) | copy-start | bytes 1540
  95.5 13.0 %copy-start.26 = (f32[128]{0:T(128)S(1)}, f32[128]{0:T(128)}, u32[]{:S(2)}) copy-start(f32[128]{0:T(128)} %copy-done.25) | copy-start | bytes 1540
  95.5 13.0 %copy-start.28 = (f32[128]{0:T(128)S(1)}, f32[128]{0:T(128)}, u32[]{:S(2)}) copy-start(f32[128]{0:T(128)} %copy-done.27) | copy-start | bytes 1540
  95.5 13.0 %copy-start.30 = (f32[128]{0:T(128)S(1)}, f32[128]{0:T(128)}, u32[]{:S(2)}) copy-start(f32[128]{0:T(128)} %copy-done.29) | copy-start | bytes 1540
  95.5 13.0 %copy-start.32 = (f32[128]{0:T(128)S(1)}, f32[128]{0:T(128)}, u32[]{:S(2)}) copy-start(f32[128]{0:T(128)} %copy-done.31) | copy-start | bytes 1540
  95.5 13.0 %copy-start.34 = (f32[128]{0:T(128)S(1)}, f32[128]{0:T(128)}, u32[]{:S(2)}) copy-start(f32[128]{0:T(128)} %copy-done.33) | copy-start | bytes 1540
  95.5 13.0 %copy-start.36 = (f32[128]{0:T(128)S(1)}, f32[128]{0:T(128)}, u32[]{:S(2)}) copy-start(f32[128]{0:T(128)} %copy-done.35) | copy-start | bytes 1540
  95.5 13.0 %copy-start.38 = (f32[128]{0:T(128)S(1)}, f32[128]{0:T(128)}, u32[]{:S(2)}) copy-start(f32[128]{0:T(128)} %copy-done.37) | copy-start | bytes 1540
  95.6 13.0 %copy-start.40 = (f32[128]{0:T(128)S(1)}, f32[128]{0:T(128)}, u32[]{:S(2)}) copy-start(f32[128]{0:T(128)} %copy-done.39) | copy-start | bytes 1540
  95.6 13.0 %copy-start.42 = (f32[128]{0:T(128)S(1)}, f32[128]{0:T(128)}, u32[]{:S(2)}) copy-start(f32[128]{0:T(128)} %copy-done.41) | copy-start | bytes 1540
  95.6 13.0 %copy-start.44 = (f32[128]{0:T(128)S(1)}, f32[128]{0:T(128)}, u32[]{:S(2)}) copy-start(f32[128]{0:T(128)} %copy-done.43) | copy-start | bytes 1540
  100.4 18.6 %all-to-all-start.2 = ((f32[64,1,620]{2,1,0:T(1,128)}), f32[64,1,620]{2,1,0:T(1,128)S(1)}, u32[]{:S(2)}, u32[]{:S(2)}) async-start(f32[64,1,620]{2,1,0:T(1,128)} %broadcast_in_dim.11), calls=%async_computation.2 | async-start | bytes 327680 | tf_op jit(solution)/shard_map/all_to_all | solution.py:28
  (13 other events, 67.2 us)
where the time goes:
time: 122 us
  starting transfers between devices  50.6 us (41%)
  other arithmetic  23.8 us (20%)
  waiting for transfers between devices  16.6 us (14%)
  matrix products  15.7 us (13%)
  local copies, waits for them, and re-layouts  13 us (11%)
  between operations  1.92 us (2%)
    ppermute x8, starting transfers between devices, passed_along(): return lax.ppermute(block, axis, route)  22.6 us
    all_to_all x1, starting transfers between devices, sent_and_summed(): lax.all_to_all(tiles, axis, split_axis=0, concat_axis=0, tiled=True)  16 us
    all_to_all x2, starting transfers between devices, from_everyone(): return lax.all_to_all(copies, axis, split_axis=0, concat_axis=0, tiled=True)  12 us
    dot_general x3, other arithmetic, kernel_grad(): jnp.einsum('sxyzc,sxyzc->c', window, upstream, preferred_element_type=jnp...  7.9 us
    all_to_all x2, waiting for transfers between devices, from_everyone(): return lax.all_to_all(copies, axis, split_axis=0, concat_axis=0, tiled=True)  6.87 us
    dot_general x2, matrix products, outer_sum(): jnp.einsum('sxyzc,sxyzd->cd', left, right, preferred_element_type=jnp.flo...  6.61 us
    broadcast_in_dim x1, other arithmetic, on_device(): grad_block[:, None]  6 us
    all_to_all x1, waiting for transfers between devices, sent_and_summed(): lax.all_to_all(tiles, axis, split_axis=0, concat_axis=0, tiled=True)  5.05 us
  transfers between devices with their start and end apart: 11, of which 5 were waited for; matrix products, arithmetic and copies ran while one was open for 11% of the time, Pallas kernels for 0%

commit v1 on v0

v1 whole, which is shorter than its diff:
```python
import functools
import math

import jax
import jax.numpy as jnp
from jax import lax
from jax.experimental import pallas as pl
from jax.experimental.pallas import tpu as pltpu
from jax.sharding import PartitionSpec as P

CH = 128
LINE = 64
CELLS = 1024
PADDED = CELLS + 2 * LINE
ROWS = 256
TERMS = 320
VMEM_LIMIT = 48 * 1024 * 1024


def mm(a, b):
    return jnp.dot(a, b, preferred_element_type=jnp.float32)


def keep_mask(count, edge):
    return lax.broadcasted_iota(jnp.int32, (count, 1), 0) % LINE != edge


def from_before(v):
    return jnp.where(keep_mask(v.shape[0], 0), pltpu.roll(v, 1, 0), 0.0)


def from_after(v):
    return jnp.where(keep_mask(v.shape[0], LINE - 1), pltpu.roll(v, v.shape[0] - 1, 0), 0.0)


def shift_sum(products, width):
    return (
        from_before(products[:, :width])
        + products[:, width : 2 * width]
        + from_after(products[:, 2 * width :])
    )


def set_plane(ref, slot, plane):
    edge = jnp.zeros((LINE, CH), jnp.bfloat16)
    ref[slot, 0:LINE, :] = edge
    ref[slot, LINE : LINE + CELLS, :] = plane
    ref[slot, LINE + CELLS : PADDED, :] = edge


def windows(ref, slots, start):
    return jnp.concatenate(
        [ref[p, start + b * LINE : start + b * LINE + ROWS, :] for p in slots for b in range(3)],
        axis=1,
    )


def fill_local(ref, tap_matrix):
    for p in range(2):
        for b in range(3):
            for e in range(3):
                for x in range(2):
                    row, col = ((p * 3 + b) * CH, (e * 2 + x) * CH)
                    ref[row : row + CH, col : col + CH] = tap_matrix(9 * (p + 1 - x) + 3 * b + e)


def fill_side(ref, tap_matrix):
    for b in range(3):
        for e in range(3):
            ref[b * CH : (b + 1) * CH, e * CH : (e + 1) * CH] = tap_matrix(3 * b + e)


def columns_of(depth):
    padded = jnp.concatenate([depth, jnp.zeros((CH - 27, CH), jnp.float32)], axis=0)
    return padded.T


def forward_taps(cols, point):
    return lambda s: (cols[:, s : s + 1] * point).astype(jnp.bfloat16)


def backward_taps(depth, point_t):
    return lambda s: (depth[26 - s : 27 - s, :] * point_t).astype(jnp.bfloat16)


def side_taps(matrix, high):
    def pick(j):
        return jnp.where(high, matrix(18 + j), matrix(j))

    return pick


def near_kernel(
    parity, block_in, block_up, near, d1, p1, d2, p2,
    pre, carried, far_w1, far_w2,
    planes_in, planes_up, w_local, w_side,
):
    core = parity[0]
    depth_one = d1[...].astype(jnp.float32)
    depth_two = d2[...].astype(jnp.float32)
    point_one = p1[...].astype(jnp.float32)
    point_two_t = p2[...].astype(jnp.float32).T
    taps_one = forward_taps(columns_of(depth_one), point_one)
    taps_two = backward_taps(depth_two, point_two_t)
    near_high = core == 0
    for which, planes, block, taps, out, far_w in (
        (0, planes_in, block_in, taps_one, pre, far_w1),
        (1, planes_up, block_up, taps_two, carried, far_w2),
    ):
        for x in range(2):
            set_plane(planes, x, block[x])
        set_plane(planes, 2, near[which])
        fill_local(w_local, taps)
        fill_side(w_side, side_taps(taps, near_high))
        fill_side(far_w, side_taps(taps, jnp.logical_not(near_high)))
        for start in range(0, CELLS, ROWS):
            both = shift_sum(mm(windows(planes, (0, 1), start), w_local[...]), 2 * CH)
            one = shift_sum(mm(windows(planes, (2,), start), w_side[...]), CH)
            out[0, start : start + ROWS, :] = both[:, :CH] + jnp.where(near_high, 0.0, one)
            out[1, start : start + ROWS, :] = both[:, CH:] + jnp.where(near_high, one, 0.0)


def tap_sums(left_t, planes, combine):
    order = [(a, b) for a in range(3) for b in range(3)]
    for at in range(0, 9, 2):
        group = order[at : at + 2]
        right = jnp.concatenate(
            [
                jnp.concatenate(
                    [planes[a + x, b * LINE : b * LINE + CELLS, :] for x in range(2)], axis=0
                )
                for a, b in group
            ],
            axis=1,
        )
        sums = mm(left_t[...], right)
        for i, (a, b) in enumerate(group):
            for e in range(3):
                combine(9 * a + 3 * b + e, sums[e * CH : (e + 1) * CH, i * CH : (i + 1) * CH])


def far_kernel(
    factor,
    parity, block_in, block_up, near, far, pre, carried, far_w1, far_w2, d1, p1, d2, p2,
    scaled_out, terms,
    planes_in, planes_up, scaled_t, hidden_t, total,
):
    core = parity[0]
    far_slot = 3 * core
    near_slot = 3 - far_slot
    for which, planes, block in ((0, planes_in, block_in), (1, planes_up, block_up)):
        for x in range(2):
            set_plane(planes, 1 + x, block[x])
        set_plane(planes, near_slot, near[which])
        set_plane(planes, far_slot, far[which])
    for start in range(0, CELLS, ROWS):
        more_pre = shift_sum(mm(windows(planes_in, (far_slot,), start), far_w1[...]), CH)
        more_carried = shift_sum(mm(windows(planes_up, (far_slot,), start), far_w2[...]), CH)
        for x in range(2):
            mine = core == x
            value = pre[x, start : start + ROWS, :] + jnp.where(mine, more_pre, 0.0)
            back = carried[x, start : start + ROWS, :] + jnp.where(mine, more_carried, 0.0)
            sigma = jax.nn.sigmoid(value)
            hidden = (value * sigma).astype(jnp.bfloat16).astype(jnp.float32)
            scaled = (back * (sigma * (1.0 + value * (1.0 - sigma)))).astype(jnp.bfloat16)
            scaled_out[x, start : start + ROWS, :] = scaled
            scaled = scaled.astype(jnp.float32)
            at = x * CELLS + start
            for ref, v in ((scaled_t, scaled), (hidden_t, hidden)):
                shifted = jnp.concatenate([from_after(v), v, from_before(v)], axis=1)
                ref[:, at : at + ROWS] = shifted.astype(jnp.bfloat16).T
    depth_one = d1[...].astype(jnp.float32)
    point_one_t = p1[...].astype(jnp.float32).T
    point_two = p2[...].astype(jnp.float32)
    cols_two = columns_of(d2[...].astype(jnp.float32))
    terms[...] = jnp.zeros((TERMS, CH), jnp.float32)
    total[...] = jnp.zeros((2, CH, CH), jnp.float32)
    lane = lax.broadcasted_iota(jnp.int32, (CH, CH), 1)

    def layer_one(s, block):
        total[0] += depth_one[s : s + 1, :] * block
        terms[s : s + 1, :] = jnp.sum(point_one_t * block, axis=0, keepdims=True) * factor

    tap_sums(scaled_t, planes_in, layer_one)
    terms[32:160, :] = total[0].T * factor
    total[0] = jnp.zeros((CH, CH), jnp.float32)

    def layer_two(s, block):
        s = 26 - s
        total[0] += cols_two[:, s : s + 1] * block
        total[1] += jnp.where(lane == s, jnp.sum(point_two * block, axis=1, keepdims=True), 0.0)

    tap_sums(hidden_t, planes_up, layer_two)
    terms[192:320, :] = total[0] * factor
    terms[160:192, :] = total[1].T[:32, :] * factor


def last_kernel(parity, scaled, near, far, d1, p1, out, planes, w_local, w_side):
    core = parity[0]
    depth_one = d1[...].astype(jnp.float32)
    taps = backward_taps(depth_one, p1[...].astype(jnp.float32).T)
    near_high = core == 0
    for x in range(2):
        set_plane(planes, x, scaled[x])
    set_plane(planes, 2, near[...])
    set_plane(planes, 3, far[...])
    fill_local(w_local, taps)
    for side, high in ((0, near_high), (1, jnp.logical_not(near_high))):
        w = w_side.at[side]
        fill_side(w, side_taps(taps, high))
    for start in range(0, CELLS, ROWS):
        both = shift_sum(mm(windows(planes, (0, 1), start), w_local[...]), 2 * CH)
        one = shift_sum(mm(windows(planes, (2,), start), w_side[0]), CH)
        two = shift_sum(mm(windows(planes, (3,), start), w_side[1]), CH)
        low = jnp.where(near_high, two, one)
        high = jnp.where(near_high, one, two)
        out[0, start : start + ROWS, :] = (both[:, :CH] + low).astype(jnp.bfloat16)
        out[1, start : start + ROWS, :] = (both[:, CH:] + high).astype(jnp.bfloat16)


def call(kernel, scratch, outs, flops, *args):
    vmem = pl.BlockSpec(memory_space=pltpu.VMEM)
    smem = pl.BlockSpec(memory_space=pltpu.SMEM)
    moved = sum(a.size * a.dtype.itemsize for a in args) + sum(
        o.size * o.dtype.itemsize for o in outs
    )
    return pl.pallas_call(
        kernel,
        out_shape=outs,
        in_specs=[smem] + [vmem] * (len(args) - 1),
        out_specs=[vmem] * len(outs),
        scratch_shapes=scratch,
        cost_estimate=pl.CostEstimate(flops=flops, bytes_accessed=moved, transcendentals=0),
        compiler_params=pltpu.CompilerParams(vmem_limit_bytes=VMEM_LIMIT),
    )(*args)


def swapped(near, far):
    count = lax.axis_size("space")
    pairs = [(i, i ^ 1) for i in range(count)]
    crossing = [(i, i + 1) for i in range(1, count - 1, 2)]
    crossing = crossing + [(j, i) for i, j in crossing]
    far = lax.ppermute(far, "space", crossing)
    near = lax.ppermute(near, "space", pairs)
    return near, far


def sum_of_terms(terms):
    count = lax.axis_size("space")
    tiles = terms.reshape(count, 1, -1)
    share = lax.all_to_all(tiles, "space", 0, 0, tiled=True).sum(axis=0)
    groups = lax.axis_size("dp")
    copies = jnp.broadcast_to(share, (groups, *share.shape))
    share = lax.all_to_all(copies, "dp", 0, 0, tiled=True).sum(axis=0)
    copies = jnp.broadcast_to(share, (count, *share.shape))
    return lax.all_to_all(copies, "space", 0, 0, tiled=True).reshape(TERMS, CH)


def on_device(inputs, depth_one, point_one, depth_two, point_two, cotangent):
    f32, bf16 = jnp.float32, jnp.bfloat16
    shape = jax.ShapeDtypeStruct
    block_in = inputs.reshape(2, CELLS, CH)
    block_up = cotangent.reshape(2, CELLS, CH)
    d1 = depth_one.reshape(27, CH)
    d2 = depth_two.reshape(27, CH)
    core = lax.axis_index("space") % 2
    parity = core.astype(jnp.int32).reshape(1)
    first = jnp.stack([block_in[0], block_up[0]])
    last = jnp.stack([block_in[1], block_up[1]])
    near, far = swapped(jnp.where(core == 0, last, first), jnp.where(core == 0, first, last))

    slots = pltpu.VMEM((4, PADDED, CH), bf16)
    local_w = pltpu.VMEM((6 * CH, 6 * CH), bf16)
    pre, carried, far_w1, far_w2 = call(
        near_kernel,
        [slots, slots, local_w, pltpu.VMEM((3 * CH, 3 * CH), bf16)],
        [shape((2, CELLS, CH), f32)] * 2 + [shape((3 * CH, 3 * CH), bf16)] * 2,
        4_000_000_000,
        parity, block_in, block_up, near, d1, point_one, d2, point_two,
    )
    cells = lax.axis_size("dp") * lax.axis_size("space") * 2 * CELLS
    scaled, terms = call(
        functools.partial(far_kernel, 1.0 / math.sqrt(cells)),
        [slots, slots] + [pltpu.VMEM((3 * CH, 2 * CELLS), bf16)] * 2 + [pltpu.VMEM((2, CH, CH), f32)],
        [shape((2, CELLS, CH), bf16), shape((TERMS, CH), f32)],
        4_000_000_000,
        parity, block_in, block_up, near, far, pre, carried, far_w1, far_w2,
        d1, point_one, d2, point_two,
    )
    near, far = swapped(
        jnp.where(core == 0, scaled[1], scaled[0]), jnp.where(core == 0, scaled[0], scaled[1])
    )
    (grad,) = call(
        last_kernel,
        [slots, local_w, pltpu.VMEM((2, 3 * CH, 3 * CH), bf16)],
        [shape((2, CELLS, CH), bf16)],
        4_000_000_000,
        parity, scaled, near, far, d1, point_one,
    )
    sums = sum_of_terms(terms)
    return (
        grad.reshape(inputs.shape),
        sums[:27].reshape(3, 3, 3, CH),
        sums[32:160],
        sums[160:187].reshape(3, 3, 3, CH),
        sums[192:320],
    )


def solution(mesh):
    slabs = P("dp", "space", None, None, None, None)
    return jax.shard_map(
        on_device,
        mesh=mesh,
        in_specs=(slabs, P(), P(), P(), P(), slabs),
        out_specs=(slabs, P(), P(), P(), P()),
        check_vma=False,
    )
```

time: 122 us -> 73.6 us (0.60)
  starting transfers between devices: 50.6 us -> 27 us
  other arithmetic: 23.8 us -> 1.08 us
  matrix products: 15.7 us -> 0 us
  Pallas kernels: 0 us -> 13.8 us
  local copies, waits for them, and re-layouts: 13 us -> 3.95 us
  blocking collectives: 0 us -> 7.99 us
  waiting for transfers between devices: 16.6 us -> 18.6 us
    dot_general x5 -> x0, matrix products: 15.7 us -> none  [the longest x2 6.61 us: outer_sum(): jnp.einsum('sxyzc,sxyzd->cd', left, right, preferred_element_type=jnp.flo...]
    ppermute x8 -> x4, starting transfers between devices: 22.6 us -> 8.78 us  [the longest x2 5.45 us: swapped(): far = lax.ppermute(far, 'space', crossing)]
    pallas_call x0 -> x3, Pallas kernels: none -> 13.8 us  [call(): pl.pallas_call(kernel, out_shape=outs, in_specs=[smem] + [vmem] * (len(ar...]
    all_to_all x3 -> x2, starting transfers between devices: 28 us -> 18.2 us  [the longest x1 11.3 us: sum_of_terms(): share = lax.all_to_all(tiles, 'space', 0, 0, tiled=True).sum(axis=0)]
    all_to_all x0 -> x1, blocking collectives: none -> 7.99 us  [sum_of_terms(): share = lax.all_to_all(copies, 'dp', 0, 0, tiled=True).sum(axis=0)]
    dot_general x3 -> x0, other arithmetic: 7.9 us -> none  [kernel_grad(): jnp.einsum('sxyzc,sxyzc->c', window, upstream, preferred_element_type=jnp...]
    broadcast_in_dim x1 -> x0, other arithmetic: 6 us -> none  [on_device(): grad_block[:, None]]
    convert_element_type x4 -> x0, other arithmetic: 4.53 us -> none  [the longest x1 4.24 us: on_device(): mixed_one = depthwise(x_framed, depth_one).astype(jnp.bfloat16)]
  transfers between devices with their start and end apart: 11 -> 6, of which waited for: 5 -> 3; matrix products, arithmetic and copies ran while one was open for 11% -> 1% of each run, Pallas kernels for 0% -> 10%
where the time goes in v1:
time: 73.6 us; the launch traced here: 73.2 us
  starting transfers between devices  27 us (37%)
  waiting for transfers between devices  18.6 us (25%)
  Pallas kernels  13.8 us (19%)
  blocking collectives  7.99 us (11%)
  local copies, waits for them, and re-layouts  3.95 us (5%)
  other arithmetic  1.08 us (1%)
  between operations  0.82 us (1%)
    pallas_call x3, Pallas kernels, call(): pl.pallas_call(kernel, out_shape=outs, in_specs=[smem] + [vmem] * (len(ar...  13.8 us
    all_to_all x1, starting transfers between devices, sum_of_terms(): share = lax.all_to_all(tiles, 'space', 0, 0, tiled=True).sum(axis=0)  11.3 us
    all_to_all x1, blocking collectives, sum_of_terms(): share = lax.all_to_all(copies, 'dp', 0, 0, tiled=True).sum(axis=0)  7.99 us
    all_to_all x1, waiting for transfers between devices, sum_of_terms(): return lax.all_to_all(copies, 'space', 0, 0, tiled=True).reshape(TERMS, CH)  7.2 us
    all_to_all x1, starting transfers between devices, sum_of_terms(): return lax.all_to_all(copies, 'space', 0, 0, tiled=True).reshape(TERMS, CH)  6.95 us
    all_to_all x1, waiting for transfers between devices, sum_of_terms(): share = lax.all_to_all(tiles, 'space', 0, 0, tiled=True).sum(axis=0)  6.9 us
    ppermute x2, starting transfers between devices, swapped(): far = lax.ppermute(far, 'space', crossing)  5.45 us
    ppermute x2, waiting for transfers between devices, swapped(): far = lax.ppermute(far, 'space', crossing)  4.45 us
  transfers between devices with their start and end apart: 6, of which 3 were waited for; matrix products, arithmetic and copies ran while one was open for 1% of the time, Pallas kernels for 10%

profile of v1, /device:TPU:1, one launch (start us, length us, event | category | flops | bytes accessed | tf_op | source)
XLA Modules:
  0.0 73.2 jit_solution(2285708470843760027)
XLA Ops:
  0.6 0.0 copy-start.1
  0.7 1.1 %fusion = (bf16[1,1,1,16,64,128]{5,4,3,2,1,0:T(8,128)(2,1)S(1)}, bf16[1,1,1,16,64,128]{5,4,3,2,1,0:T(8,128)(2,1)S(1)}) fusion(bf16[1,1,2,16,64,128]{5,4,3,2,1,0:T(8,128)(2,1)} %param.6), kind=kLoop, calls=%fused_computation.6 | loop fusion | bytes 1048576 | tf_op jit(solution)/shard_map/slice | solution.py:269
  1.8 0.1 copy-done.1
  1.9 0.0 copy-start.4
  1.9 0.0 copy-start.5
  1.9 0.0 copy-start
  1.9 0.0 copy-start.3
  1.9 0.9 %broadcast_select_fusion = (bf16[2,1024,128]{2,1,0:T(8,128)(2,1)S(1)}, bf16[2,1024,128]{2,1,0:T(8,128)(2,1)}) fusion(pred[]{:T(512)S(6)} %eq.4, bf16[1,1024,128]{2,1,0:T(8,128)(2,1)S(1)} %bitcast.21, bf16[1,1024,128]{2,1,0:T(8,128)(2,1)S(1)} %bitcast.19, bf16[1,1024,128]{2,1,0:T(8,128)(2,1)S(1)} %bitcast.20, bf16[1,1024,128]{2,1,0:T(8,128)(2,1)S(1)} %bitcast.18), kind=kLoop, calls=%fused_computation.2 | loop fusion | flops 1048576 | bytes 2097153 | tf_op jit(solution)/shard_map/jit(_where)/select_n | solution.py:270
  2.8 0.0 copy-start.2
  2.8 3.2 %collective-permute-start = (bf16[2,1024,128]{2,1,0:T(8,128)(2,1)}, bf16[2,1024,128]{2,1,0:T(8,128)(2,1)S(1)}, u32[]{:S(2)}, u32[]{:S(2)}) collective-permute-start(bf16[2,1024,128]{2,1,0:T(8,128)(2,1)} %get-tuple-element.18), channel_id=1, source_target_pairs={{0,4},{4,0},{8,12},{12,8},{16,20},{20,16},{24,28},{28,24},{32,36},... | collective-permute-start | bytes 1572872 | tf_op jit(solution)/shard_map/ppermute | solution.py:244
  6.1 1.9 %collective-permute-start.1 = (bf16[2,1024,128]{2,1,0:T(8,128)(2,1)S(1)}, bf16[2,1024,128]{2,1,0:T(8,128)(2,1)S(1)}, u32[]{:S(2)}, u32[]{:S(2)}) collective-permute-start(bf16[2,1024,128]{2,1,0:T(8,128)(2,1)S(1)} %get-tuple-element.17), channel_id=1, source_target_pairs={{4,8},{12,16},{20,24},{28,32},{36,40},{44,48},{52,56},{60,64},{68,... | collective-permute-start | bytes 1572872 | tf_op jit(solution)/shard_map/ppermute | solution.py:243
  8.0 0.0 copy-done.4
  8.0 0.0 copy-done.5
  8.0 0.0 collective-permute-done.near
  8.1 0.0 copy-done
  8.1 0.0 copy-done.3
  8.1 0.0 copy-done.2
  8.1 4.0 %shard_map.101 = (f32[2,1024,128]{2,1,0:T(8,128)S(1)}, f32[2,1024,128]{2,1,0:T(8,128)S(1)}, bf16[384,384]{1,0:T(8,128)(2,1)S(1)}, bf16[384,384]{1,0:T(8,128)(2,1)S(1)}) custom-call(s32[1]{0:T(128)} %bitcast.parity, bf16[2,1024,128]{2,1,0:T(8,128)(2,1)S(1)} %bitcast.14, bf16[2,1024,128]{2,1,0:T(8,128)(2,1)S(1)} %bitcast.16, ...), custom_call_target="tpu_custom_call" | custom-call | flops 4000000000 | bytes 4339204 | tf_op jit(solution)/shard_map/pallas_call | solution.py:227
  12.1 4.5 %collective-permute-done.1.far = bf16[2,1024,128]{2,1,0:T(8,128)(2,1)S(1)} collective-permute-done((bf16[2,1024,128]{2,1,0:T(8,128)(2,1)S(1)}, bf16[2,1024,128]{2,1,0:T(8,128)(2,1)S(1)}, u32[]{:S(2)}, u32[]{:S(2)}) %collective-permute-start.1) | collective-permute-done | bytes 524320 | tf_op jit(solution)/shard_map/ppermute | solution.py:243
  16.6 6.4 %shard_map.102 = (bf16[2,1024,128]{2,1,0:T(8,128)(2,1)S(1)}, f32[320,128]{1,0:T(8,128)}) custom-call(s32[1]{0:T(128)} %bitcast.parity, bf16[2,1024,128]{2,1,0:T(8,128)(2,1)S(1)} %bitcast.15, bf16[2,1024,128]{2,1,0:T(8,128)(2,1)S(1)} %bitcast.17, bf16[2,1024,128]{2,1,0:T(8,128)(2,1)S(1)} %collective-permute-done.near, ...), custom_call_target="tpu_custom_call" | custom-call | flops 4000000000 | bytes 5551620 | tf_op jit(solution)/shard_map/pallas_call | solution.py:227
  23.0 11.3 %all-to-all-start = ((f32[64,1,640]{2,1,0:T(1,128)}), f32[64,1,640]{2,1,0:T(1,128)S(1)}, u32[]{:S(2)}, u32[]{:S(2)}) async-start(f32[64,1,640]{2,1,0:T(1,128)} %bitcast.10), calls=%async_computation | async-start | bytes 327680 | tf_op jit(solution)/shard_map/all_to_all | solution.py:251
  34.3 3.5 %collective-permute-start.3 = (bf16[1024,128]{1,0:T(8,128)(2,1)S(1)}, bf16[1024,128]{1,0:T(8,128)(2,1)S(1)}, u32[]{:S(2)}, u32[]{:S(2)}) collective-permute-start(bf16[1024,128]{1,0:T(8,128)(2,1)S(1)} %get-tuple-element.19), channel_id=1, source_target_pairs={{4,8},{12,16},{20,24},{28,32},{36,40},{44,48},{52,56},{60,64},{68,... | collective-permute-start | bytes 786440 | tf_op jit(solution)/shard_map/ppermute | solution.py:243
  37.8 0.1 collective-permute-start.2
  37.9 6.9 %all-to-all-done = f32[64,1,640]{2,1,0:T(1,128)S(1)} async-done(((f32[64,1,640]{2,1,0:T(1,128)}), f32[64,1,640]{2,1,0:T(1,128)S(1)}, u32[]{:S(2)}, u32[]{:S(2)}) %all-to-all-start) | async-done | bytes 163872 | tf_op jit(solution)/shard_map/all_to_all | solution.py:251
  44.8 0.1 reduce_sum.18
  45.0 8.0 %all_to_all.15 = f32[4,1,640]{2,1,0:T(1,128)S(1)} all-to-all(f32[4,1,640]{2,1,0:T(1,128)S(1)} %broadcast_in_dim.6), channel_id=1, replica_groups=mesh['space'=64,'dp'=4] {'dp'}, dimensions={0} | all-to-all | bytes 20480 | tf_op jit(solution)/shard_map/all_to_all | solution.py:254
  53.0 0.8 %broadcast_in_dim.7 = f32[64,1,640]{2,1,0:T(1,128)} broadcast(f32[640]{0:T(1024)S(1)} %reduce_sum.19), dimensions={2} | broadcast | bytes 166400 | tf_op jit(solution)/shard_map/broadcast_in_dim | solution.py:255
  53.8 7.0 %all-to-all-start.2 = ((f32[64,1,640]{2,1,0:T(1,128)}), f32[64,1,640]{2,1,0:T(1,128)S(1)}, u32[]{:S(2)}, u32[]{:S(2)}) async-start(f32[64,1,640]{2,1,0:T(1,128)} %broadcast_in_dim.7), calls=%async_computation.2 | async-start | bytes 327680 | tf_op jit(solution)/shard_map/all_to_all | solution.py:256
  60.7 0.0 collective-permute-done.3.far
  60.7 0.0 collective-permute-done.2.near
  60.7 3.4 %shard_map.103 = bf16[2,1024,128]{2,1,0:T(8,128)(2,1)} custom-call(s32[1]{0:T(128)} %bitcast.parity, bf16[2,1024,128]{2,1,0:T(8,128)(2,1)S(1)} %get-tuple-element.15.scaled, bf16[1024,128]{1,0:T(8,128)(2,1)S(1)} %collective-permute-done.2.near, bf16[1024,128]{1,0:T(8,128)(2,1)S(1)} %collective-permute-done.3.far, bf16[27,128]{1,0:T(8,128)(2,1)S(1)} %reshape.57.d1, ...), custom_call_target="tpu_custom_call" | custom-call | flops 4000000000 | bytes 1612548 | tf_op jit(solution)/shard_map/pallas_call | solution.py:227
  64.1 7.2 %all-to-all-done.2 = f32[64,1,640]{2,1,0:T(1,128)S(1)} async-done(((f32[64,1,640]{2,1,0:T(1,128)}), f32[64,1,640]{2,1,0:T(1,128)S(1)}, u32[]{:S(2)}, u32[]{:S(2)}) %all-to-all-start.2) | async-done | bytes 163872 | tf_op jit(solution)/shard_map/all_to_all | solution.py:256
  71.3 0.7 fusion.2
  72.0 0.6 reshape.63
  72.6 0.6 reshape.62
  (7 shorter events, 0.1 us)
Async XLA Ops:
  0.6 1.2 %copy-start.1 = (bf16[1,1,2,16,64,128]{5,4,3,2,1,0:T(8,128)(2,1)S(1)}, bf16[1,1,2,16,64,128]{5,4,3,2,1,0:T(8,128)(2,1)}, u32[]{:S(2)}) copy-start(bf16[1,1,2,16,64,128]{5,4,3,2,1,0:T(8,128)(2,1)} %param.11) | copy-start | bytes 1572868
  1.9 6.1 %copy-start.4 = (bf16[3,3,3,128]{3,2,1,0:T(4,128)(2,1)S(1)}, bf16[3,3,3,128]{3,2,1,0:T(4,128)(2,1)}, u32[]{:S(2)}) copy-start(bf16[3,3,3,128]{3,2,1,0:T(4,128)(2,1)} %param.7) | copy-start | bytes 20740
  1.9 6.1 %copy-start.5 = (bf16[3,3,3,128]{3,2,1,0:T(4,128)(2,1)S(1)}, bf16[3,3,3,128]{3,2,1,0:T(4,128)(2,1)}, u32[]{:S(2)}) copy-start(bf16[3,3,3,128]{3,2,1,0:T(4,128)(2,1)} %param.9) | copy-start | bytes 20740
  1.9 6.1 %copy-start = (bf16[1,1,2,16,64,128]{5,4,3,2,1,0:T(8,128)(2,1)S(1)}, bf16[1,1,2,16,64,128]{5,4,3,2,1,0:T(8,128)(2,1)}, u32[]{:S(2)}) copy-start(bf16[1,1,2,16,64,128]{5,4,3,2,1,0:T(8,128)(2,1)} %param.6) | copy-start | bytes 1572868
  1.9 6.1 %copy-start.3 = (bf16[128,128]{1,0:T(8,128)(2,1)S(1)}, bf16[128,128]{1,0:T(8,128)(2,1)}, u32[]{:S(2)}) copy-start(bf16[128,128]{1,0:T(8,128)(2,1)} %p1.5) | copy-start | bytes 98308
  2.8 5.3 %copy-start.2 = (bf16[128,128]{1,0:T(8,128)(2,1)S(1)}, bf16[128,128]{1,0:T(8,128)(2,1)}, u32[]{:S(2)}) copy-start(bf16[128,128]{1,0:T(8,128)(2,1)} %p2.3) | copy-start | bytes 98308
  2.8 5.2 %collective-permute-start = (bf16[2,1024,128]{2,1,0:T(8,128)(2,1)}, bf16[2,1024,128]{2,1,0:T(8,128)(2,1)S(1)}, u32[]{:S(2)}, u32[]{:S(2)}) collective-permute-start(bf16[2,1024,128]{2,1,0:T(8,128)(2,1)} %get-tuple-element.18), channel_id=1, source_target_pairs={{0,4},{4,0},{8,12},{12,8},{16,20},{20,16},{24,28},{28,24},{32,36},... | collective-permute-start | bytes 1572872 | tf_op jit(solution)/shard_map/ppermute | solution.py:244
  6.1 10.5 %collective-permute-start.1 = (bf16[2,1024,128]{2,1,0:T(8,128)(2,1)S(1)}, bf16[2,1024,128]{2,1,0:T(8,128)(2,1)S(1)}, u32[]{:S(2)}, u32[]{:S(2)}) collective-permute-start(bf16[2,1024,128]{2,1,0:T(8,128)(2,1)S(1)} %get-tuple-element.17), channel_id=1, source_target_pairs={{4,8},{12,16},{20,24},{28,32},{36,40},{44,48},{52,56},{60,64},{68,... | collective-permute-start | bytes 1572872 | tf_op jit(solution)/shard_map/ppermute | solution.py:243
  23.0 21.9 %all-to-all-start = ((f32[64,1,640]{2,1,0:T(1,128)}), f32[64,1,640]{2,1,0:T(1,128)S(1)}, u32[]{:S(2)}, u32[]{:S(2)}) async-start(f32[64,1,640]{2,1,0:T(1,128)} %bitcast.10), calls=%async_computation | async-start | bytes 327680 | tf_op jit(solution)/shard_map/all_to_all | solution.py:251
  34.3 26.4 %collective-permute-start.3 = (bf16[1024,128]{1,0:T(8,128)(2,1)S(1)}, bf16[1024,128]{1,0:T(8,128)(2,1)S(1)}, u32[]{:S(2)}, u32[]{:S(2)}) collective-permute-start(bf16[1024,128]{1,0:T(8,128)(2,1)S(1)} %get-tuple-element.19), channel_id=1, source_target_pairs={{4,8},{12,16},{20,24},{28,32},{36,40},{44,48},{52,56},{60,64},{68,... | collective-permute-start | bytes 786440 | tf_op jit(solution)/shard_map/ppermute | solution.py:243
  37.8 22.9 %collective-permute-start.2 = (bf16[1024,128]{1,0:T(8,128)(2,1)S(1)}, bf16[1024,128]{1,0:T(8,128)(2,1)S(1)}, u32[]{:S(2)}, u32[]{:S(2)}) collective-permute-start(bf16[1024,128]{1,0:T(8,128)(2,1)S(1)} %get-tuple-element.20), channel_id=1, source_target_pairs={{0,4},{4,0},{8,12},{12,8},{16,20},{20,16},{24,28},{28,24},{32,36},... | collective-permute-start | bytes 786440 | tf_op jit(solution)/shard_map/ppermute | solution.py:244
  53.8 17.5 %all-to-all-start.2 = ((f32[64,1,640]{2,1,0:T(1,128)}), f32[64,1,640]{2,1,0:T(1,128)S(1)}, u32[]{:S(2)}, u32[]{:S(2)}) async-start(f32[64,1,640]{2,1,0:T(1,128)} %broadcast_in_dim.7), calls=%async_computation.2 | async-start | bytes 327680 | tf_op jit(solution)/shard_map/all_to_all | solution.py:256

commit v2 on v1

v2 whole, which is shorter than its diff:
```python
import functools
import math

import jax
import jax.numpy as jnp
from jax import lax
from jax.experimental import pallas as pl
from jax.experimental.pallas import tpu as pltpu
from jax.sharding import PartitionSpec as P

CH = 128
LINE = 64
CELLS = 1024
PADDED = CELLS + 2 * LINE
ROWS = 256
TERMS = 320
VMEM_LIMIT = 24 * 1024 * 1024


def mm(a, b):
    return jnp.dot(a, b, preferred_element_type=jnp.float32)


def keep_mask(count, edge):
    return lax.broadcasted_iota(jnp.int32, (count, 1), 0) % LINE != edge


def from_before(v):
    return jnp.where(keep_mask(v.shape[0], 0), pltpu.roll(v, 1, 0), 0.0)


def from_after(v):
    return jnp.where(keep_mask(v.shape[0], LINE - 1), pltpu.roll(v, v.shape[0] - 1, 0), 0.0)


def shift_sum(products, width):
    return (
        from_before(products[:, :width])
        + products[:, width : 2 * width]
        + from_after(products[:, 2 * width :])
    )


def set_plane(ref, slot, plane):
    edge = jnp.zeros((LINE, CH), jnp.bfloat16)
    ref[slot, 0:LINE, :] = edge
    ref[slot, LINE : LINE + CELLS, :] = plane
    ref[slot, LINE + CELLS : PADDED, :] = edge


def windows(ref, slot, count, start):
    return jnp.concatenate(
        [
            ref[slot + a, start + b * LINE : start + b * LINE + ROWS, :]
            for a in range(count)
            for b in range(3)
        ],
        axis=1,
    )


def fill_taps(ref, tap_matrix):
    for a in range(3):
        for b in range(3):
            for e in range(3):
                row, col = ((3 * a + b) * CH, e * CH)
                ref[row : row + CH, col : col + CH] = tap_matrix(9 * a + 3 * b + e)


def tap_rows(ref, a, count):
    return ref[pl.ds(pl.multiple_of(a * 3 * CH, CH), count * 3 * CH), :]


def columns_of(depth):
    padded = jnp.concatenate([depth, jnp.zeros((CH - 27, CH), jnp.float32)], axis=0)
    return padded.T


def forward_taps(cols, point):
    return lambda s: (cols[:, s : s + 1] * point).astype(jnp.bfloat16)


def backward_taps(depth, point_t):
    return lambda s: (depth[26 - s : 27 - s, :] * point_t).astype(jnp.bfloat16)


def tap_sums(left_t, planes, x, combine):
    order = [(a, b) for a in range(3) for b in range(3)]
    for at in range(0, 9, 2):
        group = order[at : at + 2]
        right = jnp.concatenate(
            [planes[x + a, b * LINE : b * LINE + CELLS, :] for a, b in group], axis=1
        )
        sums = mm(left_t[...], right)
        for i, (a, b) in enumerate(group):
            for e in range(3):
                combine(9 * a + 3 * b + e, sums[e * CH : (e + 1) * CH, i * CH : (i + 1) * CH])


def activate(value, back, scaled_out, scaled_t, hidden_t, start):
    sigma = jax.nn.sigmoid(value)
    hidden = (value * sigma).astype(jnp.bfloat16).astype(jnp.float32)
    scaled = (back * (sigma * (1.0 + value * (1.0 - sigma)))).astype(jnp.bfloat16)
    scaled_out[start : start + ROWS, :] = scaled
    scaled = scaled.astype(jnp.float32)
    for ref, v in ((scaled_t, scaled), (hidden_t, hidden)):
        shifted = jnp.concatenate([from_after(v), v, from_before(v)], axis=1)
        ref[:, start : start + ROWS] = shifted.astype(jnp.bfloat16).T


def weight_terms(factor, x, planes_in, planes_up, scaled_t, hidden_t, weights, total, before, terms):
    depth_one, point_one, depth_two, point_two = weights
    point_one_t = point_one.T
    cols_two = columns_of(depth_two)
    lane = lax.broadcasted_iota(jnp.int32, (CH, CH), 1)
    total[...] = jnp.zeros((3, CH, CH), jnp.float32)
    terms[...] = jnp.zeros((TERMS, CH), jnp.float32) if before is None else before[...]

    def layer_one(s, block):
        total[0] += depth_one[s : s + 1, :] * block
        terms[s : s + 1, :] += jnp.sum(point_one_t * block, axis=0, keepdims=True) * factor

    tap_sums(scaled_t, planes_in, x, layer_one)
    terms[32:160, :] += total[0].T * factor

    def layer_two(s, block):
        s = 26 - s
        total[1] += cols_two[:, s : s + 1] * block
        total[2] += jnp.where(lane == s, jnp.sum(point_two * block, axis=1, keepdims=True), 0.0)

    tap_sums(hidden_t, planes_up, x, layer_two)
    terms[192:320, :] += total[1] * factor
    terms[160:192, :] += total[2].T[:32, :] * factor


def place_planes(planes, block, core, near, far):
    for x in range(2):
        set_plane(planes, 1 + x, block[x])
    if near is not None:
        set_plane(planes, 3 - 3 * core, near)
    if far is not None:
        set_plane(planes, 3 * core, far)


def near_kernel(
    factor,
    parity, block_in, block_up, near, d1, p1, d2, p2,
    scaled_out, pre, carried, far_w1, far_w2, terms,
    planes_in, planes_up, w_one, w_two, scaled_t, hidden_t, total,
):
    core = parity[0]
    inner = 1 - core
    weights = tuple(w[...].astype(jnp.float32) for w in (d1, p1, d2, p2))
    depth_one, point_one, depth_two, point_two = weights
    place_planes(planes_in, block_in, core, near[0], None)
    place_planes(planes_up, block_up, core, near[1], None)
    fill_taps(w_one, forward_taps(columns_of(depth_one), point_one))
    fill_taps(w_two, backward_taps(depth_two, point_two.T))
    for start in range(0, CELLS, ROWS):
        value = shift_sum(mm(windows(planes_in, inner, 3, start), w_one[...]), CH)
        back = shift_sum(mm(windows(planes_up, inner, 3, start), w_two[...]), CH)
        activate(value, back, scaled_out, scaled_t, hidden_t, start)
    weight_terms(
        factor, inner, planes_in, planes_up, scaled_t, hidden_t, weights, total, None, terms
    )
    for planes, w, out, far_w in (
        (planes_in, w_one, pre, far_w1),
        (planes_up, w_two, carried, far_w2),
    ):
        far_w[...] = tap_rows(w, 2 * core, 1)
        for start in range(0, CELLS, ROWS):
            products = mm(windows(planes, 1, 2, start), tap_rows(w, 1 - core, 2))
            out[start : start + ROWS, :] = shift_sum(products, CH)


def far_kernel(
    factor,
    parity, block_in, block_up, far, pre, carried, far_w1, far_w2, d1, p1, d2, p2, before,
    scaled_out, terms,
    planes_in, planes_up, scaled_t, hidden_t, total,
):
    core = parity[0]
    weights = tuple(w[...].astype(jnp.float32) for w in (d1, p1, d2, p2))
    place_planes(planes_in, block_in, core, None, far[0])
    place_planes(planes_up, block_up, core, None, far[1])
    for start in range(0, CELLS, ROWS):
        value = shift_sum(mm(windows(planes_in, 3 * core, 1, start), far_w1[...]), CH)
        back = shift_sum(mm(windows(planes_up, 3 * core, 1, start), far_w2[...]), CH)
        value = value + pre[start : start + ROWS, :]
        back = back + carried[start : start + ROWS, :]
        activate(value, back, scaled_out, scaled_t, hidden_t, start)
    weight_terms(
        factor, core, planes_in, planes_up, scaled_t, hidden_t, weights, total, before, terms
    )


def last_kernel(parity, inner, outer, near, far, d1, p1, out, planes, w):
    core = parity[0]
    depth_one = d1[...].astype(jnp.float32)
    fill_taps(w, backward_taps(depth_one, p1[...].astype(jnp.float32).T))
    set_plane(planes, 2 - core, inner[...])
    set_plane(planes, 1 + core, outer[...])
    set_plane(planes, 3 - 3 * core, near[...])
    set_plane(planes, 3 * core, far[...])
    for x in range(2):
        for start in range(0, CELLS, ROWS):
            grad = shift_sum(mm(windows(planes, x, 3, start), w[...]), CH)
            out[x, start : start + ROWS, :] = grad.astype(jnp.bfloat16)


def parts_kernel(sums, depth_one, point_one, depth_two, point_two):
    for a in range(3):
        for b in range(3):
            row = 9 * a + 3 * b
            depth_one[a, b] = sums[row : row + 3, :]
            depth_two[a, b] = sums[160 + row : 163 + row, :]
    point_one[...] = sums[32:160, :]
    point_two[...] = sums[192:320, :]


def call(kernel, scratch, outs, flops, *args):
    vmem = pl.BlockSpec(memory_space=pltpu.VMEM)
    smem = pl.BlockSpec(memory_space=pltpu.SMEM)
    moved = sum(a.size * a.dtype.itemsize for a in args) + sum(
        o.size * o.dtype.itemsize for o in outs
    )
    return pl.pallas_call(
        kernel,
        out_shape=outs,
        in_specs=[smem if a.dtype == jnp.int32 else vmem for a in args],
        out_specs=[vmem] * len(outs),
        scratch_shapes=scratch,
        cost_estimate=pl.CostEstimate(flops=flops, bytes_accessed=moved, transcendentals=0),
        compiler_params=pltpu.CompilerParams(vmem_limit_bytes=VMEM_LIMIT),
    )(*args)


SPACE = ("outer", "ring", "core")
ACROSS = ("outer", "core", "dp")


def with_other_core(v):
    return lax.ppermute(v, "core", [(0, 1), (1, 0)])


def with_other_chip(v):
    count = math.prod(lax.axis_size(name) for name in SPACE)
    pairs = [(i, i + 1) for i in range(1, count - 1, 2)]
    return lax.ppermute(v, SPACE, pairs + [(j, i) for i, j in pairs])


def sum_of_terms(terms):
    count = math.prod(lax.axis_size(name) for name in ACROSS)
    tiles = terms.reshape(count, 1, -1)
    share = lax.all_to_all(tiles, ACROSS, 0, 0, tiled=True).sum(axis=0)
    copies = jnp.broadcast_to(share, (lax.axis_size("ring"), *share.shape))
    share = lax.all_to_all(copies, "ring", 0, 0, tiled=True).sum(axis=0)
    copies = jnp.broadcast_to(share, (count, *share.shape))
    return lax.all_to_all(copies, ACROSS, 0, 0, tiled=True).reshape(TERMS, CH)


def on_device(inputs, depth_one, point_one, depth_two, point_two, cotangent):
    f32, bf16 = jnp.float32, jnp.bfloat16
    shape = jax.ShapeDtypeStruct
    block_in = inputs.reshape(2, CELLS, CH)
    block_up = cotangent.reshape(2, CELLS, CH)
    d1 = depth_one.reshape(27, CH)
    d2 = depth_two.reshape(27, CH)
    core = lax.axis_index("core")
    parity = core.astype(jnp.int32).reshape(1)

    def both(x):
        return jnp.concatenate(
            [lax.dynamic_slice_in_dim(block, x, 1, 0) for block in (block_in, block_up)], axis=0
        )

    far = with_other_chip(both(core))
    near = with_other_core(both(1 - core))
    slots = pltpu.VMEM((4, PADDED, CH), bf16)
    taps_w = pltpu.VMEM((9 * CH, 3 * CH), bf16)
    flipped = pltpu.VMEM((3 * CH, CELLS), bf16)
    totals = pltpu.VMEM((3, CH, CH), f32)
    devices = math.prod(lax.axis_size(name) for name in ("dp", *SPACE))
    factor = 1.0 / math.sqrt(devices * 2 * CELLS)
    inner, pre, carried, far_w1, far_w2, terms = call(
        functools.partial(near_kernel, factor),
        [slots, slots, taps_w, taps_w, flipped, flipped, totals],
        [shape((CELLS, CH), bf16)]
        + [shape((CELLS, CH), f32)] * 2
        + [shape((3 * CH, 3 * CH), bf16)] * 2
        + [shape((TERMS, CH), f32)],
        8_000_000_000,
        parity, block_in, block_up, near, d1, point_one, d2, point_two,
    )
    inner_beside = with_other_core(inner)
    outer, terms = call(
        functools.partial(far_kernel, factor),
        [slots, slots, flipped, flipped, totals],
        [shape((CELLS, CH), bf16), shape((TERMS, CH), f32)],
        4_000_000_000,
        parity, block_in, block_up, far, pre, carried, far_w1, far_w2,
        d1, point_one, d2, point_two, terms,
    )
    outer_beside = with_other_chip(outer)
    (grad,) = call(
        last_kernel,
        [slots, taps_w],
        [shape((2, CELLS, CH), bf16)],
        4_000_000_000,
        parity, inner, outer, inner_beside, outer_beside, d1, point_one,
    )
    depth, point = (shape((3, 3, 3, CH), f32), shape((CH, CH), f32))
    parts = call(parts_kernel, [], [depth, point, depth, point], 0, sum_of_terms(terms))
    return (grad.reshape(inputs.shape), *parts)


def solution(mesh):
    count, samples = (mesh.shape["space"], mesh.shape["dp"])
    ring = min(8, count // 2)
    grid = mesh.devices.reshape(count // (2 * ring), ring, 2, samples)
    split = jax.sharding.Mesh(grid, (*SPACE, "dp"))
    slabs = P("dp", SPACE, None, None, None, None)
    return jax.shard_map(
        on_device,
        mesh=split,
        in_specs=(slabs, P(), P(), P(), P(), slabs),
        out_specs=(slabs, P(), P(), P(), P()),
        check_vma=False,
    )
```

time: 73.6 us -> 67.2 us (0.913)
  blocking collectives: 7.99 us -> 30.2 us
  starting transfers between devices: 27 us -> 13 us
  waiting for transfers between devices: 18.6 us -> 5.57 us
  local copies, waits for them, and re-layouts: 3.95 us -> 2.1 us
  Pallas kernels: 13.8 us -> 15 us
  other arithmetic: 1.08 us -> 0.25 us
    all_to_all x1 -> x2, blocking collectives: 7.99 us -> 30.2 us  [the longest x1 20.8 us: sum_of_terms(): share = lax.all_to_all(tiles, ACROSS, 0, 0, tiled=True).sum(axis=0)]
    all_to_all x2 -> x1, starting transfers between devices: 18.2 us -> 5.2 us  [sum_of_terms(): return lax.all_to_all(copies, ACROSS, 0, 0, tiled=True).reshape(TERMS, CH)]
    all_to_all x2 -> x1, waiting for transfers between devices: 14.1 us -> 4.22 us  [sum_of_terms(): return lax.all_to_all(copies, ACROSS, 0, 0, tiled=True).reshape(TERMS, CH)]
    ppermute x4, waiting for transfers between devices: 4.46 us -> 1.35 us  [the longest x2 1.34 us: with_other_chip(): return lax.ppermute(v, SPACE, pairs + [(j, i) for i, j in pairs])]
    slice x4 -> x0, local copies, waits for them, and re-layouts: 1.82 us -> none  [the longest x2 1.16 us: on_device(): last = jnp.stack([block_in[1], block_up[1]])]
    dynamic_slice x0 -> x1, local copies, waits for them, and re-layouts: none -> 1.26 us  [both(): lax.dynamic_slice_in_dim(block, x, 1, 0)]
    pallas_call x3 -> x4, Pallas kernels: 13.8 us -> 15 us  [call(): pl.pallas_call(kernel, out_shape=outs, in_specs=[smem if a.dtype == jnp.i...]
    reshape x2 -> x0, local copies, waits for them, and re-layouts: 1.23 us -> none  [the longest x1 0.61 us: on_device(): sums[160:187].reshape(3, 3, 3, CH)]
  transfers between devices with their start and end apart: 6 -> 5, of which waited for: 3 -> 2; matrix products, arithmetic and copies ran while one was open for 1% -> 1% of each run, Pallas kernels for 10% -> 16%
where the time goes in v2:
time: 67.2 us; the launch traced here: 66.9 us
  blocking collectives  30.2 us (45%)
  Pallas kernels  15 us (22%)
  starting transfers between devices  13 us (19%)
  waiting for transfers between devices  5.57 us (8%)
  local copies, waits for them, and re-layouts  2.1 us (3%)
  between operations  0.8 us (1%)
    all_to_all x1, blocking collectives, sum_of_terms(): share = lax.all_to_all(tiles, ACROSS, 0, 0, tiled=True).sum(axis=0)  20.8 us
    pallas_call x4, Pallas kernels, call(): pl.pallas_call(kernel, out_shape=outs, in_specs=[smem if a.dtype == jnp.i...  15 us
    all_to_all x1, blocking collectives, sum_of_terms(): share = lax.all_to_all(copies, 'ring', 0, 0, tiled=True).sum(axis=0)  9.33 us
    all_to_all x1, starting transfers between devices, sum_of_terms(): return lax.all_to_all(copies, ACROSS, 0, 0, tiled=True).reshape(TERMS, CH)  5.2 us
    ppermute x2, starting transfers between devices, with_other_chip(): return lax.ppermute(v, SPACE, pairs + [(j, i) for i, j in pairs])  4.36 us
    all_to_all x1, waiting for transfers between devices, sum_of_terms(): return lax.all_to_all(copies, ACROSS, 0, 0, tiled=True).reshape(TERMS, CH)  4.22 us
    ppermute x2, starting transfers between devices, with_other_core(): return lax.ppermute(v, 'core', [(0, 1), (1, 0)])  3.42 us
  transfers between devices with their start and end apart: 5, of which 2 were waited for; matrix products, arithmetic and copies ran while one was open for 1% of the time, Pallas kernels for 16%

profile of v2, /device:TPU:1, one launch (start us, length us, event | category | flops | bytes accessed | tf_op | source)
XLA Modules:
  0.0 66.9 jit_solution(3767669813678111366)
XLA Ops:
  0.6 1.3 %constant_dynamic-slice_fusion = (bf16[1,1024,128]{2,1,0:T(8,128)(2,1)S(1)}, bf16[1,1024,128]{2,1,0:T(8,128)(2,1)S(1)}, bf16[1,1024,128]{2,1,0:T(8,128)(2,1)S(1)}, bf16[1,1024,128]{2,1,0:T(8,128)(2,1)S(1)}) fusion(bf16[2,1024,128]{2,1,0:T(8,128)(2,1)} %bitcast.10, s32[]{:T(128)S(6)} %select_n.9, s32[]{:T(128)S(6)} %select_n.8, bf16[2,1024,128]{2,1,0:T(8,128)(2,1)} %bitcast.7), kind=kLoop, calls=%fused_computation.2 | loop fusion | bytes 2097160 | tf_op jit(solution)/shard_map/dynamic_slice | solution.py:274
  1.9 0.0 copy-start.4
  1.9 0.0 copy-start.5
  1.9 0.0 copy-start.3
  1.9 0.1 pad_maximum_fusion
  2.0 3.3 %collective-permute-start = (bf16[2,1024,128]{2,1,0:T(8,128)(2,1)S(1)}, bf16[2,1024,128]{2,1,0:T(8,128)(2,1)S(1)}, u32[]{:S(2)}, u32[]{:S(2)}) collective-permute-start(bf16[2,1024,128]{2,1,0:T(8,128)(2,1)S(1)} %pad_maximum_fusion), channel_id=1, source_target_pairs={{0,4},{4,0},{1,5},{5,1},{2,6},{6,2},{3,7},{7,3},{8,12},{12,8},{9,1... | collective-permute-start | bytes 1572872 | tf_op jit(solution)/shard_map/ppermute | solution.py:243
  5.3 0.0 copy-start
  5.3 0.0 copy-start.1
  5.3 0.1 pad_maximum_fusion.1
  5.4 0.0 copy-start.2
  5.4 2.1 %collective-permute-start.1 = (bf16[2,1024,128]{2,1,0:T(8,128)(2,1)S(1)}, bf16[2,1024,128]{2,1,0:T(8,128)(2,1)S(1)}, u32[]{:S(2)}, u32[]{:S(2)}) collective-permute-start(bf16[2,1024,128]{2,1,0:T(8,128)(2,1)S(1)} %pad_maximum_fusion.1), channel_id=1, source_target_pairs={{4,8},{12,16},{20,24},{28,32},{36,40},{44,48},{52,56},{60,64},{68,... | collective-permute-start | bytes 1572872 | tf_op jit(solution)/shard_map/ppermute | solution.py:249
  7.5 0.0 copy-done.4
  7.5 0.0 copy-done.5
  7.5 0.0 collective-permute-done.near
  7.5 0.0 copy-done.3
  7.5 0.0 copy-done
  7.5 0.0 copy-done.1
  7.6 0.0 copy-done.2
  7.6 7.1 %shard_map.101 = (bf16[1024,128]{1,0:T(8,128)(2,1)S(1)}, f32[1024,128]{1,0:T(8,128)S(1)}, f32[1024,128]{1,0:T(8,128)S(1)}, bf16[384,384]{1,0:T(8,128)(2,1)S(1)},...) custom-call(s32[1]{0:T(128)} %bitcast.parity, bf16[2,1024,128]{2,1,0:T(8,128)(2,1)S(1)} %bitcast.8, ...), custom_call_target="tpu_custom_call" | custom-call | flops 8000000000 | bytes 3716612 | tf_op jit(solution)/shard_map/pallas_call | solution.py:227
  14.7 1.3 %collective-permute-done.1.far = bf16[2,1024,128]{2,1,0:T(8,128)(2,1)S(1)} collective-permute-done((bf16[2,1024,128]{2,1,0:T(8,128)(2,1)S(1)}, bf16[2,1024,128]{2,1,0:T(8,128)(2,1)S(1)}, u32[]{:S(2)}, u32[]{:S(2)}) %collective-permute-start.1) | collective-permute-done | bytes 524320 | tf_op jit(solution)/shard_map/ppermute | solution.py:249
  16.0 3.6 %shard_map.102 = (bf16[1024,128]{1,0:T(8,128)(2,1)S(1)}, f32[320,128]{1,0:T(8,128)S(1)}) custom-call(s32[1]{0:T(128)} %bitcast.parity, bf16[2,1024,128]{2,1,0:T(8,128)(2,1)S(1)} %bitcast.9, bf16[2,1024,128]{2,1,0:T(8,128)(2,1)S(1)} %bitcast.12, bf16[2,1024,128]{2,1,0:T(8,128)(2,1)S(1)} %collective-permute-done.1.far, f32[1024,128]{1,0:T(8,128)S(1)} %get-tuple-element.18.pre, ...), custom_call_target="tpu_custom_call" | custom-call | flops 4000000000 | bytes 3880452 | tf_op jit(solution)/shard_map/pallas_call | solution.py:227
  19.6 2.3 %collective-permute-start.3 = (bf16[1024,128]{1,0:T(8,128)(2,1)S(1)}, bf16[1024,128]{1,0:T(8,128)(2,1)S(1)}, u32[]{:S(2)}, u32[]{:S(2)}) collective-permute-start(bf16[1024,128]{1,0:T(8,128)(2,1)S(1)} %get-tuple-element.23.outer), channel_id=1, source_target_pairs={{4,8},{12,16},{20,24},{28,32},{36,40},{44,48},{52,56},{60,64},{68,... | collective-permute-start | bytes 786440 | tf_op jit(solution)/shard_map/ppermute | solution.py:249
  21.9 0.1 collective-permute-start.2
  22.0 20.8 %all_to_all.15 = f32[32,1,1280]{2,1,0:T(1,128)S(1)} all-to-all(f32[32,1,1280]{2,1,0:T(1,128)S(1)} %bitcast.13), channel_id=1, replica_groups=mesh['outer'=4,'ring'=8,'core'=2,'dp'=4] {'outer','core','dp'}, dimensions={0} | all-to-all | bytes 327680 | tf_op jit(solution)/shard_map/all_to_all | solution.py:255
  42.8 0.1 reduce_sum.18
  43.0 9.3 %all_to_all.16 = f32[8,1,1280]{2,1,0:T(1,128)S(1)} all-to-all(f32[8,1,1280]{2,1,0:T(1,128)S(1)} %broadcast_in_dim.6), channel_id=1, replica_groups=mesh['outer'=4,'ring'=8,'core'=2,'dp'=4] {'ring'}, dimensions={0} | all-to-all | bytes 81920 | tf_op jit(solution)/shard_map/all_to_all | solution.py:257
  52.4 0.7 %broadcast_in_dim.7 = f32[32,1,1280]{2,1,0:T(1,128)} broadcast(f32[1280]{0:T(1024)S(1)} %reduce_sum.19), dimensions={2} | broadcast | bytes 168960 | tf_op jit(solution)/shard_map/broadcast_in_dim | solution.py:258
  53.1 5.2 %all-to-all-start.2 = ((f32[32,1,1280]{2,1,0:T(1,128)}), f32[32,1,1280]{2,1,0:T(1,128)S(1)}, u32[]{:S(2)}, u32[]{:S(2)}) async-start(f32[32,1,1280]{2,1,0:T(1,128)} %broadcast_in_dim.7), calls=%async_computation.2 | async-start | bytes 327680 | tf_op jit(solution)/shard_map/all_to_all | solution.py:259
  58.3 0.0 collective-permute-done.3.far
  58.3 0.0 collective-permute-done.2.near
  58.3 3.7 %shard_map.103 = bf16[2,1024,128]{2,1,0:T(8,128)(2,1)} custom-call(s32[1]{0:T(128)} %bitcast.parity, bf16[1024,128]{1,0:T(8,128)(2,1)S(1)} %get-tuple-element.17.inner, bf16[1024,128]{1,0:T(8,128)(2,1)S(1)} %get-tuple-element.23.outer, bf16[1024,128]{1,0:T(8,128)(2,1)S(1)} %collective-permute-done.2.near, bf16[1024,128]{1,0:T(8,128)(2,1)S(1)} %collective-permute-done.3.far, ...), custom_call_target="tpu_custom_call" | custom-call | flops 4000000000 | bytes 1612548 | tf_op jit(solution)/shard_map/pallas_call | solution.py:227
  62.0 4.2 %all-to-all-done.2 = f32[32,1,1280]{2,1,0:T(1,128)S(1)} async-done(((f32[32,1,1280]{2,1,0:T(1,128)}), f32[32,1,1280]{2,1,0:T(1,128)S(1)}, u32[]{:S(2)}, u32[]{:S(2)}) %all-to-all-start.2) | async-done | bytes 163872 | tf_op jit(solution)/shard_map/all_to_all | solution.py:259
  66.3 0.7 %shard_map.104 = (f32[3,3,3,128]{3,2,1,0:T(4,128)}, f32[128,128]{1,0:T(8,128)}, f32[3,3,3,128]{3,2,1,0:T(4,128)}, f32[128,128]{1,0:T(8,128)}) custom-call(f32[320,128]{1,0:T(8,128)S(1)} %bitcast.6), custom_call_target="tpu_custom_call" | custom-call | bytes 322560 | tf_op jit(solution)/shard_map/pallas_call | solution.py:227
  (4 shorter events, 0.1 us)
Async XLA Ops:
  1.9 5.6 %copy-start.4 = (bf16[3,3,3,128]{3,2,1,0:T(4,128)(2,1)S(1)}, bf16[3,3,3,128]{3,2,1,0:T(4,128)(2,1)}, u32[]{:S(2)}) copy-start(bf16[3,3,3,128]{3,2,1,0:T(4,128)(2,1)} %param.7) | copy-start | bytes 20740
  1.9 5.6 %copy-start.5 = (bf16[3,3,3,128]{3,2,1,0:T(4,128)(2,1)S(1)}, bf16[3,3,3,128]{3,2,1,0:T(4,128)(2,1)}, u32[]{:S(2)}) copy-start(bf16[3,3,3,128]{3,2,1,0:T(4,128)(2,1)} %param.9) | copy-start | bytes 20740
  1.9 5.6 %copy-start.3 = (bf16[128,128]{1,0:T(8,128)(2,1)S(1)}, bf16[128,128]{1,0:T(8,128)(2,1)}, u32[]{:S(2)}) copy-start(bf16[128,128]{1,0:T(8,128)(2,1)} %p1.5) | copy-start | bytes 98308
  2.0 5.5 %collective-permute-start = (bf16[2,1024,128]{2,1,0:T(8,128)(2,1)S(1)}, bf16[2,1024,128]{2,1,0:T(8,128)(2,1)S(1)}, u32[]{:S(2)}, u32[]{:S(2)}) collective-permute-start(bf16[2,1024,128]{2,1,0:T(8,128)(2,1)S(1)} %pad_maximum_fusion), channel_id=1, source_target_pairs={{0,4},{4,0},{1,5},{5,1},{2,6},{6,2},{3,7},{7,3},{8,12},{12,8},{9,1... | collective-permute-start | bytes 1572872 | tf_op jit(solution)/shard_map/ppermute | solution.py:243
  5.3 2.2 %copy-start = (bf16[1,1,2,16,64,128]{5,4,3,2,1,0:T(8,128)(2,1)S(1)}, bf16[1,1,2,16,64,128]{5,4,3,2,1,0:T(8,128)(2,1)}, u32[]{:S(2)}) copy-start(bf16[1,1,2,16,64,128]{5,4,3,2,1,0:T(8,128)(2,1)} %param.6) | copy-start | bytes 1572868
  5.3 2.2 %copy-start.1 = (bf16[1,1,2,16,64,128]{5,4,3,2,1,0:T(8,128)(2,1)S(1)}, bf16[1,1,2,16,64,128]{5,4,3,2,1,0:T(8,128)(2,1)}, u32[]{:S(2)}) copy-start(bf16[1,1,2,16,64,128]{5,4,3,2,1,0:T(8,128)(2,1)} %param.11) | copy-start | bytes 1572868
  5.4 2.2 %copy-start.2 = (bf16[128,128]{1,0:T(8,128)(2,1)S(1)}, bf16[128,128]{1,0:T(8,128)(2,1)}, u32[]{:S(2)}) copy-start(bf16[128,128]{1,0:T(8,128)(2,1)} %p2.3) | copy-start | bytes 98308
  5.4 10.6 %collective-permute-start.1 = (bf16[2,1024,128]{2,1,0:T(8,128)(2,1)S(1)}, bf16[2,1024,128]{2,1,0:T(8,128)(2,1)S(1)}, u32[]{:S(2)}, u32[]{:S(2)}) collective-permute-start(bf16[2,1024,128]{2,1,0:T(8,128)(2,1)S(1)} %pad_maximum_fusion.1), channel_id=1, source_target_pairs={{4,8},{12,16},{20,24},{28,32},{36,40},{44,48},{52,56},{60,64},{68,... | collective-permute-start | bytes 1572872 | tf_op jit(solution)/shard_map/ppermute | solution.py:249
  19.6 38.7 %collective-permute-start.3 = (bf16[1024,128]{1,0:T(8,128)(2,1)S(1)}, bf16[1024,128]{1,0:T(8,128)(2,1)S(1)}, u32[]{:S(2)}, u32[]{:S(2)}) collective-permute-start(bf16[1024,128]{1,0:T(8,128)(2,1)S(1)} %get-tuple-element.23.outer), channel_id=1, source_target_pairs={{4,8},{12,16},{20,24},{28,32},{36,40},{44,48},{52,56},{60,64},{68,... | collective-permute-start | bytes 786440 | tf_op jit(solution)/shard_map/ppermute | solution.py:249
  21.9 36.4 %collective-permute-start.2 = (bf16[1024,128]{1,0:T(8,128)(2,1)S(1)}, bf16[1024,128]{1,0:T(8,128)(2,1)S(1)}, u32[]{:S(2)}, u32[]{:S(2)}) collective-permute-start(bf16[1024,128]{1,0:T(8,128)(2,1)S(1)} %get-tuple-element.17.inner), channel_id=1, source_target_pairs={{0,4},{4,0},{1,5},{5,1},{2,6},{6,2},{3,7},{7,3},{8,12},{12,8},{9,1... | collective-permute-start | bytes 786440 | tf_op jit(solution)/shard_map/ppermute | solution.py:243
  53.1 13.2 %all-to-all-start.2 = ((f32[32,1,1280]{2,1,0:T(1,128)}), f32[32,1,1280]{2,1,0:T(1,128)S(1)}, u32[]{:S(2)}, u32[]{:S(2)}) async-start(f32[32,1,1280]{2,1,0:T(1,128)} %broadcast_in_dim.7), calls=%async_computation.2 | async-start | bytes 327680 | tf_op jit(solution)/shard_map/all_to_all | solution.py:259

commit v3 on v2

--- a/solution.py
+++ b/solution.py
@@ -194,7 +194,7 @@
     )
 
 
-def last_kernel(parity, inner, outer, near, far, d1, p1, out, planes, w):
+def last_kernel(parity, inner, outer, near, far, d1, p1, out, done, planes, w):
     core = parity[0]
     depth_one = d1[...].astype(jnp.float32)
     fill_taps(w, backward_taps(depth_one, p1[...].astype(jnp.float32).T))
@@ -206,9 +206,10 @@
         for start in range(0, CELLS, ROWS):
             grad = shift_sum(mm(windows(planes, x, 3, start), w[...]), CH)
             out[x, start : start + ROWS, :] = grad.astype(jnp.bfloat16)
-
-
-def parts_kernel(sums, depth_one, point_one, depth_two, point_two):
+    done[...] = jnp.zeros((8, CH), jnp.float32)
+
+
+def parts_kernel(sums, done, depth_one, point_one, depth_two, point_two):
     for a in range(3):
         for b in range(3):
             row = 9 * a + 3 * b
@@ -249,12 +250,19 @@
     return lax.ppermute(v, SPACE, pairs + [(j, i) for i, j in pairs])
 
 
-def sum_of_terms(terms):
+def reduced_across(terms):
     count = math.prod(lax.axis_size(name) for name in ACROSS)
     tiles = terms.reshape(count, 1, -1)
-    share = lax.all_to_all(tiles, ACROSS, 0, 0, tiled=True).sum(axis=0)
+    return lax.all_to_all(tiles, ACROSS, 0, 0, tiled=True).sum(axis=0)
+
+
+def reduced_around(share):
     copies = jnp.broadcast_to(share, (lax.axis_size("ring"), *share.shape))
-    share = lax.all_to_all(copies, "ring", 0, 0, tiled=True).sum(axis=0)
+    return lax.all_to_all(copies, "ring", 0, 0, tiled=True).sum(axis=0)
+
+
+def gathered_across(share):
+    count = math.prod(lax.axis_size(name) for name in ACROSS)
     copies = jnp.broadcast_to(share, (count, *share.shape))
     return lax.all_to_all(copies, ACROSS, 0, 0, tiled=True).reshape(TERMS, CH)
 
@@ -268,6 +276,7 @@
     d2 = depth_two.reshape(27, CH)
     core = lax.axis_index("core")
     parity = core.astype(jnp.int32).reshape(1)
+
 
     def both(x):
         return jnp.concatenate(
@@ -292,7 +301,6 @@
         8_000_000_000,
         parity, block_in, block_up, near, d1, point_one, d2, point_two,
     )
-    inner_beside = with_other_core(inner)
     outer, terms = call(
         functools.partial(far_kernel, factor),
         [slots, slots, flipped, flipped, totals],
@@ -301,16 +309,20 @@
         parity, block_in, block_up, far, pre, carried, far_w1, far_w2,
         d1, point_one, d2, point_two, terms,
     )
+    share = reduced_across(terms)
+    share, inner, outer = lax.optimization_barrier((share, inner, outer))
     outer_beside = with_other_chip(outer)
-    (grad,) = call(
+    inner_beside = with_other_core(inner)
+    grad, done = call(
         last_kernel,
         [slots, taps_w],
-        [shape((2, CELLS, CH), bf16)],
+        [shape((2, CELLS, CH), bf16), shape((8, CH), f32)],
         4_000_000_000,
         parity, inner, outer, inner_beside, outer_beside, d1, point_one,
     )
+    sums = gathered_across(reduced_around(share))
     depth, point = (shape((3, 3, 3, CH), f32), shape((CH, CH), f32))
-    parts = call(parts_kernel, [], [depth, point, depth, point], 0, sum_of_terms(terms))
+    parts = call(parts_kernel, [], [depth, point, depth, point], 0, sums, done)
     return (grad.reshape(inputs.shape), *parts)
 
 

time: 67.2 us -> 68.2 us (1.015)
  starting transfers between devices: 13 us -> 13.9 us
    all_to_all x1, starting transfers between devices: 5.2 us -> 6.2 us  [gathered_across(): return lax.all_to_all(copies, ACROSS, 0, 0, tiled=True).reshape(TERMS, CH)]
where the time goes in v3:
time: 68.2 us; the launch traced here: 67.9 us
  blocking collectives  30.3 us (44%)
  Pallas kernels  15 us (22%)
  starting transfers between devices  13.9 us (20%)
  waiting for transfers between devices  5.57 us (8%)
  local copies, waits for them, and re-layouts  2.1 us (3%)
  between operations  0.81 us (1%)
    all_to_all x1, blocking collectives, reduced_across(): return lax.all_to_all(tiles, ACROSS, 0, 0, tiled=True).sum(axis=0)  17.7 us
    pallas_call x4, Pallas kernels, call(): pl.pallas_call(kernel, out_shape=outs, in_specs=[smem if a.dtype == jnp.i...  15 us
    all_to_all x1, blocking collectives, reduced_around(): return lax.all_to_all(copies, 'ring', 0, 0, tiled=True).sum(axis=0)  12.5 us
    all_to_all x1, starting transfers between devices, gathered_across(): return lax.all_to_all(copies, ACROSS, 0, 0, tiled=True).reshape(TERMS, CH)  6.2 us
    all_to_all x1, waiting for transfers between devices, gathered_across(): return lax.all_to_all(copies, ACROSS, 0, 0, tiled=True).reshape(TERMS, CH)  4.22 us
    ppermute x2, starting transfers between devices, with_other_chip(): return lax.ppermute(v, SPACE, pairs + [(j, i) for i, j in pairs])  3.96 us
    ppermute x2, starting transfers between devices, with_other_core(): return lax.ppermute(v, 'core', [(0, 1), (1, 0)])  3.72 us
  transfers between devices with their start and end apart: 5, of which 2 were waited for; matrix products, arithmetic and copies ran while one was open for 1% of the time, Pallas kernels for 16%

profile of v3, /device:TPU:1, one launch (start us, length us, event | category | flops | bytes accessed | tf_op | source)
XLA Modules:
  0.0 67.9 jit_solution(13523814856159414505)
XLA Ops:
  0.6 1.3 %constant_dynamic-slice_fusion = (bf16[1,1024,128]{2,1,0:T(8,128)(2,1)S(1)}, bf16[1,1024,128]{2,1,0:T(8,128)(2,1)S(1)}, bf16[1,1024,128]{2,1,0:T(8,128)(2,1)S(1)}, bf16[1,1024,128]{2,1,0:T(8,128)(2,1)S(1)}) fusion(bf16[2,1024,128]{2,1,0:T(8,128)(2,1)} %bitcast.10, s32[]{:T(128)S(6)} %select_n.9, s32[]{:T(128)S(6)} %select_n.8, bf16[2,1024,128]{2,1,0:T(8,128)(2,1)} %bitcast.7), kind=kLoop, calls=%fused_computation.2 | loop fusion | bytes 2097160 | tf_op jit(solution)/shard_map/dynamic_slice | solution.py:283
  1.9 0.0 copy-start.4
  1.9 0.0 copy-start.5
  1.9 0.0 copy-start.3
  1.9 0.1 pad_maximum_fusion.1
  2.0 3.3 %collective-permute-start.1 = (bf16[2,1024,128]{2,1,0:T(8,128)(2,1)S(1)}, bf16[2,1024,128]{2,1,0:T(8,128)(2,1)S(1)}, u32[]{:S(2)}, u32[]{:S(2)}) collective-permute-start(bf16[2,1024,128]{2,1,0:T(8,128)(2,1)S(1)} %pad_maximum_fusion.1), channel_id=1, source_target_pairs={{0,4},{4,0},{1,5},{5,1},{2,6},{6,2},{3,7},{7,3},{8,12},{12,8},{9,1... | collective-permute-start | bytes 1572872 | tf_op jit(solution)/shard_map/ppermute | solution.py:244
  5.3 0.0 copy-start
  5.3 0.0 copy-start.1
  5.3 0.1 pad_maximum_fusion
  5.4 0.0 copy-start.2
  5.4 2.1 %collective-permute-start = (bf16[2,1024,128]{2,1,0:T(8,128)(2,1)S(1)}, bf16[2,1024,128]{2,1,0:T(8,128)(2,1)S(1)}, u32[]{:S(2)}, u32[]{:S(2)}) collective-permute-start(bf16[2,1024,128]{2,1,0:T(8,128)(2,1)S(1)} %pad_maximum_fusion), channel_id=1, source_target_pairs={{4,8},{12,16},{20,24},{28,32},{36,40},{44,48},{52,56},{60,64},{68,... | collective-permute-start | bytes 1572872 | tf_op jit(solution)/shard_map/ppermute | solution.py:250
  7.5 0.0 copy-done.4
  7.5 0.0 copy-done.5
  7.5 0.0 collective-permute-done.1.near
  7.5 0.0 copy-done.3
  7.5 0.0 copy-done
  7.5 0.0 copy-done.1
  7.6 0.0 copy-done.2
  7.6 7.1 %shard_map.101 = (bf16[1024,128]{1,0:T(8,128)(2,1)S(1)}, f32[1024,128]{1,0:T(8,128)S(1)}, f32[1024,128]{1,0:T(8,128)S(1)}, bf16[384,384]{1,0:T(8,128)(2,1)S(1)},...) custom-call(s32[1]{0:T(128)} %bitcast.parity, bf16[2,1024,128]{2,1,0:T(8,128)(2,1)S(1)} %bitcast.8, ...), custom_call_target="tpu_custom_call" | custom-call | flops 8000000000 | bytes 3716612 | tf_op jit(solution)/shard_map/pallas_call | solution.py:228
  14.7 1.3 %collective-permute-done.far = bf16[2,1024,128]{2,1,0:T(8,128)(2,1)S(1)} collective-permute-done((bf16[2,1024,128]{2,1,0:T(8,128)(2,1)S(1)}, bf16[2,1024,128]{2,1,0:T(8,128)(2,1)S(1)}, u32[]{:S(2)}, u32[]{:S(2)}) %collective-permute-start) | collective-permute-done | bytes 524320 | tf_op jit(solution)/shard_map/ppermute | solution.py:250
  16.0 3.6 %shard_map.102 = (bf16[1024,128]{1,0:T(8,128)(2,1)S(1)}, f32[320,128]{1,0:T(8,128)S(1)}) custom-call(s32[1]{0:T(128)} %bitcast.parity, bf16[2,1024,128]{2,1,0:T(8,128)(2,1)S(1)} %bitcast.9, bf16[2,1024,128]{2,1,0:T(8,128)(2,1)S(1)} %bitcast.12, bf16[2,1024,128]{2,1,0:T(8,128)(2,1)S(1)} %collective-permute-done.far, f32[1024,128]{1,0:T(8,128)S(1)} %get-tuple-element.22.pre, ...), custom_call_target="tpu_custom_call" | custom-call | flops 4000000000 | bytes 3880452 | tf_op jit(solution)/shard_map/pallas_call | solution.py:228
  19.6 17.7 %all_to_all.15 = f32[32,1,1280]{2,1,0:T(1,128)S(1)} all-to-all(f32[32,1,1280]{2,1,0:T(1,128)S(1)} %bitcast.13), channel_id=1, replica_groups=mesh['outer'=4,'ring'=8,'core'=2,'dp'=4] {'outer','core','dp'}, dimensions={0} | all-to-all | bytes 327680 | tf_op jit(solution)/shard_map/all_to_all | solution.py:256
  37.3 0.1 reduce_sum.20
  37.4 0.4 collective-permute-start.2
  37.8 1.9 %collective-permute-start.3 = (bf16[1024,128]{1,0:T(8,128)(2,1)S(1)}, bf16[1024,128]{1,0:T(8,128)(2,1)S(1)}, u32[]{:S(2)}, u32[]{:S(2)}) collective-permute-start(bf16[1024,128]{1,0:T(8,128)(2,1)S(1)} %get-tuple-element.31.outer), channel_id=1, source_target_pairs={{4,8},{12,16},{20,24},{28,32},{36,40},{44,48},{52,56},{60,64},{68,... | collective-permute-start | bytes 786440 | tf_op jit(solution)/shard_map/ppermute | solution.py:250
  39.8 12.5 %all_to_all.16 = f32[8,1,1280]{2,1,0:T(1,128)S(1)} all-to-all(f32[8,1,1280]{2,1,0:T(1,128)S(1)} %broadcast_in_dim.6), channel_id=1, replica_groups=mesh['outer'=4,'ring'=8,'core'=2,'dp'=4] {'ring'}, dimensions={0} | all-to-all | bytes 81920 | tf_op jit(solution)/shard_map/all_to_all | solution.py:261
  52.4 0.7 %broadcast_in_dim.7 = f32[32,1,1280]{2,1,0:T(1,128)} broadcast(f32[1280]{0:T(1024)S(1)} %reduce_sum.22), dimensions={2} | broadcast | bytes 168960 | tf_op jit(solution)/shard_map/broadcast_in_dim | solution.py:266
  53.1 6.2 %all-to-all-start.2 = ((f32[32,1,1280]{2,1,0:T(1,128)}), f32[32,1,1280]{2,1,0:T(1,128)S(1)}, u32[]{:S(2)}, u32[]{:S(2)}) async-start(f32[32,1,1280]{2,1,0:T(1,128)} %broadcast_in_dim.7), calls=%async_computation.2 | async-start | bytes 327680 | tf_op jit(solution)/shard_map/all_to_all | solution.py:267
  59.3 0.0 collective-permute-done.2.near
  59.3 0.0 collective-permute-done.3.far
  59.3 3.7 %shard_map.103 = (bf16[2,1024,128]{2,1,0:T(8,128)(2,1)}, f32[8,128]{1,0:T(8,128)S(1)}) custom-call(s32[1]{0:T(128)} %bitcast.parity, bf16[1024,128]{1,0:T(8,128)(2,1)S(1)} %get-tuple-element.30.inner, bf16[1024,128]{1,0:T(8,128)(2,1)S(1)} %get-tuple-element.31.outer, bf16[1024,128]{1,0:T(8,128)(2,1)S(1)} %collective-permute-done.2.near, ...), custom_call_target="tpu_custom_call" | custom-call | flops 4000000000 | bytes 1616644 | tf_op jit(solution)/shard_map/pallas_call | solution.py:228
  63.0 4.2 %all-to-all-done.2 = f32[32,1,1280]{2,1,0:T(1,128)S(1)} async-done(((f32[32,1,1280]{2,1,0:T(1,128)}), f32[32,1,1280]{2,1,0:T(1,128)S(1)}, u32[]{:S(2)}, u32[]{:S(2)}) %all-to-all-start.2) | async-done | bytes 163872 | tf_op jit(solution)/shard_map/all_to_all | solution.py:267
  67.2 0.7 shard_map.104
  (6 shorter events, 0.1 us)
Async XLA Ops:
  1.9 5.6 %copy-start.4 = (bf16[3,3,3,128]{3,2,1,0:T(4,128)(2,1)S(1)}, bf16[3,3,3,128]{3,2,1,0:T(4,128)(2,1)}, u32[]{:S(2)}) copy-start(bf16[3,3,3,128]{3,2,1,0:T(4,128)(2,1)} %param.7) | copy-start | bytes 20740
  1.9 5.6 %copy-start.5 = (bf16[3,3,3,128]{3,2,1,0:T(4,128)(2,1)S(1)}, bf16[3,3,3,128]{3,2,1,0:T(4,128)(2,1)}, u32[]{:S(2)}) copy-start(bf16[3,3,3,128]{3,2,1,0:T(4,128)(2,1)} %param.9) | copy-start | bytes 20740
  1.9 5.6 %copy-start.3 = (bf16[128,128]{1,0:T(8,128)(2,1)S(1)}, bf16[128,128]{1,0:T(8,128)(2,1)}, u32[]{:S(2)}) copy-start(bf16[128,128]{1,0:T(8,128)(2,1)} %p1.5) | copy-start | bytes 98308
  2.0 5.5 %collective-permute-start.1 = (bf16[2,1024,128]{2,1,0:T(8,128)(2,1)S(1)}, bf16[2,1024,128]{2,1,0:T(8,128)(2,1)S(1)}, u32[]{:S(2)}, u32[]{:S(2)}) collective-permute-start(bf16[2,1024,128]{2,1,0:T(8,128)(2,1)S(1)} %pad_maximum_fusion.1), channel_id=1, source_target_pairs={{0,4},{4,0},{1,5},{5,1},{2,6},{6,2},{3,7},{7,3},{8,12},{12,8},{9,1... | collective-permute-start | bytes 1572872 | tf_op jit(solution)/shard_map/ppermute | solution.py:244
  5.3 2.2 %copy-start = (bf16[1,1,2,16,64,128]{5,4,3,2,1,0:T(8,128)(2,1)S(1)}, bf16[1,1,2,16,64,128]{5,4,3,2,1,0:T(8,128)(2,1)}, u32[]{:S(2)}) copy-start(bf16[1,1,2,16,64,128]{5,4,3,2,1,0:T(8,128)(2,1)} %param.6) | copy-start | bytes 1572868
  5.3 2.2 %copy-start.1 = (bf16[1,1,2,16,64,128]{5,4,3,2,1,0:T(8,128)(2,1)S(1)}, bf16[1,1,2,16,64,128]{5,4,3,2,1,0:T(8,128)(2,1)}, u32[]{:S(2)}) copy-start(bf16[1,1,2,16,64,128]{5,4,3,2,1,0:T(8,128)(2,1)} %param.11) | copy-start | bytes 1572868
  5.4 2.2 %copy-start.2 = (bf16[128,128]{1,0:T(8,128)(2,1)S(1)}, bf16[128,128]{1,0:T(8,128)(2,1)}, u32[]{:S(2)}) copy-start(bf16[128,128]{1,0:T(8,128)(2,1)} %p2.3) | copy-start | bytes 98308
  5.4 10.6 %collective-permute-start = (bf16[2,1024,128]{2,1,0:T(8,128)(2,1)S(1)}, bf16[2,1024,128]{2,1,0:T(8,128)(2,1)S(1)}, u32[]{:S(2)}, u32[]{:S(2)}) collective-permute-start(bf16[2,1024,128]{2,1,0:T(8,128)(2,1)S(1)} %pad_maximum_fusion), channel_id=1, source_target_pairs={{4,8},{12,16},{20,24},{28,32},{36,40},{44,48},{52,56},{60,64},{68,... | collective-permute-start | bytes 1572872 | tf_op jit(solution)/shard_map/ppermute | solution.py:250
  37.4 21.9 %collective-permute-start.2 = (bf16[1024,128]{1,0:T(8,128)(2,1)S(1)}, bf16[1024,128]{1,0:T(8,128)(2,1)S(1)}, u32[]{:S(2)}, u32[]{:S(2)}) collective-permute-start(bf16[1024,128]{1,0:T(8,128)(2,1)S(1)} %get-tuple-element.30.inner), channel_id=1, source_target_pairs={{0,4},{4,0},{1,5},{5,1},{2,6},{6,2},{3,7},{7,3},{8,12},{12,8},{9,1... | collective-permute-start | bytes 786440 | tf_op jit(solution)/shard_map/ppermute | solution.py:244
  37.8 21.5 %collective-permute-start.3 = (bf16[1024,128]{1,0:T(8,128)(2,1)S(1)}, bf16[1024,128]{1,0:T(8,128)(2,1)S(1)}, u32[]{:S(2)}, u32[]{:S(2)}) collective-permute-start(bf16[1024,128]{1,0:T(8,128)(2,1)S(1)} %get-tuple-element.31.outer), channel_id=1, source_target_pairs={{4,8},{12,16},{20,24},{28,32},{36,40},{44,48},{52,56},{60,64},{68,... | collective-permute-start | bytes 786440 | tf_op jit(solution)/shard_map/ppermute | solution.py:250
  53.1 14.1 %all-to-all-start.2 = ((f32[32,1,1280]{2,1,0:T(1,128)}), f32[32,1,1280]{2,1,0:T(1,128)S(1)}, u32[]{:S(2)}, u32[]{:S(2)}) async-start(f32[32,1,1280]{2,1,0:T(1,128)} %broadcast_in_dim.7), calls=%async_computation.2 | async-start | bytes 327680 | tf_op jit(solution)/shard_map/all_to_all | solution.py:267

commit v4 on v3

--- a/solution.py
+++ b/solution.py
@@ -48,27 +48,64 @@
     ref[slot, LINE + CELLS : PADDED, :] = edge
 
 
-def windows(ref, slot, count, start):
-    return jnp.concatenate(
+def local_products(planes, weights, start):
+    left = jnp.concatenate(
         [
-            ref[slot + a, start + b * LINE : start + b * LINE + ROWS, :]
-            for a in range(count)
+            planes[1 + p, start + b * LINE : start + b * LINE + ROWS, :]
+            for p in range(2)
             for b in range(3)
         ],
         axis=1,
     )
-
-
-def fill_taps(ref, tap_matrix):
+    return shift_sum(mm(left, weights[...]), 2 * CH)
+
+
+def side_products(planes, slot, weights, start):
+    pairs = ROWS // LINE
+    left = jnp.concatenate(
+        [
+            jnp.concatenate(
+                [
+                    planes[slot, start + (2 * j + i) * LINE : start + (2 * j + i + 1) * LINE, :]
+                    for j in range(pairs)
+                ],
+                axis=0,
+            )
+            for i in range(4)
+        ],
+        axis=1,
+    )
+    out = shift_sum(mm(left, weights[...]), 2 * CH)
+    return jnp.concatenate(
+        [
+            out[j * LINE : (j + 1) * LINE, q * CH : (q + 1) * CH]
+            for j in range(pairs)
+            for q in range(2)
+        ],
+        axis=0,
+    )
+
+
+def fill_local(ref, tap_matrix):
     for a in range(3):
         for b in range(3):
             for e in range(3):
-                row, col = ((3 * a + b) * CH, e * CH)
-                ref[row : row + CH, col : col + CH] = tap_matrix(9 * a + 3 * b + e)
-
-
-def tap_rows(ref, a, count):
-    return ref[pl.ds(pl.multiple_of(a * 3 * CH, CH), count * 3 * CH), :]
+                block = tap_matrix(9 * a + 3 * b + e)
+                for p in range(2):
+                    x = p + 1 - a
+                    if 0 <= x < 2:
+                        row, col = ((3 * p + b) * CH, (2 * e + x) * CH)
+                        ref[row : row + CH, col : col + CH] = block
+
+
+def fill_side(ref, tap_matrix, high):
+    ref[...] = jnp.zeros(ref.shape, jnp.bfloat16)
+    for b in range(3):
+        for e in range(3):
+            block = jnp.where(high, tap_matrix(18 + 3 * b + e), tap_matrix(3 * b + e))
+            for q in range(2):
+                row, col = ((b + q) * CH, (2 * e + q) * CH)
+                ref[row : row + CH, col : col + CH] = block
 
 
 def columns_of(depth):
@@ -146,7 +183,7 @@
     factor,
     parity, block_in, block_up, near, d1, p1, d2, p2,
     scaled_out, pre, carried, far_w1, far_w2, terms,
-    planes_in, planes_up, w_one, w_two, scaled_t, hidden_t, total,
+    planes_in, planes_up, local_one, local_two, side_one, side_two, scaled_t, hidden_t, total,
 ):
     core = parity[0]
     inner = 1 - core
@@ -154,23 +191,34 @@
     depth_one, point_one, depth_two, point_two = weights
     place_planes(planes_in, block_in, core, near[0], None)
     place_planes(planes_up, block_up, core, near[1], None)
-    fill_taps(w_one, forward_taps(columns_of(depth_one), point_one))
-    fill_taps(w_two, backward_taps(depth_two, point_two.T))
-    for start in range(0, CELLS, ROWS):
-        value = shift_sum(mm(windows(planes_in, inner, 3, start), w_one[...]), CH)
-        back = shift_sum(mm(windows(planes_up, inner, 3, start), w_two[...]), CH)
-        activate(value, back, scaled_out, scaled_t, hidden_t, start)
+    near_high = core == 0
+    taps_one = forward_taps(columns_of(depth_one), point_one)
+    taps_two = backward_taps(depth_two, point_two.T)
+    for taps, local, side, other in (
+        (taps_one, local_one, side_one, far_w1),
+        (taps_two, local_two, side_two, far_w2),
+    ):
+        fill_local(local, taps)
+        fill_side(side, taps, near_high)
+        fill_side(other, taps, jnp.logical_not(near_high))
+    near_slot = 3 - 3 * core
+    for half in range(0, CELLS, 2 * ROWS):
+        side_in = side_products(planes_in, near_slot, side_one, half)
+        side_up = side_products(planes_up, near_slot, side_two, half)
+        for at in range(0, 2 * ROWS, ROWS):
+            start = half + at
+            both_in = local_products(planes_in, local_one, start)
+            both_up = local_products(planes_up, local_two, start)
+            low, high = (both_in[:, :CH], both_in[:, CH:])
+            pre[start : start + ROWS, :] = jnp.where(near_high, low, high)
+            value = jnp.where(near_high, high, low) + side_in[at : at + ROWS, :]
+            low, high = (both_up[:, :CH], both_up[:, CH:])
+            carried[start : start + ROWS, :] = jnp.where(near_high, low, high)
+            back = jnp.where(near_high, high, low) + side_up[at : at + ROWS, :]
+            activate(value, back, scaled_out, scaled_t, hidden_t, start)
     weight_terms(
         factor, inner, planes_in, planes_up, scaled_t, hidden_t, weights, total, None, terms
     )
-    for planes, w, out, far_w in (
-        (planes_in, w_one, pre, far_w1),
-        (planes_up, w_two, carried, far_w2),
-    ):
-        far_w[...] = tap_rows(w, 2 * core, 1)
-        for start in range(0, CELLS, ROWS):
-            products = mm(windows(planes, 1, 2, start), tap_rows(w, 1 - core, 2))
-            out[start : start + ROWS, :] = shift_sum(products, CH)
 
 
 def far_kernel(
@@ -183,29 +231,40 @@
     weights = tuple(w[...].astype(jnp.float32) for w in (d1, p1, d2, p2))
     place_planes(planes_in, block_in, core, None, far[0])
     place_planes(planes_up, block_up, core, None, far[1])
-    for start in range(0, CELLS, ROWS):
-        value = shift_sum(mm(windows(planes_in, 3 * core, 1, start), far_w1[...]), CH)
-        back = shift_sum(mm(windows(planes_up, 3 * core, 1, start), far_w2[...]), CH)
-        value = value + pre[start : start + ROWS, :]
-        back = back + carried[start : start + ROWS, :]
-        activate(value, back, scaled_out, scaled_t, hidden_t, start)
+    for half in range(0, CELLS, 2 * ROWS):
+        side_in = side_products(planes_in, 3 * core, far_w1, half)
+        side_up = side_products(planes_up, 3 * core, far_w2, half)
+        for at in range(0, 2 * ROWS, ROWS):
+            start = half + at
+            value = side_in[at : at + ROWS, :] + pre[start : start + ROWS, :]
+            back = side_up[at : at + ROWS, :] + carried[start : start + ROWS, :]
+            activate(value, back, scaled_out, scaled_t, hidden_t, start)
     weight_terms(
         factor, core, planes_in, planes_up, scaled_t, hidden_t, weights, total, before, terms
     )
 
 
-def last_kernel(parity, inner, outer, near, far, d1, p1, out, done, planes, w):
+def last_kernel(parity, inner, outer, near, far, d1, p1, out, done, planes, local, low_side, high_side):
     core = parity[0]
     depth_one = d1[...].astype(jnp.float32)
-    fill_taps(w, backward_taps(depth_one, p1[...].astype(jnp.float32).T))
+    taps = backward_taps(depth_one, p1[...].astype(jnp.float32).T)
+    fill_local(local, taps)
+    fill_side(low_side, taps, False)
+    fill_side(high_side, taps, True)
     set_plane(planes, 2 - core, inner[...])
     set_plane(planes, 1 + core, outer[...])
     set_plane(planes, 3 - 3 * core, near[...])
     set_plane(planes, 3 * core, far[...])
-    for x in range(2):
-        for start in range(0, CELLS, ROWS):
-            grad = shift_sum(mm(windows(planes, x, 3, start), w[...]), CH)
-            out[x, start : start + ROWS, :] = grad.astype(jnp.bfloat16)
+    for half in range(0, CELLS, 2 * ROWS):
+        low = side_products(planes, 0, low_side, half)
+        high = side_products(planes, 3, high_side, half)
+        for at in range(0, 2 * ROWS, ROWS):
+            start = half + at
+            both = local_products(planes, local, start)
+            grad = both[:, :CH] + low[at : at + ROWS, :]
+            out[0, start : start + ROWS, :] = grad.astype(jnp.bfloat16)
+            grad = both[:, CH:] + high[at : at + ROWS, :]
+            out[1, start : start + ROWS, :] = grad.astype(jnp.bfloat16)
     done[...] = jnp.zeros((8, CH), jnp.float32)
 
 
@@ -286,17 +345,18 @@
     far = with_other_chip(both(core))
     near = with_other_core(both(1 - core))
     slots = pltpu.VMEM((4, PADDED, CH), bf16)
-    taps_w = pltpu.VMEM((9 * CH, 3 * CH), bf16)
+    local_w = pltpu.VMEM((6 * CH, 6 * CH), bf16)
+    side_w = pltpu.VMEM((4 * CH, 6 * CH), bf16)
     flipped = pltpu.VMEM((3 * CH, CELLS), bf16)
     totals = pltpu.VMEM((3, CH, CH), f32)
     devices = math.prod(lax.axis_size(name) for name in ("dp", *SPACE))
     factor = 1.0 / math.sqrt(devices * 2 * CELLS)
     inner, pre, carried, far_w1, far_w2, terms = call(
         functools.partial(near_kernel, factor),
-        [slots, slots, taps_w, taps_w, flipped, flipped, totals],
+        [slots, slots, local_w, local_w, side_w, side_w, flipped, flipped, totals],
         [shape((CELLS, CH), bf16)]
         + [shape((CELLS, CH), f32)] * 2
-        + [shape((3 * CH, 3 * CH), bf16)] * 2
+        + [shape((4 * CH, 6 * CH), bf16)] * 2
         + [shape((TERMS, CH), f32)],
         8_000_000_000,
         parity, block_in, block_up, near, d1, point_one, d2, point_two,
@@ -310,12 +370,11 @@
         d1, point_one, d2, point_two, terms,
     )
     share = reduced_across(terms)
-    share, inner, outer = lax.optimization_barrier((share, inner, outer))
     outer_beside = with_other_chip(outer)
     inner_beside = with_other_core(inner)
     grad, done = call(
         last_kernel,
-        [slots, taps_w],
+        [slots, local_w, side_w, side_w],
         [shape((2, CELLS, CH), bf16), shape((8, CH), f32)],
         4_000_000_000,
         parity, inner, outer, inner_beside, outer_beside, d1, point_one,

time: 68.2 us -> 67.3 us (0.987)
  starting transfers between devices: 13.9 us -> 12.6 us
  waiting for transfers between devices: 5.57 us -> 6.43 us
  Pallas kernels: 15 us -> 14.2 us
    all_to_all x1, blocking collectives: 17.7 us -> 21.2 us  [reduced_across(): return lax.all_to_all(tiles, ACROSS, 0, 0, tiled=True).sum(axis=0)]
    all_to_all x1, blocking collectives: 12.5 us -> 9.33 us  [reduced_around(): return lax.all_to_all(copies, 'ring', 0, 0, tiled=True).sum(axis=0)]
    all_to_all x1, starting transfers between devices: 6.2 us -> 5.2 us  [gathered_across(): return lax.all_to_all(copies, ACROSS, 0, 0, tiled=True).reshape(TERMS, CH)]
    pallas_call x4, Pallas kernels: 15 us -> 14.2 us  [call(): pl.pallas_call(kernel, out_shape=outs, in_specs=[smem if a.dtype == jnp.i...]
  transfers between devices with their start and end apart: 5 -> 5, of which waited for: 2 -> 2; matrix products, arithmetic and copies ran while one was open for 1% -> 1% of each run, Pallas kernels for 16% -> 15%
where the time goes in v4:
time: 67.3 us; the launch traced here: 67 us
  blocking collectives  30.6 us (45%)
  Pallas kernels  14.2 us (21%)
  starting transfers between devices  12.6 us (19%)
  waiting for transfers between devices  6.43 us (10%)
  local copies, waits for them, and re-layouts  2.1 us (3%)
  between operations  0.8 us (1%)
    all_to_all x1, blocking collectives, reduced_across(): return lax.all_to_all(tiles, ACROSS, 0, 0, tiled=True).sum(axis=0)  21.2 us
    pallas_call x4, Pallas kernels, call(): pl.pallas_call(kernel, out_shape=outs, in_specs=[smem if a.dtype == jnp.i...  14.2 us
    all_to_all x1, blocking collectives, reduced_around(): return lax.all_to_all(copies, 'ring', 0, 0, tiled=True).sum(axis=0)  9.33 us
    all_to_all x1, starting transfers between devices, gathered_across(): return lax.all_to_all(copies, ACROSS, 0, 0, tiled=True).reshape(TERMS, CH)  5.2 us
    all_to_all x1, waiting for transfers between devices, gathered_across(): return lax.all_to_all(copies, ACROSS, 0, 0, tiled=True).reshape(TERMS, CH)  4.55 us
    ppermute x2, starting transfers between devices, with_other_chip(): return lax.ppermute(v, SPACE, pairs + [(j, i) for i, j in pairs])  3.97 us
    ppermute x2, starting transfers between devices, with_other_core(): return lax.ppermute(v, 'core', [(0, 1), (1, 0)])  3.42 us
    ppermute x2, waiting for transfers between devices, with_other_chip(): return lax.ppermute(v, SPACE, pairs + [(j, i) for i, j in pairs])  1.87 us
  transfers between devices with their start and end apart: 5, of which 2 were waited for; matrix products, arithmetic and copies ran while one was open for 1% of the time, Pallas kernels for 15%

profile of v4, /device:TPU:1, one launch (start us, length us, event | category | flops | bytes accessed | tf_op | source)
XLA Modules:
  0.0 67.0 jit_solution(7662063103800130647)
XLA Ops:
  0.6 1.3 %constant_dynamic-slice_fusion = (bf16[1,1024,128]{2,1,0:T(8,128)(2,1)S(1)}, bf16[1,1024,128]{2,1,0:T(8,128)(2,1)S(1)}, bf16[1,1024,128]{2,1,0:T(8,128)(2,1)S(1)}, bf16[1,1024,128]{2,1,0:T(8,128)(2,1)S(1)}) fusion(bf16[2,1024,128]{2,1,0:T(8,128)(2,1)} %bitcast.10, s32[]{:T(128)S(6)} %select_n.9, s32[]{:T(128)S(6)} %select_n.8, bf16[2,1024,128]{2,1,0:T(8,128)(2,1)} %bitcast.7), kind=kLoop, calls=%fused_computation.2 | loop fusion | bytes 2097160 | tf_op jit(solution)/shard_map/dynamic_slice | solution.py:342
  1.9 0.0 copy-start.4
  1.9 0.0 copy-start.5
  1.9 0.0 copy-start.3
  1.9 0.1 pad_maximum_fusion
  2.0 3.3 %collective-permute-start = (bf16[2,1024,128]{2,1,0:T(8,128)(2,1)S(1)}, bf16[2,1024,128]{2,1,0:T(8,128)(2,1)S(1)}, u32[]{:S(2)}, u32[]{:S(2)}) collective-permute-start(bf16[2,1024,128]{2,1,0:T(8,128)(2,1)S(1)} %pad_maximum_fusion), channel_id=1, source_target_pairs={{0,4},{4,0},{1,5},{5,1},{2,6},{6,2},{3,7},{7,3},{8,12},{12,8},{9,1... | collective-permute-start | bytes 1572872 | tf_op jit(solution)/shard_map/ppermute | solution.py:303
  5.3 0.0 copy-start
  5.3 0.0 copy-start.1
  5.3 0.1 pad_maximum_fusion.1
  5.4 0.0 copy-start.2
  5.4 2.1 %collective-permute-start.1 = (bf16[2,1024,128]{2,1,0:T(8,128)(2,1)S(1)}, bf16[2,1024,128]{2,1,0:T(8,128)(2,1)S(1)}, u32[]{:S(2)}, u32[]{:S(2)}) collective-permute-start(bf16[2,1024,128]{2,1,0:T(8,128)(2,1)S(1)} %pad_maximum_fusion.1), channel_id=1, source_target_pairs={{4,8},{12,16},{20,24},{28,32},{36,40},{44,48},{52,56},{60,64},{68,... | collective-permute-start | bytes 1572872 | tf_op jit(solution)/shard_map/ppermute | solution.py:309
  7.5 0.0 copy-done.4
  7.5 0.0 copy-done.5
  7.5 0.0 collective-permute-done.near
  7.5 0.0 copy-done.3
  7.5 0.0 copy-done
  7.5 0.0 copy-done.1
  7.6 0.0 copy-done.2
  7.6 6.6 %shard_map.101 = (bf16[1024,128]{1,0:T(8,128)(2,1)S(1)}, f32[1024,128]{1,0:T(8,128)S(1)}, f32[1024,128]{1,0:T(8,128)S(1)}, bf16[512,768]{1,0:T(8,128)(2,1)S(1)},...) custom-call(s32[1]{0:T(128)} %bitcast.parity, bf16[2,1024,128]{2,1,0:T(8,128)(2,1)S(1)} %bitcast.8, ...), custom_call_target="tpu_custom_call" | custom-call | flops 8000000000 | bytes 4699652 | tf_op jit(solution)/shard_map/pallas_call | solution.py:287
  14.2 1.9 %collective-permute-done.1.far = bf16[2,1024,128]{2,1,0:T(8,128)(2,1)S(1)} collective-permute-done((bf16[2,1024,128]{2,1,0:T(8,128)(2,1)S(1)}, bf16[2,1024,128]{2,1,0:T(8,128)(2,1)S(1)}, u32[]{:S(2)}, u32[]{:S(2)}) %collective-permute-start.1) | collective-permute-done | bytes 524320 | tf_op jit(solution)/shard_map/ppermute | solution.py:309
  16.0 3.6 %shard_map.102 = (bf16[1024,128]{1,0:T(8,128)(2,1)S(1)}, f32[320,128]{1,0:T(8,128)S(1)}) custom-call(s32[1]{0:T(128)} %bitcast.parity, bf16[2,1024,128]{2,1,0:T(8,128)(2,1)S(1)} %bitcast.9, bf16[2,1024,128]{2,1,0:T(8,128)(2,1)S(1)} %bitcast.12, bf16[2,1024,128]{2,1,0:T(8,128)(2,1)S(1)} %collective-permute-done.1.far, f32[1024,128]{1,0:T(8,128)S(1)} %get-tuple-element.20.pre, ...), custom_call_target="tpu_custom_call" | custom-call | flops 4000000000 | bytes 4863492 | tf_op jit(solution)/shard_map/pallas_call | solution.py:287
  19.6 1.9 %collective-permute-start.3 = (bf16[1024,128]{1,0:T(8,128)(2,1)S(1)}, bf16[1024,128]{1,0:T(8,128)(2,1)S(1)}, u32[]{:S(2)}, u32[]{:S(2)}) collective-permute-start(bf16[1024,128]{1,0:T(8,128)(2,1)S(1)} %get-tuple-element.25.outer), channel_id=1, source_target_pairs={{4,8},{12,16},{20,24},{28,32},{36,40},{44,48},{52,56},{60,64},{68,... | collective-permute-start | bytes 786440 | tf_op jit(solution)/shard_map/ppermute | solution.py:309
  21.6 0.1 collective-permute-start.2
  21.7 21.2 %all_to_all.15 = f32[32,1,1280]{2,1,0:T(1,128)S(1)} all-to-all(f32[32,1,1280]{2,1,0:T(1,128)S(1)} %bitcast.13), channel_id=1, replica_groups=mesh['outer'=4,'ring'=8,'core'=2,'dp'=4] {'outer','core','dp'}, dimensions={0} | all-to-all | bytes 327680 | tf_op jit(solution)/shard_map/all_to_all | solution.py:315
  42.9 0.1 reduce_sum.18
  43.0 9.3 %all_to_all.16 = f32[8,1,1280]{2,1,0:T(1,128)S(1)} all-to-all(f32[8,1,1280]{2,1,0:T(1,128)S(1)} %broadcast_in_dim.6), channel_id=1, replica_groups=mesh['outer'=4,'ring'=8,'core'=2,'dp'=4] {'ring'}, dimensions={0} | all-to-all | bytes 81920 | tf_op jit(solution)/shard_map/all_to_all | solution.py:320
  52.4 0.7 %broadcast_in_dim.7 = f32[32,1,1280]{2,1,0:T(1,128)} broadcast(f32[1280]{0:T(1024)S(1)} %reduce_sum.19), dimensions={2} | broadcast | bytes 168960 | tf_op jit(solution)/shard_map/broadcast_in_dim | solution.py:325
  53.2 5.2 %all-to-all-start.2 = ((f32[32,1,1280]{2,1,0:T(1,128)}), f32[32,1,1280]{2,1,0:T(1,128)S(1)}, u32[]{:S(2)}, u32[]{:S(2)}) async-start(f32[32,1,1280]{2,1,0:T(1,128)} %broadcast_in_dim.7), calls=%async_computation.2 | async-start | bytes 327680 | tf_op jit(solution)/shard_map/all_to_all | solution.py:326
  58.4 0.0 collective-permute-done.3.far
  58.4 0.0 collective-permute-done.2.near
  58.4 3.4 %shard_map.103 = (bf16[2,1024,128]{2,1,0:T(8,128)(2,1)}, f32[8,128]{1,0:T(8,128)S(1)}) custom-call(s32[1]{0:T(128)} %bitcast.parity, bf16[1024,128]{1,0:T(8,128)(2,1)S(1)} %get-tuple-element.19.inner, bf16[1024,128]{1,0:T(8,128)(2,1)S(1)} %get-tuple-element.25.outer, bf16[1024,128]{1,0:T(8,128)(2,1)S(1)} %collective-permute-done.2.near, ...), custom_call_target="tpu_custom_call" | custom-call | flops 4000000000 | bytes 1616644 | tf_op jit(solution)/shard_map/pallas_call | solution.py:287
  61.8 4.5 %all-to-all-done.2 = f32[32,1,1280]{2,1,0:T(1,128)S(1)} async-done(((f32[32,1,1280]{2,1,0:T(1,128)}), f32[32,1,1280]{2,1,0:T(1,128)S(1)}, u32[]{:S(2)}, u32[]{:S(2)}) %all-to-all-start.2) | async-done | bytes 163872 | tf_op jit(solution)/shard_map/all_to_all | solution.py:326
  66.3 0.7 %shard_map.104 = (f32[3,3,3,128]{3,2,1,0:T(4,128)}, f32[128,128]{1,0:T(8,128)}, f32[3,3,3,128]{3,2,1,0:T(4,128)}, f32[128,128]{1,0:T(8,128)}) custom-call(f32[320,128]{1,0:T(8,128)S(1)} %bitcast.6, f32[8,128]{1,0:T(8,128)S(1)} %get-tuple-element.28.done), custom_call_target="tpu_custom_call" | custom-call | bytes 326656 | tf_op jit(solution)/shard_map/pallas_call | solution.py:287
  (4 shorter events, 0.1 us)
Async XLA Ops:
  1.9 5.6 %copy-start.4 = (bf16[3,3,3,128]{3,2,1,0:T(4,128)(2,1)S(1)}, bf16[3,3,3,128]{3,2,1,0:T(4,128)(2,1)}, u32[]{:S(2)}) copy-start(bf16[3,3,3,128]{3,2,1,0:T(4,128)(2,1)} %param.7) | copy-start | bytes 20740
  1.9 5.6 %copy-start.5 = (bf16[3,3,3,128]{3,2,1,0:T(4,128)(2,1)S(1)}, bf16[3,3,3,128]{3,2,1,0:T(4,128)(2,1)}, u32[]{:S(2)}) copy-start(bf16[3,3,3,128]{3,2,1,0:T(4,128)(2,1)} %param.9) | copy-start | bytes 20740
  1.9 5.6 %copy-start.3 = (bf16[128,128]{1,0:T(8,128)(2,1)S(1)}, bf16[128,128]{1,0:T(8,128)(2,1)}, u32[]{:S(2)}) copy-start(bf16[128,128]{1,0:T(8,128)(2,1)} %p1.5) | copy-start | bytes 98308
  2.0 5.5 %collective-permute-start = (bf16[2,1024,128]{2,1,0:T(8,128)(2,1)S(1)}, bf16[2,1024,128]{2,1,0:T(8,128)(2,1)S(1)}, u32[]{:S(2)}, u32[]{:S(2)}) collective-permute-start(bf16[2,1024,128]{2,1,0:T(8,128)(2,1)S(1)} %pad_maximum_fusion), channel_id=1, source_target_pairs={{0,4},{4,0},{1,5},{5,1},{2,6},{6,2},{3,7},{7,3},{8,12},{12,8},{9,1... | collective-permute-start | bytes 1572872 | tf_op jit(solution)/shard_map/ppermute | solution.py:303
  5.3 2.2 %copy-start = (bf16[1,1,2,16,64,128]{5,4,3,2,1,0:T(8,128)(2,1)S(1)}, bf16[1,1,2,16,64,128]{5,4,3,2,1,0:T(8,128)(2,1)}, u32[]{:S(2)}) copy-start(bf16[1,1,2,16,64,128]{5,4,3,2,1,0:T(8,128)(2,1)} %param.6) | copy-start | bytes 1572868
  5.3 2.2 %copy-start.1 = (bf16[1,1,2,16,64,128]{5,4,3,2,1,0:T(8,128)(2,1)S(1)}, bf16[1,1,2,16,64,128]{5,4,3,2,1,0:T(8,128)(2,1)}, u32[]{:S(2)}) copy-start(bf16[1,1,2,16,64,128]{5,4,3,2,1,0:T(8,128)(2,1)} %param.11) | copy-start | bytes 1572868
  5.4 2.2 %copy-start.2 = (bf16[128,128]{1,0:T(8,128)(2,1)S(1)}, bf16[128,128]{1,0:T(8,128)(2,1)}, u32[]{:S(2)}) copy-start(bf16[128,128]{1,0:T(8,128)(2,1)} %p2.3) | copy-start | bytes 98308
  5.4 10.6 %collective-permute-start.1 = (bf16[2,1024,128]{2,1,0:T(8,128)(2,1)S(1)}, bf16[2,1024,128]{2,1,0:T(8,128)(2,1)S(1)}, u32[]{:S(2)}, u32[]{:S(2)}) collective-permute-start(bf16[2,1024,128]{2,1,0:T(8,128)(2,1)S(1)} %pad_maximum_fusion.1), channel_id=1, source_target_pairs={{4,8},{12,16},{20,24},{28,32},{36,40},{44,48},{52,56},{60,64},{68,... | collective-permute-start | bytes 1572872 | tf_op jit(solution)/shard_map/ppermute | solution.py:309
  19.6 38.7 %collective-permute-start.3 = (bf16[1024,128]{1,0:T(8,128)(2,1)S(1)}, bf16[1024,128]{1,0:T(8,128)(2,1)S(1)}, u32[]{:S(2)}, u32[]{:S(2)}) collective-permute-start(bf16[1024,128]{1,0:T(8,128)(2,1)S(1)} %get-tuple-element.25.outer), channel_id=1, source_target_pairs={{4,8},{12,16},{20,24},{28,32},{36,40},{44,48},{52,56},{60,64},{68,... | collective-permute-start | bytes 786440 | tf_op jit(solution)/shard_map/ppermute | solution.py:309
  21.6 36.8 %collective-permute-start.2 = (bf16[1024,128]{1,0:T(8,128)(2,1)S(1)}, bf16[1024,128]{1,0:T(8,128)(2,1)S(1)}, u32[]{:S(2)}, u32[]{:S(2)}) collective-permute-start(bf16[1024,128]{1,0:T(8,128)(2,1)S(1)} %get-tuple-element.19.inner), channel_id=1, source_target_pairs={{0,4},{4,0},{1,5},{5,1},{2,6},{6,2},{3,7},{7,3},{8,12},{12,8},{9,1... | collective-permute-start | bytes 786440 | tf_op jit(solution)/shard_map/ppermute | solution.py:303
  53.2 13.2 %all-to-all-start.2 = ((f32[32,1,1280]{2,1,0:T(1,128)}), f32[32,1,1280]{2,1,0:T(1,128)S(1)}, u32[]{:S(2)}, u32[]{:S(2)}) async-start(f32[32,1,1280]{2,1,0:T(1,128)} %broadcast_in_dim.7), calls=%async_computation.2 | async-start | bytes 327680 | tf_op jit(solution)/shard_map/all_to_all | solution.py:326

commit v5 on v4

--- a/solution.py
+++ b/solution.py
@@ -60,7 +60,7 @@
     return shift_sum(mm(left, weights[...]), 2 * CH)
 
 
-def side_products(planes, slot, weights, start):
+def side_products(planes, slots, weights, start):
     pairs = ROWS // LINE
     left = jnp.concatenate(
         [
@@ -71,6 +71,7 @@
                 ],
                 axis=0,
             )
+            for slot in slots
             for i in range(4)
         ],
         axis=1,
@@ -106,6 +107,17 @@
             for q in range(2):
                 row, col = ((b + q) * CH, (2 * e + q) * CH)
                 ref[row : row + CH, col : col + CH] = block
+
+
+def fill_lines(ref, tap_matrix):
+    ref[...] = jnp.zeros(ref.shape, jnp.bfloat16)
+    for a in range(3):
+        for b in range(3):
+            for e in range(3):
+                block = tap_matrix(9 * a + 3 * b + e)
+                for q in range(2):
+                    row, col = ((4 * a + b + q) * CH, (2 * e + q) * CH)
+                    ref[row : row + CH, col : col + CH] = block
 
 
 def columns_of(depth):
@@ -203,8 +215,8 @@
         fill_side(other, taps, jnp.logical_not(near_high))
     near_slot = 3 - 3 * core
     for half in range(0, CELLS, 2 * ROWS):
-        side_in = side_products(planes_in, near_slot, side_one, half)
-        side_up = side_products(planes_up, near_slot, side_two, half)
+        side_in = side_products(planes_in, (near_slot,), side_one, half)
+        side_up = side_products(planes_up, (near_slot,), side_two, half)
         for at in range(0, 2 * ROWS, ROWS):
             start = half + at
             both_in = local_products(planes_in, local_one, start)
@@ -232,8 +244,8 @@
     place_planes(planes_in, block_in, core, None, far[0])
     place_planes(planes_up, block_up, core, None, far[1])
     for half in range(0, CELLS, 2 * ROWS):
-        side_in = side_products(planes_in, 3 * core, far_w1, half)
-        side_up = side_products(planes_up, 3 * core, far_w2, half)
+        side_in = side_products(planes_in, (3 * core,), far_w1, half)
+        side_up = side_products(planes_up, (3 * core,), far_w2, half)
         for at in range(0, 2 * ROWS, ROWS):
             start = half + at
             value = side_in[at : at + ROWS, :] + pre[start : start + ROWS, :]
@@ -242,6 +254,30 @@
     weight_terms(
         factor, core, planes_in, planes_up, scaled_t, hidden_t, weights, total, before, terms
     )
+
+
+def beside_kernel(
+    place, block_in, block_up, far, beyond, d1, p1, d2, p2,
+    scaled_out,
+    planes_in, planes_up, w_one, w_two,
+):
+    core = place[0]
+    depth_one, point_one, depth_two, point_two = (
+        w[...].astype(jnp.float32) for w in (d1, p1, d2, p2)
+    )
+    for which, planes, block in ((0, planes_in, block_in), (1, planes_up, block_up)):
+        set_plane(planes, 2 * core, beyond[which])
+        set_plane(planes, 1, far[which])
+        set_plane(planes, 2 - 2 * core, block[core])
+    fill_lines(w_one, forward_taps(columns_of(depth_one), point_one))
+    fill_lines(w_two, backward_taps(depth_two, point_two.T))
+    inside = place[1] > 0
+    for half in range(0, CELLS, 2 * ROWS):
+        value = side_products(planes_in, (0, 1, 2), w_one, half)
+        back = side_products(planes_up, (0, 1, 2), w_two, half)
+        sigma = jax.nn.sigmoid(value)
+        scaled = back * (sigma * (1.0 + value * (1.0 - sigma)))
+        scaled_out[half : half + 2 * ROWS, :] = jnp.where(inside, scaled, 0.0).astype(jnp.bfloat16)
 
 
 def last_kernel(parity, inner, outer, near, far, d1, p1, out, done, planes, local, low_side, high_side):
@@ -256,8 +292,8 @@
     set_plane(planes, 3 - 3 * core, near[...])
     set_plane(planes, 3 * core, far[...])
     for half in range(0, CELLS, 2 * ROWS):
-        low = side_products(planes, 0, low_side, half)
-        high = side_products(planes, 3, high_side, half)
+        low = side_products(planes, (0,), low_side, half)
+        high = side_products(planes, (3,), high_side, half)
         for at in range(0, 2 * ROWS, ROWS):
             start = half + at
             both = local_products(planes, local, start)
@@ -309,10 +345,10 @@
     return lax.ppermute(v, SPACE, pairs + [(j, i) for i, j in pairs])
 
 
-def reduced_across(terms):
+def sent_across(terms):
     count = math.prod(lax.axis_size(name) for name in ACROSS)
     tiles = terms.reshape(count, 1, -1)
-    return lax.all_to_all(tiles, ACROSS, 0, 0, tiled=True).sum(axis=0)
+    return lax.all_to_all(tiles, ACROSS, 0, 0, tiled=True)
 
 
 def reduced_around(share):
@@ -334,7 +370,10 @@
     d1 = depth_one.reshape(27, CH)
     d2 = depth_two.reshape(27, CH)
     core = lax.axis_index("core")
-    parity = core.astype(jnp.int32).reshape(1)
+    count = math.prod(lax.axis_size(name) for name in SPACE)
+    index = lax.axis_index(SPACE)
+    inside = jnp.logical_and(index > 0, index < count - 1)
+    place = jnp.stack([core, inside]).astype(jnp.int32)
 
 
     def both(x):
@@ -342,8 +381,9 @@
             [lax.dynamic_slice_in_dim(block, x, 1, 0) for block in (block_in, block_up)], axis=0
         )
 
+    beside = both(1 - core)
     far = with_other_chip(both(core))
-    near = with_other_core(both(1 - core))
+    near = with_other_core(beside)
     slots = pltpu.VMEM((4, PADDED, CH), bf16)
     local_w = pltpu.VMEM((6 * CH, 6 * CH), bf16)
     side_w = pltpu.VMEM((4 * CH, 6 * CH), bf16)
@@ -359,25 +399,34 @@
         + [shape((4 * CH, 6 * CH), bf16)] * 2
         + [shape((TERMS, CH), f32)],
         8_000_000_000,
-        parity, block_in, block_up, near, d1, point_one, d2, point_two,
-    )
+        place, block_in, block_up, near, d1, point_one, d2, point_two,
+    )
+    beside, inner = lax.optimization_barrier((beside, inner))
+    beyond = with_other_chip(beside)
+    inner_beside = with_other_core(inner)
     outer, terms = call(
         functools.partial(far_kernel, factor),
         [slots, slots, flipped, flipped, totals],
         [shape((CELLS, CH), bf16), shape((TERMS, CH), f32)],
         4_000_000_000,
-        parity, block_in, block_up, far, pre, carried, far_w1, far_w2,
+        place, block_in, block_up, far, pre, carried, far_w1, far_w2,
         d1, point_one, d2, point_two, terms,
     )
-    share = reduced_across(terms)
-    outer_beside = with_other_chip(outer)
-    inner_beside = with_other_core(inner)
+    share = sent_across(terms).sum(axis=0)
+    lines_w = pltpu.VMEM((12 * CH, 6 * CH), bf16)
+    (outer_beside,) = call(
+        beside_kernel,
+        [slots, slots, lines_w, lines_w],
+        [shape((CELLS, CH), bf16)],
+        6_000_000_000,
+        place, block_in, block_up, far, beyond, d1, point_one, d2, point_two,
+    )
     grad, done = call(
         last_kernel,
         [slots, local_w, side_w, side_w],
         [shape((2, CELLS, CH), bf16), shape((8, CH), f32)],
         4_000_000_000,
-        parity, inner, outer, inner_beside, outer_beside, d1, point_one,
+        place, inner, outer, inner_beside, outer_beside, d1, point_one,
     )
     sums = gathered_across(reduced_around(share))
     depth, point = (shape((3, 3, 3, CH), f32), shape((CH, CH), f32))

time: 67.3 us -> 69.3 us (1.030)
  blocking collectives: 30.6 us -> 17.3 us
  starting transfers between devices: 12.6 us -> 20 us
  Pallas kernels: 14.2 us -> 19.6 us
  local copies, waits for them, and re-layouts: 2.1 us -> 3.32 us
  other arithmetic: 0.25 us -> 1.12 us
    all_to_all x2 -> x1, blocking collectives: 30.6 us -> 17.3 us  [sent_across(): return lax.all_to_all(tiles, ACROSS, 0, 0, tiled=True)]
    all_to_all x0 -> x1, waiting for transfers between devices: none -> 6.54 us  [reduced_around(): return lax.all_to_all(copies, 'ring', 0, 0, tiled=True).sum(axis=0)]
    pallas_call x4 -> x5, Pallas kernels: 14.2 us -> 19.6 us  [call(): pl.pallas_call(kernel, out_shape=outs, in_specs=[smem if a.dtype == jnp.i...]
    all_to_all x0 -> x1, starting transfers between devices: none -> 5.16 us  [reduced_around(): return lax.all_to_all(copies, 'ring', 0, 0, tiled=True).sum(axis=0)]
    all_to_all x1, waiting for transfers between devices: 4.55 us -> 0.24 us  [gathered_across(): return lax.all_to_all(copies, ACROSS, 0, 0, tiled=True).reshape(TERMS, CH)]
    ppermute x2, waiting for transfers between devices: 1.87 us -> 0.01 us  [with_other_chip(): return lax.ppermute(v, SPACE, pairs + [(j, i) for i, j in pairs])]
    ppermute x2, starting transfers between devices: 3.97 us -> 5.68 us  [with_other_chip(): return lax.ppermute(v, SPACE, pairs + [(j, i) for i, j in pairs])]
    concatenate x2, other arithmetic: 0.1 us -> 0.89 us  [both(): jnp.concatenate([lax.dynamic_slice_in_dim(block, x, 1, 0) for block in (b...]
  transfers between devices with their start and end apart: 5 -> 6, of which waited for: 2 -> 2; matrix products, arithmetic and copies ran while one was open for 1% -> 2% of each run, Pallas kernels for 15% -> 27%
where the time goes in v5:
time: 69.3 us; the launch traced here: 68.9 us
  starting transfers between devices  20 us (29%)
  Pallas kernels  19.6 us (28%)
  blocking collectives  17.3 us (25%)
  waiting for transfers between devices  6.78 us (10%)
  local copies, waits for them, and re-layouts  3.32 us (5%)
  other arithmetic  1.12 us (2%)
  between operations  0.79 us (1%)
    pallas_call x5, Pallas kernels, call(): pl.pallas_call(kernel, out_shape=outs, in_specs=[smem if a.dtype == jnp.i...  19.6 us
    all_to_all x1, blocking collectives, sent_across(): return lax.all_to_all(tiles, ACROSS, 0, 0, tiled=True)  17.3 us
    all_to_all x1, waiting for transfers between devices, reduced_around(): return lax.all_to_all(copies, 'ring', 0, 0, tiled=True).sum(axis=0)  6.54 us
    ppermute x2, starting transfers between devices, with_other_chip(): return lax.ppermute(v, SPACE, pairs + [(j, i) for i, j in pairs])  5.68 us
    all_to_all x1, starting transfers between devices, gathered_across(): return lax.all_to_all(copies, ACROSS, 0, 0, tiled=True).reshape(TERMS, CH)  5.48 us
    all_to_all x1, starting transfers between devices, reduced_around(): return lax.all_to_all(copies, 'ring', 0, 0, tiled=True).sum(axis=0)  5.16 us
    ppermute x2, starting transfers between devices, with_other_core(): return lax.ppermute(v, 'core', [(0, 1), (1, 0)])  3.67 us
  transfers between devices with their start and end apart: 6, of which 2 were waited for; matrix products, arithmetic and copies ran while one was open for 2% of the time, Pallas kernels for 27%

profile of v5, /device:TPU:1, one launch (start us, length us, event | category | flops | bytes accessed | tf_op | source)
XLA Modules:
  0.0 68.9 jit_solution(740519405655676094)
XLA Ops:
  0.6 1.3 %constant_dynamic-slice_fusion = (bf16[1,1024,128]{2,1,0:T(8,128)(2,1)S(1)}, bf16[1,1024,128]{2,1,0:T(8,128)(2,1)S(1)}, bf16[1,1024,128]{2,1,0:T(8,128)(2,1)S(1)}, bf16[1,1024,128]{2,1,0:T(8,128)(2,1)S(1)}) fusion(bf16[2,1024,128]{2,1,0:T(8,128)(2,1)} %bitcast.12, s32[]{:T(128)S(6)} %select_n.9, s32[]{:T(128)S(6)} %select_n.8, bf16[2,1024,128]{2,1,0:T(8,128)(2,1)} %bitcast.8), kind=kLoop, calls=%fused_computation.2 | loop fusion | bytes 2097160 | tf_op jit(solution)/shard_map/dynamic_slice | solution.py:381
  1.9 0.0 copy-start.4
  1.9 0.0 copy-start.5
  1.9 0.8 %pad_maximum_fusion = bf16[2,1024,128]{2,1,0:T(8,128)(2,1)} fusion(bf16[1,1024,128]{2,1,0:T(8,128)(2,1)S(1)} %get-tuple-element.40, bf16[1,1024,128]{2,1,0:T(8,128)(2,1)S(1)} %get-tuple-element.41), kind=kLoop, calls=%fused_computation | loop fusion | flops 262144 | bytes 1048576 | tf_op jit(solution)/shard_map/concatenate | solution.py:380
  2.8 3.2 %collective-permute-start = (bf16[2,1024,128]{2,1,0:T(8,128)(2,1)}, bf16[2,1024,128]{2,1,0:T(8,128)(2,1)S(1)}, u32[]{:S(2)}, u32[]{:S(2)}) collective-permute-start(bf16[2,1024,128]{2,1,0:T(8,128)(2,1)} %pad_maximum_fusion), channel_id=1, source_target_pairs={{0,4},{4,0},{1,5},{5,1},{2,6},{6,2},{3,7},{7,3},{8,12},{12,8},{9,1... | collective-permute-start | bytes 1572872 | tf_op jit(solution)/shard_map/ppermute | solution.py:339
  6.0 0.0 copy-start
  6.0 0.0 copy-start.1
  6.0 0.1 pad_maximum_fusion.1
  6.1 2.1 %collective-permute-start.1 = (bf16[2,1024,128]{2,1,0:T(8,128)(2,1)S(1)}, bf16[2,1024,128]{2,1,0:T(8,128)(2,1)S(1)}, u32[]{:S(2)}, u32[]{:S(2)}) collective-permute-start(bf16[2,1024,128]{2,1,0:T(8,128)(2,1)S(1)} %pad_maximum_fusion.1), channel_id=1, source_target_pairs={{4,8},{12,16},{20,24},{28,32},{36,40},{44,48},{52,56},{60,64},{68,... | collective-permute-start | bytes 1572872 | tf_op jit(solution)/shard_map/ppermute | solution.py:345
  8.1 0.0 copy-start.2
  8.2 0.0 copy-start.3
  8.2 0.0 copy-done.4
  8.2 0.0 copy-done.5
  8.2 0.1 pad_add_fusion.parity.place
  8.3 0.0 collective-permute-done.near
  8.3 0.0 copy-done
  8.3 0.0 copy-done.1
  8.3 0.6 copy-done.2
  8.9 0.0 copy-done.3
  8.9 7.1 %shard_map.101 = (bf16[1024,128]{1,0:T(8,128)(2,1)S(1)}, f32[1024,128]{1,0:T(8,128)S(1)}, f32[1024,128]{1,0:T(8,128)S(1)}, bf16[512,768]{1,0:T(8,128)(2,1)S(1)},...) custom-call(s32[2]{0:T(128)S(1)} %pad_add_fusion.parity.place, bf16[2,1024,128]{2,1,0:T(8,128)(2,1)S(1)} %bitcast.9, ...), custom_call_target="tpu_custom_call" | custom-call | flops 8000000000 | bytes 4699656 | tf_op jit(solution)/shard_map/pallas_call | solution.py:323
  16.0 3.6 %collective-permute-start.3 = (bf16[2,1024,128]{2,1,0:T(8,128)(2,1)}, bf16[2,1024,128]{2,1,0:T(8,128)(2,1)S(1)}, u32[]{:S(2)}, u32[]{:S(2)}) collective-permute-start(bf16[2,1024,128]{2,1,0:T(8,128)(2,1)} %pad_maximum_fusion), channel_id=1, source_target_pairs={{4,8},{12,16},{20,24},{28,32},{36,40},{44,48},{52,56},{60,64},{68,... | collective-permute-start | bytes 1572872 | tf_op jit(solution)/shard_map/ppermute | solution.py:345
  19.6 0.0 collective-permute-done.1.far
  19.7 4.2 %shard_map.102 = (bf16[1024,128]{1,0:T(8,128)(2,1)S(1)}, f32[320,128]{1,0:T(8,128)S(1)}) custom-call(s32[2]{0:T(128)S(1)} %pad_add_fusion.parity.place, bf16[2,1024,128]{2,1,0:T(8,128)(2,1)S(1)} %bitcast.10, bf16[2,1024,128]{2,1,0:T(8,128)(2,1)S(1)} %bitcast.14, bf16[2,1024,128]{2,1,0:T(8,128)(2,1)S(1)} %collective-permute-done.1.far, ...), custom_call_target="tpu_custom_call" | custom-call | flops 4000000000 | bytes 4863496 | tf_op jit(solution)/shard_map/pallas_call | solution.py:323
  23.8 17.3 %all_to_all.15 = f32[32,1,1280]{2,1,0:T(1,128)S(1)} all-to-all(f32[32,1,1280]{2,1,0:T(1,128)S(1)} %bitcast.16), channel_id=1, replica_groups=mesh['outer'=4,'ring'=8,'core'=2,'dp'=4] {'outer','core','dp'}, dimensions={0} | all-to-all | bytes 327680 | tf_op jit(solution)/shard_map/all_to_all | solution.py:351
  41.1 0.1 reduce_sum.18
  41.3 0.6 broadcast_in_dim.6
  41.9 5.2 %all-to-all-start.1 = ((f32[8,1,1280]{2,1,0:T(1,128)}), f32[8,1,1280]{2,1,0:T(1,128)S(1)}, u32[]{:S(2)}, u32[]{:S(2)}) async-start(f32[8,1,1280]{2,1,0:T(1,128)} %broadcast_in_dim.6), calls=%async_computation.1 | async-start | bytes 81920 | tf_op jit(solution)/shard_map/all_to_all | solution.py:356
  47.1 0.4 collective-permute-start.2
  47.5 6.5 %all-to-all-done.1 = f32[8,1,1280]{2,1,0:T(1,128)S(1)} async-done(((f32[8,1,1280]{2,1,0:T(1,128)}), f32[8,1,1280]{2,1,0:T(1,128)S(1)}, u32[]{:S(2)}, u32[]{:S(2)}) %all-to-all-start.1) | async-done | bytes 40992 | tf_op jit(solution)/shard_map/all_to_all | solution.py:356
  54.1 0.8 %broadcast_in_dim.7 = f32[32,1,1280]{2,1,0:T(1,128)} broadcast(f32[1280]{0:T(1024)S(1)} %reduce_sum.19), dimensions={2} | broadcast | bytes 168960 | tf_op jit(solution)/shard_map/broadcast_in_dim | solution.py:361
  54.8 5.5 %all-to-all-start.2 = ((f32[32,1,1280]{2,1,0:T(1,128)}), f32[32,1,1280]{2,1,0:T(1,128)S(1)}, u32[]{:S(2)}, u32[]{:S(2)}) async-start(f32[32,1,1280]{2,1,0:T(1,128)} %broadcast_in_dim.7), calls=%async_computation.2 | async-start | bytes 327680 | tf_op jit(solution)/shard_map/all_to_all | solution.py:362
  60.3 0.0 collective-permute-done.3.beyond
  60.3 3.7 %shard_map.103.far = bf16[1024,128]{1,0:T(8,128)(2,1)S(1)} custom-call(s32[2]{0:T(128)S(1)} %pad_add_fusion.parity.place, bf16[2,1024,128]{2,1,0:T(8,128)(2,1)S(1)} %bitcast.11, bf16[2,1024,128]{2,1,0:T(8,128)(2,1)S(1)} %bitcast.15, bf16[2,1024,128]{2,1,0:T(8,128)(2,1)S(1)} %collective-permute-done.1.far, ...), custom_call_target="tpu_custom_call" | custom-call | flops 6000000000 | bytes 2438664 | tf_op jit(solution)/shard_map/pallas_call | solution.py:323
  64.1 0.0 collective-permute-done.2.near
  64.1 3.9 %shard_map.104 = (bf16[2,1024,128]{2,1,0:T(8,128)(2,1)}, f32[8,128]{1,0:T(8,128)S(1)}) custom-call(s32[2]{0:T(128)S(1)} %pad_add_fusion.parity.place, bf16[1024,128]{1,0:T(8,128)(2,1)S(1)} %get-tuple-element.22.inner, bf16[1024,128]{1,0:T(8,128)(2,1)S(1)} %get-tuple-element.28.outer, bf16[1024,128]{1,0:T(8,128)(2,1)S(1)} %collective-permute-done.2.near, ...), custom_call_target="tpu_custom_call" | custom-call | flops 4000000000 | bytes 1616648 | tf_op jit(solution)/shard_map/pallas_call | solution.py:323
  68.0 0.2 all-to-all-done.2
  68.3 0.7 shard_map.105
  (3 shorter events, 0.1 us)
Async XLA Ops:
  1.9 6.3 %copy-start.4 = (bf16[3,3,3,128]{3,2,1,0:T(4,128)(2,1)S(1)}, bf16[3,3,3,128]{3,2,1,0:T(4,128)(2,1)}, u32[]{:S(2)}) copy-start(bf16[3,3,3,128]{3,2,1,0:T(4,128)(2,1)} %param.7) | copy-start | bytes 20740
  1.9 6.3 %copy-start.5 = (bf16[3,3,3,128]{3,2,1,0:T(4,128)(2,1)S(1)}, bf16[3,3,3,128]{3,2,1,0:T(4,128)(2,1)}, u32[]{:S(2)}) copy-start(bf16[3,3,3,128]{3,2,1,0:T(4,128)(2,1)} %param.9) | copy-start | bytes 20740
  2.8 5.5 %collective-permute-start = (bf16[2,1024,128]{2,1,0:T(8,128)(2,1)}, bf16[2,1024,128]{2,1,0:T(8,128)(2,1)S(1)}, u32[]{:S(2)}, u32[]{:S(2)}) collective-permute-start(bf16[2,1024,128]{2,1,0:T(8,128)(2,1)} %pad_maximum_fusion), channel_id=1, source_target_pairs={{0,4},{4,0},{1,5},{5,1},{2,6},{6,2},{3,7},{7,3},{8,12},{12,8},{9,1... | collective-permute-start | bytes 1572872 | tf_op jit(solution)/shard_map/ppermute | solution.py:339
  6.0 2.3 %copy-start = (bf16[1,1,2,16,64,128]{5,4,3,2,1,0:T(8,128)(2,1)S(1)}, bf16[1,1,2,16,64,128]{5,4,3,2,1,0:T(8,128)(2,1)}, u32[]{:S(2)}) copy-start(bf16[1,1,2,16,64,128]{5,4,3,2,1,0:T(8,128)(2,1)} %param.6) | copy-start | bytes 1572868
  6.0 2.3 %copy-start.1 = (bf16[1,1,2,16,64,128]{5,4,3,2,1,0:T(8,128)(2,1)S(1)}, bf16[1,1,2,16,64,128]{5,4,3,2,1,0:T(8,128)(2,1)}, u32[]{:S(2)}) copy-start(bf16[1,1,2,16,64,128]{5,4,3,2,1,0:T(8,128)(2,1)} %param.11) | copy-start | bytes 1572868
  6.1 13.6 %collective-permute-start.1 = (bf16[2,1024,128]{2,1,0:T(8,128)(2,1)S(1)}, bf16[2,1024,128]{2,1,0:T(8,128)(2,1)S(1)}, u32[]{:S(2)}, u32[]{:S(2)}) collective-permute-start(bf16[2,1024,128]{2,1,0:T(8,128)(2,1)S(1)} %pad_maximum_fusion.1), channel_id=1, source_target_pairs={{4,8},{12,16},{20,24},{28,32},{36,40},{44,48},{52,56},{60,64},{68,... | collective-permute-start | bytes 1572872 | tf_op jit(solution)/shard_map/ppermute | solution.py:345
  8.1 0.8 %copy-start.2 = (bf16[128,128]{1,0:T(8,128)(2,1)S(1)}, bf16[128,128]{1,0:T(8,128)(2,1)}, u32[]{:S(2)}) copy-start(bf16[128,128]{1,0:T(8,128)(2,1)} %p2.5) | copy-start | bytes 98308
  8.2 0.8 %copy-start.3 = (bf16[128,128]{1,0:T(8,128)(2,1)S(1)}, bf16[128,128]{1,0:T(8,128)(2,1)}, u32[]{:S(2)}) copy-start(bf16[128,128]{1,0:T(8,128)(2,1)} %p1.7) | copy-start | bytes 98308
  16.0 44.3 %collective-permute-start.3 = (bf16[2,1024,128]{2,1,0:T(8,128)(2,1)}, bf16[2,1024,128]{2,1,0:T(8,128)(2,1)S(1)}, u32[]{:S(2)}, u32[]{:S(2)}) collective-permute-start(bf16[2,1024,128]{2,1,0:T(8,128)(2,1)} %pad_maximum_fusion), channel_id=1, source_target_pairs={{4,8},{12,16},{20,24},{28,32},{36,40},{44,48},{52,56},{60,64},{68,... | collective-permute-start | bytes 1572872 | tf_op jit(solution)/shard_map/ppermute | solution.py:345
  41.9 12.1 %all-to-all-start.1 = ((f32[8,1,1280]{2,1,0:T(1,128)}), f32[8,1,1280]{2,1,0:T(1,128)S(1)}, u32[]{:S(2)}, u32[]{:S(2)}) async-start(f32[8,1,1280]{2,1,0:T(1,128)} %broadcast_in_dim.6), calls=%async_computation.1 | async-start | bytes 81920 | tf_op jit(solution)/shard_map/all_to_all | solution.py:356
  47.1 17.0 %collective-permute-start.2 = (bf16[1024,128]{1,0:T(8,128)(2,1)S(1)}, bf16[1024,128]{1,0:T(8,128)(2,1)S(1)}, u32[]{:S(2)}, u32[]{:S(2)}) collective-permute-start(bf16[1024,128]{1,0:T(8,128)(2,1)S(1)} %get-tuple-element.22.inner), channel_id=1, source_target_pairs={{0,4},{4,0},{1,5},{5,1},{2,6},{6,2},{3,7},{7,3},{8,12},{12,8},{9,1... | collective-permute-start | bytes 786440 | tf_op jit(solution)/shard_map/ppermute | solution.py:339
  54.8 13.4 %all-to-all-start.2 = ((f32[32,1,1280]{2,1,0:T(1,128)}), f32[32,1,1280]{2,1,0:T(1,128)S(1)}, u32[]{:S(2)}, u32[]{:S(2)}) async-start(f32[32,1,1280]{2,1,0:T(1,128)} %broadcast_in_dim.7), calls=%async_computation.2 | async-start | bytes 327680 | tf_op jit(solution)/shard_map/all_to_all | solution.py:362

commit v6 on v4

--- a/solution.py
+++ b/solution.py
@@ -179,19 +179,13 @@
         set_plane(planes, 3 * core, far)
 
 
-def near_kernel(
-    factor,
-    parity, block_in, block_up, near, d1, p1, d2, p2,
-    scaled_out, pre, carried, far_w1, far_w2, terms,
-    planes_in, planes_up, local_one, local_two, side_one, side_two, scaled_t, hidden_t, total,
+def taps_kernel(
+    parity, d1, p1, d2, p2, local_one, local_two, side_one, side_two, far_w1, far_w2
 ):
-    core = parity[0]
-    inner = 1 - core
-    weights = tuple(w[...].astype(jnp.float32) for w in (d1, p1, d2, p2))
-    depth_one, point_one, depth_two, point_two = weights
-    place_planes(planes_in, block_in, core, near[0], None)
-    place_planes(planes_up, block_up, core, near[1], None)
-    near_high = core == 0
+    near_high = parity[0] == 0
+    depth_one, point_one, depth_two, point_two = (
+        w[...].astype(jnp.float32) for w in (d1, p1, d2, p2)
+    )
     taps_one = forward_taps(columns_of(depth_one), point_one)
     taps_two = backward_taps(depth_two, point_two.T)
     for taps, local, side, other in (
@@ -201,6 +195,20 @@
         fill_local(local, taps)
         fill_side(side, taps, near_high)
         fill_side(other, taps, jnp.logical_not(near_high))
+
+
+def near_kernel(
+    factor,
+    parity, block_in, block_up, near, local_one, local_two, side_one, side_two, d1, p1, d2, p2,
+    scaled_out, pre, carried, terms,
+    planes_in, planes_up, scaled_t, hidden_t, total,
+):
+    core = parity[0]
+    inner = 1 - core
+    weights = tuple(w[...].astype(jnp.float32) for w in (d1, p1, d2, p2))
+    place_planes(planes_in, block_in, core, near[0], None)
+    place_planes(planes_up, block_up, core, near[1], None)
+    near_high = core == 0
     near_slot = 3 - 3 * core
     for half in range(0, CELLS, 2 * ROWS):
         side_in = side_products(planes_in, near_slot, side_one, half)
@@ -268,6 +276,14 @@
     done[...] = jnp.zeros((8, CH), jnp.float32)
 
 
+def sum_kernel(arrived, copies):
+    total = arrived[0]
+    for i in range(1, arrived.shape[0]):
+        total = total + arrived[i]
+    for i in range(copies.shape[0]):
+        copies[i] = total
+
+
 def parts_kernel(sums, done, depth_one, point_one, depth_two, point_two):
     for a in range(3):
         for b in range(3):
@@ -317,12 +333,15 @@
 
 def reduced_around(share):
     copies = jnp.broadcast_to(share, (lax.axis_size("ring"), *share.shape))
-    return lax.all_to_all(copies, "ring", 0, 0, tiled=True).sum(axis=0)
-
-
-def gathered_across(share):
+    arrived = lax.all_to_all(copies, "ring", 0, 0, tiled=True)
     count = math.prod(lax.axis_size(name) for name in ACROSS)
-    copies = jnp.broadcast_to(share, (count, *share.shape))
+    (copies,) = call(
+        sum_kernel, [], [jax.ShapeDtypeStruct((count, *share.shape), share.dtype)], 0, arrived
+    )
+    return copies
+
+
+def gathered_across(copies):
     return lax.all_to_all(copies, ACROSS, 0, 0, tiled=True).reshape(TERMS, CH)
 
 
@@ -342,8 +361,10 @@
             [lax.dynamic_slice_in_dim(block, x, 1, 0) for block in (block_in, block_up)], axis=0
         )
 
-    far = with_other_chip(both(core))
-    near = with_other_core(both(1 - core))
+    outer = both(core)
+    outer, inner = lax.optimization_barrier((outer, 1 - core))
+    far = with_other_chip(outer)
+    near = with_other_core(both(inner))
     slots = pltpu.VMEM((4, PADDED, CH), bf16)
     local_w = pltpu.VMEM((6 * CH, 6 * CH), bf16)
     side_w = pltpu.VMEM((4 * CH, 6 * CH), bf16)
@@ -351,15 +372,20 @@
     totals = pltpu.VMEM((3, CH, CH), f32)
     devices = math.prod(lax.axis_size(name) for name in ("dp", *SPACE))
     factor = 1.0 / math.sqrt(devices * 2 * CELLS)
-    inner, pre, carried, far_w1, far_w2, terms = call(
+    local_one, local_two, side_one, side_two, far_w1, far_w2 = call(
+        taps_kernel,
+        [],
+        [shape((6 * CH, 6 * CH), bf16)] * 2 + [shape((4 * CH, 6 * CH), bf16)] * 4,
+        1_000_000_000,
+        parity, d1, point_one, d2, point_two,
+    )
+    inner, pre, carried, terms = call(
         functools.partial(near_kernel, factor),
-        [slots, slots, local_w, local_w, side_w, side_w, flipped, flipped, totals],
-        [shape((CELLS, CH), bf16)]
-        + [shape((CELLS, CH), f32)] * 2
-        + [shape((4 * CH, 6 * CH), bf16)] * 2
-        + [shape((TERMS, CH), f32)],
-        8_000_000_000,
-        parity, block_in, block_up, near, d1, point_one, d2, point_two,
+        [slots, slots, flipped, flipped, totals],
+        [shape((CELLS, CH), bf16)] + [shape((CELLS, CH), f32)] * 2 + [shape((TERMS, CH), f32)],
+        6_000_000_000,
+        parity, block_in, block_up, near, local_one, local_two, side_one, side_two,
+        d1, point_one, d2, point_two,
     )
     outer, terms = call(
         functools.partial(far_kernel, factor),

time: 67.3 us -> 67.1 us (level)
  Pallas kernels: 14.2 us -> 15.2 us
  local copies, waits for them, and re-layouts: 2.1 us -> 1.32 us
    pallas_call x4 -> x6, Pallas kernels: 14.2 us -> 15.2 us  [call(): pl.pallas_call(kernel, out_shape=outs, in_specs=[smem if a.dtype == jnp.i...]
    broadcast_in_dim x1 -> x0, local copies, waits for them, and re-layouts: 0.75 us -> none  [gathered_across(): copies = jnp.broadcast_to(share, (count, *share.shape))]
  transfers between devices with their start and end apart: 5 -> 5, of which waited for: 2 -> 2; matrix products, arithmetic and copies ran while one was open for 1% -> 0% of each run, Pallas kernels for 15% -> 16%
where the time goes in v6:
time: 67.1 us; the launch traced here: 66.7 us
  blocking collectives  30.4 us (45%)
  Pallas kernels  15.2 us (23%)
  starting transfers between devices  12.6 us (19%)
  waiting for transfers between devices  6.12 us (9%)
  local copies, waits for them, and re-layouts  1.32 us (2%)
  between operations  0.84 us (1%)
    all_to_all x1, blocking collectives, reduced_across(): return lax.all_to_all(tiles, ACROSS, 0, 0, tiled=True).sum(axis=0)  21.1 us
    pallas_call x6, Pallas kernels, call(): pl.pallas_call(kernel, out_shape=outs, in_specs=[smem if a.dtype == jnp.i...  15.2 us
    all_to_all x1, blocking collectives, reduced_around(): arrived = lax.all_to_all(copies, 'ring', 0, 0, tiled=True)  9.33 us
    all_to_all x1, starting transfers between devices, gathered_across(): return lax.all_to_all(copies, ACROSS, 0, 0, tiled=True).reshape(TERMS, CH)  5.2 us
    all_to_all x1, waiting for transfers between devices, gathered_across(): return lax.all_to_all(copies, ACROSS, 0, 0, tiled=True).reshape(TERMS, CH)  4.54 us
    ppermute x2, starting transfers between devices, with_other_chip(): return lax.ppermute(v, SPACE, pairs + [(j, i) for i, j in pairs])  3.99 us
    ppermute x2, starting transfers between devices, with_other_core(): return lax.ppermute(v, 'core', [(0, 1), (1, 0)])  3.42 us
    ppermute x2, waiting for transfers between devices, with_other_chip(): return lax.ppermute(v, SPACE, pairs + [(j, i) for i, j in pairs])  1.57 us
  transfers between devices with their start and end apart: 5, of which 2 were waited for; matrix products, arithmetic and copies ran while one was open for 0% of the time, Pallas kernels for 16%

profile of v6, /device:TPU:1, one launch (start us, length us, event | category | flops | bytes accessed | tf_op | source)
XLA Modules:
  0.0 66.7 jit_solution(15732365882942141051)
XLA Ops:
  0.6 0.0 copy-start.1
  0.6 0.0 copy-start
  0.7 1.2 %constant_dynamic-slice_fusion.2 = (bf16[1,1024,128]{2,1,0:T(8,128)(2,1)S(1)}, bf16[1,1024,128]{2,1,0:T(8,128)(2,1)S(1)}) fusion(bf16[2,1024,128]{2,1,0:T(8,128)(2,1)} %bitcast.11, s32[]{:T(128)S(6)} %select_n.8, bf16[2,1024,128]{2,1,0:T(8,128)(2,1)} %bitcast.7), kind=kLoop, calls=%fused_computation.4 | loop fusion | bytes 1048580 | tf_op jit(solution)/shard_map/dynamic_slice | solution.py:361
  1.8 0.1 pad_maximum_fusion
  1.9 0.0 copy-start.4
  1.9 0.0 copy-start.5
  1.9 0.0 copy-start.2
  1.9 0.0 copy-start.3
  1.9 0.0 copy-done.1
  2.0 0.0 copy-done
  2.0 0.1 pad_maximum_fusion.1
  2.1 3.3 %collective-permute-start = (bf16[2,1024,128]{2,1,0:T(8,128)(2,1)S(1)}, bf16[2,1024,128]{2,1,0:T(8,128)(2,1)S(1)}, u32[]{:S(2)}, u32[]{:S(2)}) collective-permute-start(bf16[2,1024,128]{2,1,0:T(8,128)(2,1)S(1)} %pad_maximum_fusion.1), channel_id=1, source_target_pairs={{0,4},{4,0},{1,5},{5,1},{2,6},{6,2},{3,7},{7,3},{8,12},{12,8},{9,1... | collective-permute-start | bytes 1572872 | tf_op jit(solution)/shard_map/ppermute | solution.py:319
  5.4 1.9 %collective-permute-start.1 = (bf16[2,1024,128]{2,1,0:T(8,128)(2,1)S(1)}, bf16[2,1024,128]{2,1,0:T(8,128)(2,1)S(1)}, u32[]{:S(2)}, u32[]{:S(2)}) collective-permute-start(bf16[2,1024,128]{2,1,0:T(8,128)(2,1)S(1)} %pad_maximum_fusion), channel_id=1, source_target_pairs={{4,8},{12,16},{20,24},{28,32},{36,40},{44,48},{52,56},{60,64},{68,... | collective-permute-start | bytes 1572872 | tf_op jit(solution)/shard_map/ppermute | solution.py:325
  7.3 0.0 copy-done.4
  7.3 0.0 copy-done.5
  7.4 0.0 copy-done.2
  7.4 0.0 copy-done.3
  7.4 0.9 %shard_map.101 = (bf16[768,768]{1,0:T(8,128)(2,1)S(1)}, bf16[768,768]{1,0:T(8,128)(2,1)S(1)}, bf16[512,768]{1,0:T(8,128)(2,1)S(1)}, bf16[512,768]{1,0:T(8,128)(2...) custom-call(s32[1]{0:T(128)} %bitcast.parity, bf16[27,128]{1,0:T(8,128)(2,1)S(1)} %reshape.40.d1, ...), custom_call_target="tpu_custom_call" | custom-call | flops 1000000000 | bytes 5584388 | tf_op jit(solution)/shard_map/pallas_call | solution.py:303
  8.3 0.0 collective-permute-done.near
  8.3 6.0 %shard_map.102 = (bf16[1024,128]{1,0:T(8,128)(2,1)S(1)}, f32[1024,128]{1,0:T(8,128)S(1)}, f32[1024,128]{1,0:T(8,128)S(1)}, f32[320,128]{1,0:T(8,128)S(1)}) custom-call(s32[1]{0:T(128)} %bitcast.parity, bf16[2,1024,128]{2,1,0:T(8,128)(2,1)S(1)} %bitcast.9, bf16[2,1024,128]{2,1,0:T(8,128)(2,1)S(1)} %bitcast.13, ...), custom_call_target="tpu_custom_call" | custom-call | flops 6000000000 | bytes 7058948 | tf_op jit(solution)/shard_map/pallas_call | solution.py:303
  14.3 1.6 %collective-permute-done.1.far = bf16[2,1024,128]{2,1,0:T(8,128)(2,1)S(1)} collective-permute-done((bf16[2,1024,128]{2,1,0:T(8,128)(2,1)S(1)}, bf16[2,1024,128]{2,1,0:T(8,128)(2,1)S(1)}, u32[]{:S(2)}, u32[]{:S(2)}) %collective-permute-start.1) | collective-permute-done | bytes 524320 | tf_op jit(solution)/shard_map/ppermute | solution.py:325
  15.9 3.6 %shard_map.103 = (bf16[1024,128]{1,0:T(8,128)(2,1)S(1)}, f32[320,128]{1,0:T(8,128)S(1)}) custom-call(s32[1]{0:T(128)} %bitcast.parity, bf16[2,1024,128]{2,1,0:T(8,128)(2,1)S(1)} %bitcast.10, bf16[2,1024,128]{2,1,0:T(8,128)(2,1)S(1)} %bitcast.14, bf16[2,1024,128]{2,1,0:T(8,128)(2,1)S(1)} %collective-permute-done.1.far, ...), custom_call_target="tpu_custom_call" | custom-call | flops 4000000000 | bytes 4863492 | tf_op jit(solution)/shard_map/pallas_call | solution.py:303
  19.5 2.1 %collective-permute-start.3 = (bf16[1024,128]{1,0:T(8,128)(2,1)S(1)}, bf16[1024,128]{1,0:T(8,128)(2,1)S(1)}, u32[]{:S(2)}, u32[]{:S(2)}) collective-permute-start(bf16[1024,128]{1,0:T(8,128)(2,1)S(1)} %get-tuple-element.37.outer), channel_id=1, source_target_pairs={{4,8},{12,16},{20,24},{28,32},{36,40},{44,48},{52,56},{60,64},{68,... | collective-permute-start | bytes 786440 | tf_op jit(solution)/shard_map/ppermute | solution.py:325
  21.6 0.1 collective-permute-start.2
  21.7 21.1 %all_to_all.15 = f32[32,1,1280]{2,1,0:T(1,128)S(1)} all-to-all(f32[32,1,1280]{2,1,0:T(1,128)S(1)} %bitcast.15), channel_id=1, replica_groups=mesh['outer'=4,'ring'=8,'core'=2,'dp'=4] {'outer','core','dp'}, dimensions={0} | all-to-all | bytes 327680 | tf_op jit(solution)/shard_map/all_to_all | solution.py:331
  42.8 0.1 reduce_sum.9
  42.9 9.3 %all_to_all.16.arrived = f32[8,1,1280]{2,1,0:T(1,128)S(1)} all-to-all(f32[8,1,1280]{2,1,0:T(1,128)S(1)} %broadcast_in_dim.3), channel_id=1, replica_groups=mesh['outer'=4,'ring'=8,'core'=2,'dp'=4] {'ring'}, dimensions={0} | all-to-all | bytes 81920 | tf_op jit(solution)/shard_map/all_to_all | solution.py:336
  52.2 0.7 %shard_map.105 = f32[32,1,1280]{2,1,0:T(1,128)} custom-call(f32[8,1,1280]{2,1,0:T(1,128)S(1)} %all_to_all.16.arrived), custom_call_target="tpu_custom_call" | custom-call | bytes 204800 | tf_op jit(solution)/shard_map/pallas_call | solution.py:303
  52.9 5.2 %all-to-all-start.2 = ((f32[32,1,1280]{2,1,0:T(1,128)}), f32[32,1,1280]{2,1,0:T(1,128)S(1)}, u32[]{:S(2)}, u32[]{:S(2)}) async-start(f32[32,1,1280]{2,1,0:T(1,128)} %shard_map.105), calls=%async_computation.2 | async-start | bytes 327680 | tf_op jit(solution)/shard_map/all_to_all | solution.py:345
  58.1 0.0 collective-permute-done.3.far
  58.1 0.0 collective-permute-done.2.near
  58.2 3.4 %shard_map.104 = (bf16[2,1024,128]{2,1,0:T(8,128)(2,1)}, f32[8,128]{1,0:T(8,128)S(1)}) custom-call(s32[1]{0:T(128)} %bitcast.parity, bf16[1024,128]{1,0:T(8,128)(2,1)S(1)} %get-tuple-element.30.inner, bf16[1024,128]{1,0:T(8,128)(2,1)S(1)} %get-tuple-element.37.outer, bf16[1024,128]{1,0:T(8,128)(2,1)S(1)} %collective-permute-done.2.near, ...), custom_call_target="tpu_custom_call" | custom-call | flops 4000000000 | bytes 1616644 | tf_op jit(solution)/shard_map/pallas_call | solution.py:303
  61.5 4.5 %all-to-all-done.2 = f32[32,1,1280]{2,1,0:T(1,128)S(1)} async-done(((f32[32,1,1280]{2,1,0:T(1,128)}), f32[32,1,1280]{2,1,0:T(1,128)S(1)}, u32[]{:S(2)}, u32[]{:S(2)}) %all-to-all-start.2) | async-done | bytes 163872 | tf_op jit(solution)/shard_map/all_to_all | solution.py:345
  66.1 0.7 %shard_map.106 = (f32[3,3,3,128]{3,2,1,0:T(4,128)}, f32[128,128]{1,0:T(8,128)}, f32[3,3,3,128]{3,2,1,0:T(4,128)}, f32[128,128]{1,0:T(8,128)}) custom-call(f32[320,128]{1,0:T(8,128)S(1)} %bitcast.6, f32[8,128]{1,0:T(8,128)S(1)} %get-tuple-element.40.done), custom_call_target="tpu_custom_call" | custom-call | bytes 326656 | tf_op jit(solution)/shard_map/pallas_call | solution.py:303
  (5 shorter events, 0.1 us)
Async XLA Ops:
  0.6 1.3 %copy-start.1 = (bf16[1,1,2,16,64,128]{5,4,3,2,1,0:T(8,128)(2,1)S(1)}, bf16[1,1,2,16,64,128]{5,4,3,2,1,0:T(8,128)(2,1)}, u32[]{:S(2)}) copy-start(bf16[1,1,2,16,64,128]{5,4,3,2,1,0:T(8,128)(2,1)} %param.11) | copy-start | bytes 1572868
  0.6 1.3 %copy-start = (bf16[1,1,2,16,64,128]{5,4,3,2,1,0:T(8,128)(2,1)S(1)}, bf16[1,1,2,16,64,128]{5,4,3,2,1,0:T(8,128)(2,1)}, u32[]{:S(2)}) copy-start(bf16[1,1,2,16,64,128]{5,4,3,2,1,0:T(8,128)(2,1)} %param.6) | copy-start | bytes 1572868
  1.9 5.4 %copy-start.4 = (bf16[3,3,3,128]{3,2,1,0:T(4,128)(2,1)S(1)}, bf16[3,3,3,128]{3,2,1,0:T(4,128)(2,1)}, u32[]{:S(2)}) copy-start(bf16[3,3,3,128]{3,2,1,0:T(4,128)(2,1)} %param.7) | copy-start | bytes 20740
  1.9 5.5 %copy-start.5 = (bf16[3,3,3,128]{3,2,1,0:T(4,128)(2,1)S(1)}, bf16[3,3,3,128]{3,2,1,0:T(4,128)(2,1)}, u32[]{:S(2)}) copy-start(bf16[3,3,3,128]{3,2,1,0:T(4,128)(2,1)} %param.9) | copy-start | bytes 20740
  1.9 5.5 %copy-start.2 = (bf16[128,128]{1,0:T(8,128)(2,1)S(1)}, bf16[128,128]{1,0:T(8,128)(2,1)}, u32[]{:S(2)}) copy-start(bf16[128,128]{1,0:T(8,128)(2,1)} %p2.5) | copy-start | bytes 98308
  1.9 5.5 %copy-start.3 = (bf16[128,128]{1,0:T(8,128)(2,1)S(1)}, bf16[128,128]{1,0:T(8,128)(2,1)}, u32[]{:S(2)}) copy-start(bf16[128,128]{1,0:T(8,128)(2,1)} %p1.7) | copy-start | bytes 98308
  2.1 6.2 %collective-permute-start = (bf16[2,1024,128]{2,1,0:T(8,128)(2,1)S(1)}, bf16[2,1024,128]{2,1,0:T(8,128)(2,1)S(1)}, u32[]{:S(2)}, u32[]{:S(2)}) collective-permute-start(bf16[2,1024,128]{2,1,0:T(8,128)(2,1)S(1)} %pad_maximum_fusion.1), channel_id=1, source_target_pairs={{0,4},{4,0},{1,5},{5,1},{2,6},{6,2},{3,7},{7,3},{8,12},{12,8},{9,1... | collective-permute-start | bytes 1572872 | tf_op jit(solution)/shard_map/ppermute | solution.py:319
  5.4 10.5 %collective-permute-start.1 = (bf16[2,1024,128]{2,1,0:T(8,128)(2,1)S(1)}, bf16[2,1024,128]{2,1,0:T(8,128)(2,1)S(1)}, u32[]{:S(2)}, u32[]{:S(2)}) collective-permute-start(bf16[2,1024,128]{2,1,0:T(8,128)(2,1)S(1)} %pad_maximum_fusion), channel_id=1, source_target_pairs={{4,8},{12,16},{20,24},{28,32},{36,40},{44,48},{52,56},{60,64},{68,... | collective-permute-start | bytes 1572872 | tf_op jit(solution)/shard_map/ppermute | solution.py:325
  19.5 38.6 %collective-permute-start.3 = (bf16[1024,128]{1,0:T(8,128)(2,1)S(1)}, bf16[1024,128]{1,0:T(8,128)(2,1)S(1)}, u32[]{:S(2)}, u32[]{:S(2)}) collective-permute-start(bf16[1024,128]{1,0:T(8,128)(2,1)S(1)} %get-tuple-element.37.outer), channel_id=1, source_target_pairs={{4,8},{12,16},{20,24},{28,32},{36,40},{44,48},{52,56},{60,64},{68,... | collective-permute-start | bytes 786440 | tf_op jit(solution)/shard_map/ppermute | solution.py:325
  21.6 36.6 %collective-permute-start.2 = (bf16[1024,128]{1,0:T(8,128)(2,1)S(1)}, bf16[1024,128]{1,0:T(8,128)(2,1)S(1)}, u32[]{:S(2)}, u32[]{:S(2)}) collective-permute-start(bf16[1024,128]{1,0:T(8,128)(2,1)S(1)} %get-tuple-element.30.inner), channel_id=1, source_target_pairs={{0,4},{4,0},{1,5},{5,1},{2,6},{6,2},{3,7},{7,3},{8,12},{12,8},{9,1... | collective-permute-start | bytes 786440 | tf_op jit(solution)/shard_map/ppermute | solution.py:319
  52.9 13.1 %all-to-all-start.2 = ((f32[32,1,1280]{2,1,0:T(1,128)}), f32[32,1,1280]{2,1,0:T(1,128)S(1)}, u32[]{:S(2)}, u32[]{:S(2)}) async-start(f32[32,1,1280]{2,1,0:T(1,128)} %shard_map.105), calls=%async_computation.2 | async-start | bytes 327680 | tf_op jit(solution)/shard_map/all_to_all | solution.py:345

commit v7 on v6

--- a/solution.py
+++ b/solution.py
@@ -395,7 +395,8 @@
         parity, block_in, block_up, far, pre, carried, far_w1, far_w2,
         d1, point_one, d2, point_two, terms,
     )
-    share = reduced_across(terms)
+    copies = reduced_around(reduced_across(terms))
+    copies, inner, outer = lax.optimization_barrier((copies, inner, outer))
     outer_beside = with_other_chip(outer)
     inner_beside = with_other_core(inner)
     grad, done = call(
@@ -405,7 +406,7 @@
         4_000_000_000,
         parity, inner, outer, inner_beside, outer_beside, d1, point_one,
     )
-    sums = gathered_across(reduced_around(share))
+    sums = gathered_across(copies)
     depth, point = (shape((3, 3, 3, CH), f32), shape((CH, CH), f32))
     parts = call(parts_kernel, [], [depth, point, depth, point], 0, sums, done)
     return (grad.reshape(inputs.shape), *parts)

time: 67.1 us -> 67.2 us (level)
  starting transfers between devices: 12.6 us -> 13.9 us
  blocking collectives: 30.4 us -> 29.3 us
    all_to_all x1, blocking collectives: 21.1 us -> 17.5 us  [reduced_across(): return lax.all_to_all(tiles, ACROSS, 0, 0, tiled=True).sum(axis=0)]
    all_to_all x1, blocking collectives: 9.33 us -> 11.8 us  [reduced_around(): arrived = lax.all_to_all(copies, 'ring', 0, 0, tiled=True)]
    ppermute x2, starting transfers between devices: 3.42 us -> 4.91 us  [with_other_core(): return lax.ppermute(v, 'core', [(0, 1), (1, 0)])]
  transfers between devices with their start and end apart: 5 -> 5, of which waited for: 2 -> 3; matrix products, arithmetic and copies ran while one was open for 0% -> 0% of each run, Pallas kernels for 16% -> 15%
where the time goes in v7:
time: 67.2 us; the launch traced here: 66.9 us
  blocking collectives  29.3 us (44%)
  Pallas kernels  15.2 us (23%)
  starting transfers between devices  13.9 us (21%)
  waiting for transfers between devices  6.13 us (9%)
  local copies, waits for them, and re-layouts  1.32 us (2%)
  between operations  0.83 us (1%)
    all_to_all x1, blocking collectives, reduced_across(): return lax.all_to_all(tiles, ACROSS, 0, 0, tiled=True).sum(axis=0)  17.5 us
    pallas_call x6, Pallas kernels, call(): pl.pallas_call(kernel, out_shape=outs, in_specs=[smem if a.dtype == jnp.i...  15.2 us
    all_to_all x1, blocking collectives, reduced_around(): arrived = lax.all_to_all(copies, 'ring', 0, 0, tiled=True)  11.8 us
    all_to_all x1, starting transfers between devices, gathered_across(): return lax.all_to_all(copies, ACROSS, 0, 0, tiled=True).reshape(TERMS, CH)  4.99 us
    ppermute x2, starting transfers between devices, with_other_core(): return lax.ppermute(v, 'core', [(0, 1), (1, 0)])  4.91 us
    ppermute x2, starting transfers between devices, with_other_chip(): return lax.ppermute(v, SPACE, pairs + [(j, i) for i, j in pairs])  3.98 us
    all_to_all x1, waiting for transfers between devices, gathered_across(): return lax.all_to_all(copies, ACROSS, 0, 0, tiled=True).reshape(TERMS, CH)  3.96 us
    ppermute x2, waiting for transfers between devices, with_other_chip(): return lax.ppermute(v, SPACE, pairs + [(j, i) for i, j in pairs])  2.16 us
  transfers between devices with their start and end apart: 5, of which 3 were waited for; matrix products, arithmetic and copies ran while one was open for 0% of the time, Pallas kernels for 15%

profile of v7, /device:TPU:1, one launch (start us, length us, event | category | flops | bytes accessed | tf_op | source)
XLA Modules:
  0.0 66.9 jit_solution(16549242408984170501)
XLA Ops:
  0.6 0.0 copy-start.1
  0.6 0.0 copy-start
  0.7 1.2 %constant_dynamic-slice_fusion.2 = (bf16[1,1024,128]{2,1,0:T(8,128)(2,1)S(1)}, bf16[1,1024,128]{2,1,0:T(8,128)(2,1)S(1)}) fusion(bf16[2,1024,128]{2,1,0:T(8,128)(2,1)} %bitcast.11, s32[]{:T(128)S(6)} %select_n.8, bf16[2,1024,128]{2,1,0:T(8,128)(2,1)} %bitcast.7), kind=kLoop, calls=%fused_computation.4 | loop fusion | bytes 1048580 | tf_op jit(solution)/shard_map/dynamic_slice | solution.py:361
  1.8 0.1 pad_maximum_fusion
  1.9 0.0 copy-start.4
  1.9 0.0 copy-start.5
  1.9 0.0 copy-start.2
  1.9 0.0 copy-start.3
  1.9 0.0 copy-done.1
  2.0 0.0 copy-done
  2.0 0.1 pad_maximum_fusion.1
  2.1 3.3 %collective-permute-start.1 = (bf16[2,1024,128]{2,1,0:T(8,128)(2,1)S(1)}, bf16[2,1024,128]{2,1,0:T(8,128)(2,1)S(1)}, u32[]{:S(2)}, u32[]{:S(2)}) collective-permute-start(bf16[2,1024,128]{2,1,0:T(8,128)(2,1)S(1)} %pad_maximum_fusion.1), channel_id=1, source_target_pairs={{0,4},{4,0},{1,5},{5,1},{2,6},{6,2},{3,7},{7,3},{8,12},{12,8},{9,1... | collective-permute-start | bytes 1572872 | tf_op jit(solution)/shard_map/ppermute | solution.py:319
  5.4 1.9 %collective-permute-start = (bf16[2,1024,128]{2,1,0:T(8,128)(2,1)S(1)}, bf16[2,1024,128]{2,1,0:T(8,128)(2,1)S(1)}, u32[]{:S(2)}, u32[]{:S(2)}) collective-permute-start(bf16[2,1024,128]{2,1,0:T(8,128)(2,1)S(1)} %pad_maximum_fusion), channel_id=1, source_target_pairs={{4,8},{12,16},{20,24},{28,32},{36,40},{44,48},{52,56},{60,64},{68,... | collective-permute-start | bytes 1572872 | tf_op jit(solution)/shard_map/ppermute | solution.py:325
  7.3 0.0 copy-done.4
  7.3 0.0 copy-done.5
  7.4 0.0 copy-done.2
  7.4 0.0 copy-done.3
  7.4 0.9 %shard_map.101 = (bf16[768,768]{1,0:T(8,128)(2,1)S(1)}, bf16[768,768]{1,0:T(8,128)(2,1)S(1)}, bf16[512,768]{1,0:T(8,128)(2,1)S(1)}, bf16[512,768]{1,0:T(8,128)(2...) custom-call(s32[1]{0:T(128)} %bitcast.parity, bf16[27,128]{1,0:T(8,128)(2,1)S(1)} %reshape.40.d1, ...), custom_call_target="tpu_custom_call" | custom-call | flops 1000000000 | bytes 5584388 | tf_op jit(solution)/shard_map/pallas_call | solution.py:303
  8.3 0.0 collective-permute-done.1.near
  8.3 6.0 %shard_map.102 = (bf16[1024,128]{1,0:T(8,128)(2,1)S(1)}, f32[1024,128]{1,0:T(8,128)S(1)}, f32[1024,128]{1,0:T(8,128)S(1)}, f32[320,128]{1,0:T(8,128)S(1)}) custom-call(s32[1]{0:T(128)} %bitcast.parity, bf16[2,1024,128]{2,1,0:T(8,128)(2,1)S(1)} %bitcast.9, bf16[2,1024,128]{2,1,0:T(8,128)(2,1)S(1)} %bitcast.13, ...), custom_call_target="tpu_custom_call" | custom-call | flops 6000000000 | bytes 7058948 | tf_op jit(solution)/shard_map/pallas_call | solution.py:303
  14.3 1.6 %collective-permute-done.far = bf16[2,1024,128]{2,1,0:T(8,128)(2,1)S(1)} collective-permute-done((bf16[2,1024,128]{2,1,0:T(8,128)(2,1)S(1)}, bf16[2,1024,128]{2,1,0:T(8,128)(2,1)S(1)}, u32[]{:S(2)}, u32[]{:S(2)}) %collective-permute-start) | collective-permute-done | bytes 524320 | tf_op jit(solution)/shard_map/ppermute | solution.py:325
  15.9 3.6 %shard_map.103 = (bf16[1024,128]{1,0:T(8,128)(2,1)S(1)}, f32[320,128]{1,0:T(8,128)S(1)}) custom-call(s32[1]{0:T(128)} %bitcast.parity, bf16[2,1024,128]{2,1,0:T(8,128)(2,1)S(1)} %bitcast.10, bf16[2,1024,128]{2,1,0:T(8,128)(2,1)S(1)} %bitcast.14, bf16[2,1024,128]{2,1,0:T(8,128)(2,1)S(1)} %collective-permute-done.far, f32[1024,128]{1,0:T(8,128)S(1)} %get-tuple-element.34.pre, ...), custom_call_target="tpu_custom_call" | custom-call | flops 4000000000 | bytes 4863492 | tf_op jit(solution)/shard_map/pallas_call | solution.py:303
  19.5 17.5 %all_to_all.15 = f32[32,1,1280]{2,1,0:T(1,128)S(1)} all-to-all(f32[32,1,1280]{2,1,0:T(1,128)S(1)} %bitcast.15), channel_id=1, replica_groups=mesh['outer'=4,'ring'=8,'core'=2,'dp'=4] {'outer','core','dp'}, dimensions={0} | all-to-all | bytes 327680 | tf_op jit(solution)/shard_map/all_to_all | solution.py:331
  37.0 0.1 reduce_sum.9
  37.1 11.8 %all_to_all.16.arrived = f32[8,1,1280]{2,1,0:T(1,128)S(1)} all-to-all(f32[8,1,1280]{2,1,0:T(1,128)S(1)} %broadcast_in_dim.3), channel_id=1, replica_groups=mesh['outer'=4,'ring'=8,'core'=2,'dp'=4] {'ring'}, dimensions={0} | all-to-all | bytes 81920 | tf_op jit(solution)/shard_map/all_to_all | solution.py:336
  48.9 0.7 %shard_map.104 = f32[32,1,1280]{2,1,0:T(1,128)} custom-call(f32[8,1,1280]{2,1,0:T(1,128)S(1)} %all_to_all.16.arrived), custom_call_target="tpu_custom_call" | custom-call | bytes 204800 | tf_op jit(solution)/shard_map/pallas_call | solution.py:303
  49.6 1.6 %collective-permute-start.2 = (bf16[1024,128]{1,0:T(8,128)(2,1)S(1)}, bf16[1024,128]{1,0:T(8,128)(2,1)S(1)}, u32[]{:S(2)}, u32[]{:S(2)}) collective-permute-start(bf16[1024,128]{1,0:T(8,128)(2,1)S(1)} %get-tuple-element.42.inner), channel_id=1, source_target_pairs={{0,4},{4,0},{1,5},{5,1},{2,6},{6,2},{3,7},{7,3},{8,12},{12,8},{9,1... | collective-permute-start | bytes 786440 | tf_op jit(solution)/shard_map/ppermute | solution.py:319
  51.2 2.1 %collective-permute-start.3 = (bf16[1024,128]{1,0:T(8,128)(2,1)S(1)}, bf16[1024,128]{1,0:T(8,128)(2,1)S(1)}, u32[]{:S(2)}, u32[]{:S(2)}) collective-permute-start(bf16[1024,128]{1,0:T(8,128)(2,1)S(1)} %get-tuple-element.43.outer), channel_id=1, source_target_pairs={{4,8},{12,16},{20,24},{28,32},{36,40},{44,48},{52,56},{60,64},{68,... | collective-permute-start | bytes 786440 | tf_op jit(solution)/shard_map/ppermute | solution.py:325
  53.2 5.0 %all-to-all-start.2 = ((f32[32,1,1280]{2,1,0:T(1,128)}), f32[32,1,1280]{2,1,0:T(1,128)S(1)}, u32[]{:S(2)}, u32[]{:S(2)}) async-start(f32[32,1,1280]{2,1,0:T(1,128)} %shard_map.104), calls=%async_computation.2 | async-start | bytes 327680 | tf_op jit(solution)/shard_map/all_to_all | solution.py:345
  58.2 0.0 collective-permute-done.2.near
  58.3 0.6 collective-permute-done.3.far
  58.8 3.4 %shard_map.105 = (bf16[2,1024,128]{2,1,0:T(8,128)(2,1)}, f32[8,128]{1,0:T(8,128)S(1)}) custom-call(s32[1]{0:T(128)} %bitcast.parity, bf16[1024,128]{1,0:T(8,128)(2,1)S(1)} %get-tuple-element.42.inner, bf16[1024,128]{1,0:T(8,128)(2,1)S(1)} %get-tuple-element.43.outer, bf16[1024,128]{1,0:T(8,128)(2,1)S(1)} %collective-permute-done.2.near, ...), custom_call_target="tpu_custom_call" | custom-call | flops 4000000000 | bytes 1616644 | tf_op jit(solution)/shard_map/pallas_call | solution.py:303
  62.2 4.0 %all-to-all-done.2 = f32[32,1,1280]{2,1,0:T(1,128)S(1)} async-done(((f32[32,1,1280]{2,1,0:T(1,128)}), f32[32,1,1280]{2,1,0:T(1,128)S(1)}, u32[]{:S(2)}, u32[]{:S(2)}) %all-to-all-start.2) | async-done | bytes 163872 | tf_op jit(solution)/shard_map/all_to_all | solution.py:345
  66.2 0.7 %shard_map.106 = (f32[3,3,3,128]{3,2,1,0:T(4,128)}, f32[128,128]{1,0:T(8,128)}, f32[3,3,3,128]{3,2,1,0:T(4,128)}, f32[128,128]{1,0:T(8,128)}) custom-call(f32[320,128]{1,0:T(8,128)S(1)} %bitcast.6, f32[8,128]{1,0:T(8,128)S(1)} %get-tuple-element.46.done), custom_call_target="tpu_custom_call" | custom-call | bytes 326656 | tf_op jit(solution)/shard_map/pallas_call | solution.py:303
  (5 shorter events, 0.1 us)
Async XLA Ops:
  0.6 1.3 %copy-start.1 = (bf16[1,1,2,16,64,128]{5,4,3,2,1,0:T(8,128)(2,1)S(1)}, bf16[1,1,2,16,64,128]{5,4,3,2,1,0:T(8,128)(2,1)}, u32[]{:S(2)}) copy-start(bf16[1,1,2,16,64,128]{5,4,3,2,1,0:T(8,128)(2,1)} %param.11) | copy-start | bytes 1572868
  0.6 1.3 %copy-start = (bf16[1,1,2,16,64,128]{5,4,3,2,1,0:T(8,128)(2,1)S(1)}, bf16[1,1,2,16,64,128]{5,4,3,2,1,0:T(8,128)(2,1)}, u32[]{:S(2)}) copy-start(bf16[1,1,2,16,64,128]{5,4,3,2,1,0:T(8,128)(2,1)} %param.6) | copy-start | bytes 1572868
  1.9 5.4 %copy-start.4 = (bf16[3,3,3,128]{3,2,1,0:T(4,128)(2,1)S(1)}, bf16[3,3,3,128]{3,2,1,0:T(4,128)(2,1)}, u32[]{:S(2)}) copy-start(bf16[3,3,3,128]{3,2,1,0:T(4,128)(2,1)} %param.7) | copy-start | bytes 20740
  1.9 5.5 %copy-start.5 = (bf16[3,3,3,128]{3,2,1,0:T(4,128)(2,1)S(1)}, bf16[3,3,3,128]{3,2,1,0:T(4,128)(2,1)}, u32[]{:S(2)}) copy-start(bf16[3,3,3,128]{3,2,1,0:T(4,128)(2,1)} %param.9) | copy-start | bytes 20740
  1.9 5.5 %copy-start.2 = (bf16[128,128]{1,0:T(8,128)(2,1)S(1)}, bf16[128,128]{1,0:T(8,128)(2,1)}, u32[]{:S(2)}) copy-start(bf16[128,128]{1,0:T(8,128)(2,1)} %p2.5) | copy-start | bytes 98308
  1.9 5.5 %copy-start.3 = (bf16[128,128]{1,0:T(8,128)(2,1)S(1)}, bf16[128,128]{1,0:T(8,128)(2,1)}, u32[]{:S(2)}) copy-start(bf16[128,128]{1,0:T(8,128)(2,1)} %p1.7) | copy-start | bytes 98308
  2.1 6.2 %collective-permute-start.1 = (bf16[2,1024,128]{2,1,0:T(8,128)(2,1)S(1)}, bf16[2,1024,128]{2,1,0:T(8,128)(2,1)S(1)}, u32[]{:S(2)}, u32[]{:S(2)}) collective-permute-start(bf16[2,1024,128]{2,1,0:T(8,128)(2,1)S(1)} %pad_maximum_fusion.1), channel_id=1, source_target_pairs={{0,4},{4,0},{1,5},{5,1},{2,6},{6,2},{3,7},{7,3},{8,12},{12,8},{9,1... | collective-permute-start | bytes 1572872 | tf_op jit(solution)/shard_map/ppermute | solution.py:319
  5.4 10.5 %collective-permute-start = (bf16[2,1024,128]{2,1,0:T(8,128)(2,1)S(1)}, bf16[2,1024,128]{2,1,0:T(8,128)(2,1)S(1)}, u32[]{:S(2)}, u32[]{:S(2)}) collective-permute-start(bf16[2,1024,128]{2,1,0:T(8,128)(2,1)S(1)} %pad_maximum_fusion), channel_id=1, source_target_pairs={{4,8},{12,16},{20,24},{28,32},{36,40},{44,48},{52,56},{60,64},{68,... | collective-permute-start | bytes 1572872 | tf_op jit(solution)/shard_map/ppermute | solution.py:325
  49.6 8.7 %collective-permute-start.2 = (bf16[1024,128]{1,0:T(8,128)(2,1)S(1)}, bf16[1024,128]{1,0:T(8,128)(2,1)S(1)}, u32[]{:S(2)}, u32[]{:S(2)}) collective-permute-start(bf16[1024,128]{1,0:T(8,128)(2,1)S(1)} %get-tuple-element.42.inner), channel_id=1, source_target_pairs={{0,4},{4,0},{1,5},{5,1},{2,6},{6,2},{3,7},{7,3},{8,12},{12,8},{9,1... | collective-permute-start | bytes 786440 | tf_op jit(solution)/shard_map/ppermute | solution.py:319
  51.2 7.7 %collective-permute-start.3 = (bf16[1024,128]{1,0:T(8,128)(2,1)S(1)}, bf16[1024,128]{1,0:T(8,128)(2,1)S(1)}, u32[]{:S(2)}, u32[]{:S(2)}) collective-permute-start(bf16[1024,128]{1,0:T(8,128)(2,1)S(1)} %get-tuple-element.43.outer), channel_id=1, source_target_pairs={{4,8},{12,16},{20,24},{28,32},{36,40},{44,48},{52,56},{60,64},{68,... | collective-permute-start | bytes 786440 | tf_op jit(solution)/shard_map/ppermute | solution.py:325
  53.2 12.9 %all-to-all-start.2 = ((f32[32,1,1280]{2,1,0:T(1,128)}), f32[32,1,1280]{2,1,0:T(1,128)S(1)}, u32[]{:S(2)}, u32[]{:S(2)}) async-start(f32[32,1,1280]{2,1,0:T(1,128)} %shard_map.104), calls=%async_computation.2 | async-start | bytes 327680 | tf_op jit(solution)/shard_map/all_to_all | solution.py:345

commit v8 on v6

--- a/solution.py
+++ b/solution.py
@@ -252,27 +252,32 @@
     )
 
 
-def last_kernel(parity, inner, outer, near, far, d1, p1, out, done, planes, local, low_side, high_side):
+def own_kernel(parity, inner, outer, d1, p1, out, planes, local):
+    core = parity[0]
+    depth_one = d1[...].astype(jnp.float32)
+    fill_local(local, backward_taps(depth_one, p1[...].astype(jnp.float32).T))
+    set_plane(planes, 2 - core, inner[...])
+    set_plane(planes, 1 + core, outer[...])
+    for start in range(0, CELLS, ROWS):
+        both = local_products(planes, local, start)
+        out[0, start : start + ROWS, :] = both[:, :CH]
+        out[1, start : start + ROWS, :] = both[:, CH:]
+
+
+def last_kernel(parity, own, near, far, d1, p1, out, done, planes, low_side, high_side):
     core = parity[0]
     depth_one = d1[...].astype(jnp.float32)
     taps = backward_taps(depth_one, p1[...].astype(jnp.float32).T)
-    fill_local(local, taps)
     fill_side(low_side, taps, False)
     fill_side(high_side, taps, True)
-    set_plane(planes, 2 - core, inner[...])
-    set_plane(planes, 1 + core, outer[...])
-    set_plane(planes, 3 - 3 * core, near[...])
-    set_plane(planes, 3 * core, far[...])
-    for half in range(0, CELLS, 2 * ROWS):
-        low = side_products(planes, 0, low_side, half)
-        high = side_products(planes, 3, high_side, half)
-        for at in range(0, 2 * ROWS, ROWS):
-            start = half + at
-            both = local_products(planes, local, start)
-            grad = both[:, :CH] + low[at : at + ROWS, :]
-            out[0, start : start + ROWS, :] = grad.astype(jnp.bfloat16)
-            grad = both[:, CH:] + high[at : at + ROWS, :]
-            out[1, start : start + ROWS, :] = grad.astype(jnp.bfloat16)
+    set_plane(planes, 1 - core, near[...])
+    set_plane(planes, core, far[...])
+    for start in range(0, CELLS, 2 * ROWS):
+        rows = slice(start, start + 2 * ROWS)
+        low = side_products(planes, 0, low_side, start)
+        out[0, rows, :] = (own[0, rows, :] + low).astype(jnp.bfloat16)
+        high = side_products(planes, 1, high_side, start)
+        out[1, rows, :] = (own[1, rows, :] + high).astype(jnp.bfloat16)
     done[...] = jnp.zeros((8, CH), jnp.float32)
 
 
@@ -398,12 +403,19 @@
     share = reduced_across(terms)
     outer_beside = with_other_chip(outer)
     inner_beside = with_other_core(inner)
+    (own,) = call(
+        own_kernel,
+        [slots, local_w],
+        [shape((2, CELLS, CH), f32)],
+        8_000_000_000,
+        parity, inner, outer, d1, point_one,
+    )
     grad, done = call(
         last_kernel,
-        [slots, local_w, side_w, side_w],
+        [pltpu.VMEM((2, PADDED, CH), bf16), side_w, side_w],
         [shape((2, CELLS, CH), bf16), shape((8, CH), f32)],
-        4_000_000_000,
-        parity, inner, outer, inner_beside, outer_beside, d1, point_one,
+        2_000_000_000,
+        parity, own, inner_beside, outer_beside, d1, point_one,
     )
     sums = gathered_across(reduced_around(share))
     depth, point = (shape((3, 3, 3, CH), f32), shape((CH, CH), f32))

time: 67.1 us -> 65.8 us (0.981)
  blocking collectives: 30.4 us -> 0 us
  starting transfers between devices: 12.6 us -> 27.5 us
  waiting for transfers between devices: 6.12 us -> 18.8 us
  Pallas kernels: 15.2 us -> 16.1 us
    all_to_all x2 -> x0, blocking collectives: 30.4 us -> none  [the longest x1 21.1 us: reduced_across(): return lax.all_to_all(tiles, ACROSS, 0, 0, tiled=True).sum(axis=0)]
    all_to_all x0 -> x2, starting transfers between devices: none -> 14.8 us  [the longest x1 9.75 us: reduced_across(): return lax.all_to_all(tiles, ACROSS, 0, 0, tiled=True).sum(axis=0)]
    all_to_all x0 -> x2, waiting for transfers between devices: none -> 11.3 us  [the longest x1 5.91 us: reduced_across(): return lax.all_to_all(tiles, ACROSS, 0, 0, tiled=True).sum(axis=0)]
    all_to_all x1, waiting for transfers between devices: 4.54 us -> 5.91 us  [gathered_across(): return lax.all_to_all(copies, ACROSS, 0, 0, tiled=True).reshape(TERMS, CH)]
    pallas_call x6 -> x7, Pallas kernels: 15.2 us -> 16.1 us  [call(): pl.pallas_call(kernel, out_shape=outs, in_specs=[smem if a.dtype == jnp.i...]
  transfers between devices with their start and end apart: 5 -> 7, of which waited for: 2 -> 4; matrix products, arithmetic and copies ran while one was open for 0% -> 1% of each run, Pallas kernels for 16% -> 17%
where the time goes in v8:
time: 65.8 us; the launch traced here: 65.4 us
  starting transfers between devices  27.5 us (42%)
  waiting for transfers between devices  18.8 us (29%)
  Pallas kernels  16.1 us (24%)
  local copies, waits for them, and re-layouts  1.93 us (3%)
  between operations  0.85 us (1%)
    pallas_call x7, Pallas kernels, call(): pl.pallas_call(kernel, out_shape=outs, in_specs=[smem if a.dtype == jnp.i...  16.1 us
    all_to_all x1, starting transfers between devices, reduced_across(): return lax.all_to_all(tiles, ACROSS, 0, 0, tiled=True).sum(axis=0)  9.75 us
    all_to_all x1, waiting for transfers between devices, reduced_across(): return lax.all_to_all(tiles, ACROSS, 0, 0, tiled=True).sum(axis=0)  5.91 us
    all_to_all x1, waiting for transfers between devices, gathered_across(): return lax.all_to_all(copies, ACROSS, 0, 0, tiled=True).reshape(TERMS, CH)  5.91 us
    all_to_all x1, starting transfers between devices, gathered_across(): return lax.all_to_all(copies, ACROSS, 0, 0, tiled=True).reshape(TERMS, CH)  5.48 us
    all_to_all x1, waiting for transfers between devices, reduced_around(): arrived = lax.all_to_all(copies, 'ring', 0, 0, tiled=True)  5.42 us
    all_to_all x1, starting transfers between devices, reduced_around(): arrived = lax.all_to_all(copies, 'ring', 0, 0, tiled=True)  5.03 us
    ppermute x2, starting transfers between devices, with_other_chip(): return lax.ppermute(v, SPACE, pairs + [(j, i) for i, j in pairs])  3.83 us
  transfers between devices with their start and end apart: 7, of which 4 were waited for; matrix products, arithmetic and copies ran while one was open for 1% of the time, Pallas kernels for 17%

profile of v8, /device:TPU:1, one launch (start us, length us, event | category | flops | bytes accessed | tf_op | source)
XLA Modules:
  0.0 65.4 jit_solution(7229568235100347900)
XLA Ops:
  0.6 0.0 copy-start.1
  0.6 0.0 copy-start
  0.7 1.2 %constant_dynamic-slice_fusion.2 = (bf16[1,1024,128]{2,1,0:T(8,128)(2,1)S(1)}, bf16[1,1024,128]{2,1,0:T(8,128)(2,1)S(1)}) fusion(bf16[2,1024,128]{2,1,0:T(8,128)(2,1)} %bitcast.11, s32[]{:T(128)S(6)} %select_n.8, bf16[2,1024,128]{2,1,0:T(8,128)(2,1)} %bitcast.7), kind=kLoop, calls=%fused_computation.4 | loop fusion | bytes 1048580 | tf_op jit(solution)/shard_map/dynamic_slice | solution.py:366
  1.8 0.1 pad_maximum_fusion
  1.9 0.0 copy-start.4
  1.9 0.0 copy-start.5
  1.9 0.0 copy-start.2
  1.9 0.0 copy-start.3
  1.9 0.0 copy-done.1
  2.0 0.0 copy-done
  2.0 0.1 pad_maximum_fusion.1
  2.1 3.3 %collective-permute-start = (bf16[2,1024,128]{2,1,0:T(8,128)(2,1)S(1)}, bf16[2,1024,128]{2,1,0:T(8,128)(2,1)S(1)}, u32[]{:S(2)}, u32[]{:S(2)}) collective-permute-start(bf16[2,1024,128]{2,1,0:T(8,128)(2,1)S(1)} %pad_maximum_fusion.1), channel_id=1, source_target_pairs={{0,4},{4,0},{1,5},{5,1},{2,6},{6,2},{3,7},{7,3},{8,12},{12,8},{9,1... | collective-permute-start | bytes 1572872 | tf_op jit(solution)/shard_map/ppermute | solution.py:324
  5.4 1.9 %collective-permute-start.1 = (bf16[2,1024,128]{2,1,0:T(8,128)(2,1)S(1)}, bf16[2,1024,128]{2,1,0:T(8,128)(2,1)S(1)}, u32[]{:S(2)}, u32[]{:S(2)}) collective-permute-start(bf16[2,1024,128]{2,1,0:T(8,128)(2,1)S(1)} %pad_maximum_fusion), channel_id=1, source_target_pairs={{4,8},{12,16},{20,24},{28,32},{36,40},{44,48},{52,56},{60,64},{68,... | collective-permute-start | bytes 1572872 | tf_op jit(solution)/shard_map/ppermute | solution.py:330
  7.3 0.0 copy-done.4
  7.3 0.0 copy-done.5
  7.4 0.0 copy-done.2
  7.4 0.0 copy-done.3
  7.4 0.9 %shard_map.101 = (bf16[768,768]{1,0:T(8,128)(2,1)S(1)}, bf16[768,768]{1,0:T(8,128)(2,1)S(1)}, bf16[512,768]{1,0:T(8,128)(2,1)S(1)}, bf16[512,768]{1,0:T(8,128)(2...) custom-call(s32[1]{0:T(128)} %bitcast.parity, bf16[27,128]{1,0:T(8,128)(2,1)S(1)} %reshape.40.d1, ...), custom_call_target="tpu_custom_call" | custom-call | flops 1000000000 | bytes 5584388 | tf_op jit(solution)/shard_map/pallas_call | solution.py:308
  8.3 0.0 collective-permute-done.near
  8.3 6.0 %shard_map.102 = (bf16[1024,128]{1,0:T(8,128)(2,1)S(1)}, f32[1024,128]{1,0:T(8,128)S(1)}, f32[1024,128]{1,0:T(8,128)S(1)}, f32[320,128]{1,0:T(8,128)S(1)}) custom-call(s32[1]{0:T(128)} %bitcast.parity, bf16[2,1024,128]{2,1,0:T(8,128)(2,1)S(1)} %bitcast.9, bf16[2,1024,128]{2,1,0:T(8,128)(2,1)S(1)} %bitcast.13, ...), custom_call_target="tpu_custom_call" | custom-call | flops 6000000000 | bytes 7058948 | tf_op jit(solution)/shard_map/pallas_call | solution.py:308
  14.3 1.6 %collective-permute-done.1.far = bf16[2,1024,128]{2,1,0:T(8,128)(2,1)S(1)} collective-permute-done((bf16[2,1024,128]{2,1,0:T(8,128)(2,1)S(1)}, bf16[2,1024,128]{2,1,0:T(8,128)(2,1)S(1)}, u32[]{:S(2)}, u32[]{:S(2)}) %collective-permute-start.1) | collective-permute-done | bytes 524320 | tf_op jit(solution)/shard_map/ppermute | solution.py:330
  15.9 4.3 %shard_map.103 = (bf16[1024,128]{1,0:T(8,128)(2,1)S(1)}, f32[320,128]{1,0:T(8,128)}) custom-call(s32[1]{0:T(128)} %bitcast.parity, bf16[2,1024,128]{2,1,0:T(8,128)(2,1)S(1)} %bitcast.10, bf16[2,1024,128]{2,1,0:T(8,128)(2,1)S(1)} %bitcast.14, bf16[2,1024,128]{2,1,0:T(8,128)(2,1)S(1)} %collective-permute-done.1.far, f32[1024,128]{1,0:T(8,128)S(1)} %get-tuple-element.32.pre, ...), custom_call_target="tpu_custom_call" | custom-call | flops 4000000000 | bytes 4863492 | tf_op jit(solution)/shard_map/pallas_call | solution.py:308
  20.2 9.8 %all-to-all-start = ((f32[32,1,1280]{2,1,0:T(1,128)}), f32[32,1,1280]{2,1,0:T(1,128)S(1)}, u32[]{:S(2)}, u32[]{:S(2)}) async-start(f32[32,1,1280]{2,1,0:T(1,128)} %bitcast.4), calls=%async_computation | async-start | bytes 327680 | tf_op jit(solution)/shard_map/all_to_all | solution.py:336
  29.9 1.9 %collective-permute-start.3 = (bf16[1024,128]{1,0:T(8,128)(2,1)S(1)}, bf16[1024,128]{1,0:T(8,128)(2,1)S(1)}, u32[]{:S(2)}, u32[]{:S(2)}) collective-permute-start(bf16[1024,128]{1,0:T(8,128)(2,1)S(1)} %get-tuple-element.37.outer), channel_id=1, source_target_pairs={{4,8},{12,16},{20,24},{28,32},{36,40},{44,48},{52,56},{60,64},{68,... | collective-permute-start | bytes 786440 | tf_op jit(solution)/shard_map/ppermute | solution.py:330
  31.8 0.1 collective-permute-start.2
  31.9 5.9 %all-to-all-done = f32[32,1,1280]{2,1,0:T(1,128)S(1)} async-done(((f32[32,1,1280]{2,1,0:T(1,128)}), f32[32,1,1280]{2,1,0:T(1,128)S(1)}, u32[]{:S(2)}, u32[]{:S(2)}) %all-to-all-start) | async-done | bytes 163872 | tf_op jit(solution)/shard_map/all_to_all | solution.py:336
  37.9 0.1 reduce_sum.9
  38.0 0.6 broadcast_in_dim.3
  38.6 5.0 %all-to-all-start.1 = ((f32[8,1,1280]{2,1,0:T(1,128)}), f32[8,1,1280]{2,1,0:T(1,128)S(1)}, u32[]{:S(2)}, u32[]{:S(2)}) async-start(f32[8,1,1280]{2,1,0:T(1,128)} %broadcast_in_dim.3), calls=%async_computation.1 | async-start | bytes 81920 | tf_op jit(solution)/shard_map/all_to_all | solution.py:341
  43.6 1.5 %shard_map.104.own = f32[2,1024,128]{2,1,0:T(8,128)S(1)} custom-call(s32[1]{0:T(128)} %bitcast.parity, bf16[1024,128]{1,0:T(8,128)(2,1)S(1)} %get-tuple-element.30.inner, bf16[1024,128]{1,0:T(8,128)(2,1)S(1)} %get-tuple-element.37.outer, bf16[27,128]{1,0:T(8,128)(2,1)S(1)} %reshape.40.d1, bf16[128,128]{1,0:T(8,128)(2,1)S(1)} %copy-done.3), custom_call_target="tpu_custom_call" | custom-call | flops 8000000000 | bytes 1612548 | tf_op jit(solution)/shard_map/pallas_call | solution.py:308
  45.2 5.4 %all-to-all-done.1.arrived = f32[8,1,1280]{2,1,0:T(1,128)S(1)} async-done(((f32[8,1,1280]{2,1,0:T(1,128)}), f32[8,1,1280]{2,1,0:T(1,128)S(1)}, u32[]{:S(2)}, u32[]{:S(2)}) %all-to-all-start.1) | async-done | bytes 40992 | tf_op jit(solution)/shard_map/all_to_all | solution.py:341
  50.6 0.7 %shard_map.106 = f32[32,1,1280]{2,1,0:T(1,128)} custom-call(f32[8,1,1280]{2,1,0:T(1,128)S(1)} %all-to-all-done.1.arrived), custom_call_target="tpu_custom_call" | custom-call | bytes 204800 | tf_op jit(solution)/shard_map/pallas_call | solution.py:308
  51.3 5.5 %all-to-all-start.2 = ((f32[32,1,1280]{2,1,0:T(1,128)}), f32[32,1,1280]{2,1,0:T(1,128)S(1)}, u32[]{:S(2)}, u32[]{:S(2)}) async-start(f32[32,1,1280]{2,1,0:T(1,128)} %shard_map.106), calls=%async_computation.2 | async-start | bytes 327680 | tf_op jit(solution)/shard_map/all_to_all | solution.py:350
  56.8 0.0 collective-permute-done.3.far
  56.8 0.0 collective-permute-done.2.near
  56.8 2.0 %shard_map.105 = (bf16[2,1024,128]{2,1,0:T(8,128)(2,1)}, f32[8,128]{1,0:T(8,128)S(1)}) custom-call(s32[1]{0:T(128)} %bitcast.parity, f32[2,1024,128]{2,1,0:T(8,128)S(1)} %shard_map.104.own, bf16[1024,128]{1,0:T(8,128)(2,1)S(1)} %collective-permute-done.2.near, bf16[1024,128]{1,0:T(8,128)(2,1)S(1)} %collective-permute-done.3.far, ...), custom_call_target="tpu_custom_call" | custom-call | flops 2000000000 | bytes 2140932 | tf_op jit(solution)/shard_map/pallas_call | solution.py:308
  58.8 5.9 %all-to-all-done.2 = f32[32,1,1280]{2,1,0:T(1,128)S(1)} async-done(((f32[32,1,1280]{2,1,0:T(1,128)}), f32[32,1,1280]{2,1,0:T(1,128)S(1)}, u32[]{:S(2)}, u32[]{:S(2)}) %all-to-all-start.2) | async-done | bytes 163872 | tf_op jit(solution)/shard_map/all_to_all | solution.py:350
  64.7 0.7 %shard_map.107 = (f32[3,3,3,128]{3,2,1,0:T(4,128)}, f32[128,128]{1,0:T(8,128)}, f32[3,3,3,128]{3,2,1,0:T(4,128)}, f32[128,128]{1,0:T(8,128)}) custom-call(f32[320,128]{1,0:T(8,128)S(1)} %bitcast.6, f32[8,128]{1,0:T(8,128)S(1)} %get-tuple-element.40.done), custom_call_target="tpu_custom_call" | custom-call | bytes 326656 | tf_op jit(solution)/shard_map/pallas_call | solution.py:308
  (4 shorter events, 0.1 us)
Async XLA Ops:
  0.6 1.3 %copy-start.1 = (bf16[1,1,2,16,64,128]{5,4,3,2,1,0:T(8,128)(2,1)S(1)}, bf16[1,1,2,16,64,128]{5,4,3,2,1,0:T(8,128)(2,1)}, u32[]{:S(2)}) copy-start(bf16[1,1,2,16,64,128]{5,4,3,2,1,0:T(8,128)(2,1)} %param.11) | copy-start | bytes 1572868
  0.6 1.3 %copy-start = (bf16[1,1,2,16,64,128]{5,4,3,2,1,0:T(8,128)(2,1)S(1)}, bf16[1,1,2,16,64,128]{5,4,3,2,1,0:T(8,128)(2,1)}, u32[]{:S(2)}) copy-start(bf16[1,1,2,16,64,128]{5,4,3,2,1,0:T(8,128)(2,1)} %param.6) | copy-start | bytes 1572868
  1.9 5.4 %copy-start.4 = (bf16[3,3,3,128]{3,2,1,0:T(4,128)(2,1)S(1)}, bf16[3,3,3,128]{3,2,1,0:T(4,128)(2,1)}, u32[]{:S(2)}) copy-start(bf16[3,3,3,128]{3,2,1,0:T(4,128)(2,1)} %param.7) | copy-start | bytes 20740
  1.9 5.5 %copy-start.5 = (bf16[3,3,3,128]{3,2,1,0:T(4,128)(2,1)S(1)}, bf16[3,3,3,128]{3,2,1,0:T(4,128)(2,1)}, u32[]{:S(2)}) copy-start(bf16[3,3,3,128]{3,2,1,0:T(4,128)(2,1)} %param.9) | copy-start | bytes 20740
  1.9 5.5 %copy-start.2 = (bf16[128,128]{1,0:T(8,128)(2,1)S(1)}, bf16[128,128]{1,0:T(8,128)(2,1)}, u32[]{:S(2)}) copy-start(bf16[128,128]{1,0:T(8,128)(2,1)} %p2.5) | copy-start | bytes 98308
  1.9 5.5 %copy-start.3 = (bf16[128,128]{1,0:T(8,128)(2,1)S(1)}, bf16[128,128]{1,0:T(8,128)(2,1)}, u32[]{:S(2)}) copy-start(bf16[128,128]{1,0:T(8,128)(2,1)} %p1.9) | copy-start | bytes 98308
  2.1 6.2 %collective-permute-start = (bf16[2,1024,128]{2,1,0:T(8,128)(2,1)S(1)}, bf16[2,1024,128]{2,1,0:T(8,128)(2,1)S(1)}, u32[]{:S(2)}, u32[]{:S(2)}) collective-permute-start(bf16[2,1024,128]{2,1,0:T(8,128)(2,1)S(1)} %pad_maximum_fusion.1), channel_id=1, source_target_pairs={{0,4},{4,0},{1,5},{5,1},{2,6},{6,2},{3,7},{7,3},{8,12},{12,8},{9,1... | collective-permute-start | bytes 1572872 | tf_op jit(solution)/shard_map/ppermute | solution.py:324
  5.4 10.5 %collective-permute-start.1 = (bf16[2,1024,128]{2,1,0:T(8,128)(2,1)S(1)}, bf16[2,1024,128]{2,1,0:T(8,128)(2,1)S(1)}, u32[]{:S(2)}, u32[]{:S(2)}) collective-permute-start(bf16[2,1024,128]{2,1,0:T(8,128)(2,1)S(1)} %pad_maximum_fusion), channel_id=1, source_target_pairs={{4,8},{12,16},{20,24},{28,32},{36,40},{44,48},{52,56},{60,64},{68,... | collective-permute-start | bytes 1572872 | tf_op jit(solution)/shard_map/ppermute | solution.py:330
  20.2 17.7 %all-to-all-start = ((f32[32,1,1280]{2,1,0:T(1,128)}), f32[32,1,1280]{2,1,0:T(1,128)S(1)}, u32[]{:S(2)}, u32[]{:S(2)}) async-start(f32[32,1,1280]{2,1,0:T(1,128)} %bitcast.4), calls=%async_computation | async-start | bytes 327680 | tf_op jit(solution)/shard_map/all_to_all | solution.py:336
  29.9 26.9 %collective-permute-start.3 = (bf16[1024,128]{1,0:T(8,128)(2,1)S(1)}, bf16[1024,128]{1,0:T(8,128)(2,1)S(1)}, u32[]{:S(2)}, u32[]{:S(2)}) collective-permute-start(bf16[1024,128]{1,0:T(8,128)(2,1)S(1)} %get-tuple-element.37.outer), channel_id=1, source_target_pairs={{4,8},{12,16},{20,24},{28,32},{36,40},{44,48},{52,56},{60,64},{68,... | collective-permute-start | bytes 786440 | tf_op jit(solution)/shard_map/ppermute | solution.py:330
  31.8 24.9 %collective-permute-start.2 = (bf16[1024,128]{1,0:T(8,128)(2,1)S(1)}, bf16[1024,128]{1,0:T(8,128)(2,1)S(1)}, u32[]{:S(2)}, u32[]{:S(2)}) collective-permute-start(bf16[1024,128]{1,0:T(8,128)(2,1)S(1)} %get-tuple-element.30.inner), channel_id=1, source_target_pairs={{0,4},{4,0},{1,5},{5,1},{2,6},{6,2},{3,7},{7,3},{8,12},{12,8},{9,1... | collective-permute-start | bytes 786440 | tf_op jit(solution)/shard_map/ppermute | solution.py:324
  38.6 12.0 %all-to-all-start.1 = ((f32[8,1,1280]{2,1,0:T(1,128)}), f32[8,1,1280]{2,1,0:T(1,128)S(1)}, u32[]{:S(2)}, u32[]{:S(2)}) async-start(f32[8,1,1280]{2,1,0:T(1,128)} %broadcast_in_dim.3), calls=%async_computation.1 | async-start | bytes 81920 | tf_op jit(solution)/shard_map/all_to_all | solution.py:341
  51.3 13.4 %all-to-all-start.2 = ((f32[32,1,1280]{2,1,0:T(1,128)}), f32[32,1,1280]{2,1,0:T(1,128)S(1)}, u32[]{:S(2)}, u32[]{:S(2)}) async-start(f32[32,1,1280]{2,1,0:T(1,128)} %shard_map.106), calls=%async_computation.2 | async-start | bytes 327680 | tf_op jit(solution)/shard_map/all_to_all | solution.py:350

commit v9 on v8

--- a/solution.py
+++ b/solution.py
@@ -403,12 +403,14 @@
     share = reduced_across(terms)
     outer_beside = with_other_chip(outer)
     inner_beside = with_other_core(inner)
+    copies = reduced_around(share)
+    copies, own_inner, own_outer = lax.optimization_barrier((copies, inner, outer))
     (own,) = call(
         own_kernel,
         [slots, local_w],
         [shape((2, CELLS, CH), f32)],
-        8_000_000_000,
-        parity, inner, outer, d1, point_one,
+        2_000_000_000,
+        parity, own_inner, own_outer, d1, point_one,
     )
     grad, done = call(
         last_kernel,
@@ -417,7 +419,7 @@
         2_000_000_000,
         parity, own, inner_beside, outer_beside, d1, point_one,
     )
-    sums = gathered_across(reduced_around(share))
+    sums = gathered_across(copies)
     depth, point = (shape((3, 3, 3, CH), f32), shape((CH, CH), f32))
     parts = call(parts_kernel, [], [depth, point, depth, point], 0, sums, done)
     return (grad.reshape(inputs.shape), *parts)

time: 65.8 us -> 65 us (0.988)
  blocking collectives: 0 us -> 11.8 us
  waiting for transfers between devices: 18.8 us -> 11.8 us
  starting transfers between devices: 27.5 us -> 22.5 us
    all_to_all x0 -> x1, blocking collectives: none -> 11.8 us  [reduced_around(): arrived = lax.all_to_all(copies, 'ring', 0, 0, tiled=True)]
    all_to_all x1 -> x0, waiting for transfers between devices: 5.42 us -> none  [reduced_around(): arrived = lax.all_to_all(copies, 'ring', 0, 0, tiled=True)]
    all_to_all x1 -> x0, starting transfers between devices: 5.03 us -> none  [reduced_around(): arrived = lax.all_to_all(copies, 'ring', 0, 0, tiled=True)]
    all_to_all x1, waiting for transfers between devices: 5.91 us -> 4.34 us  [gathered_across(): return lax.all_to_all(copies, ACROSS, 0, 0, tiled=True).reshape(TERMS, CH)]
  transfers between devices with their start and end apart: 7 -> 6, of which waited for: 4 -> 3; matrix products, arithmetic and copies ran while one was open for 1% -> 0% of each run, Pallas kernels for 17% -> 17%
where the time goes in v9:
time: 65 us; the launch traced here: 64.6 us
  starting transfers between devices  22.5 us (35%)
  Pallas kernels  16.1 us (25%)
  waiting for transfers between devices  11.8 us (18%)
  blocking collectives  11.8 us (18%)
  local copies, waits for them, and re-layouts  1.32 us (2%)
  between operations  0.85 us (1%)
    pallas_call x7, Pallas kernels, call(): pl.pallas_call(kernel, out_shape=outs, in_specs=[smem if a.dtype == jnp.i...  16.1 us
    all_to_all x1, blocking collectives, reduced_around(): arrived = lax.all_to_all(copies, 'ring', 0, 0, tiled=True)  11.8 us
    all_to_all x1, starting transfers between devices, reduced_across(): return lax.all_to_all(tiles, ACROSS, 0, 0, tiled=True).sum(axis=0)  9.75 us
    all_to_all x1, waiting for transfers between devices, reduced_across(): return lax.all_to_all(tiles, ACROSS, 0, 0, tiled=True).sum(axis=0)  5.91 us
    all_to_all x1, starting transfers between devices, gathered_across(): return lax.all_to_all(copies, ACROSS, 0, 0, tiled=True).reshape(TERMS, CH)  5.48 us
    all_to_all x1, waiting for transfers between devices, gathered_across(): return lax.all_to_all(copies, ACROSS, 0, 0, tiled=True).reshape(TERMS, CH)  4.34 us
    ppermute x2, starting transfers between devices, with_other_chip(): return lax.ppermute(v, SPACE, pairs + [(j, i) for i, j in pairs])  3.83 us
    ppermute x2, starting transfers between devices, with_other_core(): return lax.ppermute(v, 'core', [(0, 1), (1, 0)])  3.42 us
  transfers between devices with their start and end apart: 6, of which 3 were waited for; matrix products, arithmetic and copies ran while one was open for 0% of the time, Pallas kernels for 17%

profile of v9, /device:TPU:1, one launch (start us, length us, event | category | flops | bytes accessed | tf_op | source)
XLA Modules:
  0.0 64.6 jit_solution(17071232228970941149)
XLA Ops:
  0.6 0.0 copy-start.1
  0.6 0.0 copy-start
  0.7 1.2 %constant_dynamic-slice_fusion.2 = (bf16[1,1024,128]{2,1,0:T(8,128)(2,1)S(1)}, bf16[1,1024,128]{2,1,0:T(8,128)(2,1)S(1)}) fusion(bf16[2,1024,128]{2,1,0:T(8,128)(2,1)} %bitcast.11, s32[]{:T(128)S(6)} %select_n.8, bf16[2,1024,128]{2,1,0:T(8,128)(2,1)} %bitcast.7), kind=kLoop, calls=%fused_computation.4 | loop fusion | bytes 1048580 | tf_op jit(solution)/shard_map/dynamic_slice | solution.py:366
  1.8 0.1 pad_maximum_fusion
  1.9 0.0 copy-start.4
  1.9 0.0 copy-start.5
  1.9 0.0 copy-start.2
  1.9 0.0 copy-start.3
  1.9 0.0 copy-done.1
  2.0 0.0 copy-done
  2.0 0.1 pad_maximum_fusion.1
  2.1 3.3 %collective-permute-start.1 = (bf16[2,1024,128]{2,1,0:T(8,128)(2,1)S(1)}, bf16[2,1024,128]{2,1,0:T(8,128)(2,1)S(1)}, u32[]{:S(2)}, u32[]{:S(2)}) collective-permute-start(bf16[2,1024,128]{2,1,0:T(8,128)(2,1)S(1)} %pad_maximum_fusion.1), channel_id=1, source_target_pairs={{0,4},{4,0},{1,5},{5,1},{2,6},{6,2},{3,7},{7,3},{8,12},{12,8},{9,1... | collective-permute-start | bytes 1572872 | tf_op jit(solution)/shard_map/ppermute | solution.py:324
  5.4 1.9 %collective-permute-start = (bf16[2,1024,128]{2,1,0:T(8,128)(2,1)S(1)}, bf16[2,1024,128]{2,1,0:T(8,128)(2,1)S(1)}, u32[]{:S(2)}, u32[]{:S(2)}) collective-permute-start(bf16[2,1024,128]{2,1,0:T(8,128)(2,1)S(1)} %pad_maximum_fusion), channel_id=1, source_target_pairs={{4,8},{12,16},{20,24},{28,32},{36,40},{44,48},{52,56},{60,64},{68,... | collective-permute-start | bytes 1572872 | tf_op jit(solution)/shard_map/ppermute | solution.py:330
  7.3 0.0 copy-done.4
  7.3 0.0 copy-done.5
  7.4 0.0 copy-done.2
  7.4 0.0 copy-done.3
  7.4 0.9 %shard_map.101 = (bf16[768,768]{1,0:T(8,128)(2,1)S(1)}, bf16[768,768]{1,0:T(8,128)(2,1)S(1)}, bf16[512,768]{1,0:T(8,128)(2,1)S(1)}, bf16[512,768]{1,0:T(8,128)(2...) custom-call(s32[1]{0:T(128)} %bitcast.parity, bf16[27,128]{1,0:T(8,128)(2,1)S(1)} %reshape.40.d1, ...), custom_call_target="tpu_custom_call" | custom-call | flops 1000000000 | bytes 5584388 | tf_op jit(solution)/shard_map/pallas_call | solution.py:308
  8.3 0.0 collective-permute-done.1.near
  8.3 6.0 %shard_map.102 = (bf16[1024,128]{1,0:T(8,128)(2,1)S(1)}, f32[1024,128]{1,0:T(8,128)S(1)}, f32[1024,128]{1,0:T(8,128)S(1)}, f32[320,128]{1,0:T(8,128)S(1)}) custom-call(s32[1]{0:T(128)} %bitcast.parity, bf16[2,1024,128]{2,1,0:T(8,128)(2,1)S(1)} %bitcast.9, bf16[2,1024,128]{2,1,0:T(8,128)(2,1)S(1)} %bitcast.13, ...), custom_call_target="tpu_custom_call" | custom-call | flops 6000000000 | bytes 7058948 | tf_op jit(solution)/shard_map/pallas_call | solution.py:308
  14.3 1.6 %collective-permute-done.far = bf16[2,1024,128]{2,1,0:T(8,128)(2,1)S(1)} collective-permute-done((bf16[2,1024,128]{2,1,0:T(8,128)(2,1)S(1)}, bf16[2,1024,128]{2,1,0:T(8,128)(2,1)S(1)}, u32[]{:S(2)}, u32[]{:S(2)}) %collective-permute-start) | collective-permute-done | bytes 524320 | tf_op jit(solution)/shard_map/ppermute | solution.py:330
  15.9 4.3 %shard_map.103 = (bf16[1024,128]{1,0:T(8,128)(2,1)S(1)}, f32[320,128]{1,0:T(8,128)}) custom-call(s32[1]{0:T(128)} %bitcast.parity, bf16[2,1024,128]{2,1,0:T(8,128)(2,1)S(1)} %bitcast.10, bf16[2,1024,128]{2,1,0:T(8,128)(2,1)S(1)} %bitcast.14, bf16[2,1024,128]{2,1,0:T(8,128)(2,1)S(1)} %collective-permute-done.far, f32[1024,128]{1,0:T(8,128)S(1)} %get-tuple-element.34.pre, ...), custom_call_target="tpu_custom_call" | custom-call | flops 4000000000 | bytes 4863492 | tf_op jit(solution)/shard_map/pallas_call | solution.py:308
  20.2 9.8 %all-to-all-start = ((f32[32,1,1280]{2,1,0:T(1,128)}), f32[32,1,1280]{2,1,0:T(1,128)S(1)}, u32[]{:S(2)}, u32[]{:S(2)}) async-start(f32[32,1,1280]{2,1,0:T(1,128)} %bitcast.3), calls=%async_computation | async-start | bytes 327680 | tf_op jit(solution)/shard_map/all_to_all | solution.py:336
  29.9 1.9 %collective-permute-start.3 = (bf16[1024,128]{1,0:T(8,128)(2,1)S(1)}, bf16[1024,128]{1,0:T(8,128)(2,1)S(1)}, u32[]{:S(2)}, u32[]{:S(2)}) collective-permute-start(bf16[1024,128]{1,0:T(8,128)(2,1)S(1)} %get-tuple-element.43.outer), channel_id=1, source_target_pairs={{4,8},{12,16},{20,24},{28,32},{36,40},{44,48},{52,56},{60,64},{68,... | collective-permute-start | bytes 786440 | tf_op jit(solution)/shard_map/ppermute | solution.py:330
  31.8 0.1 collective-permute-start.2
  31.9 5.9 %all-to-all-done = f32[32,1,1280]{2,1,0:T(1,128)S(1)} async-done(((f32[32,1,1280]{2,1,0:T(1,128)}), f32[32,1,1280]{2,1,0:T(1,128)S(1)}, u32[]{:S(2)}, u32[]{:S(2)}) %all-to-all-start) | async-done | bytes 163872 | tf_op jit(solution)/shard_map/all_to_all | solution.py:336
  37.9 0.1 reduce_sum.9
  38.0 11.8 %all_to_all.15.arrived = f32[8,1,1280]{2,1,0:T(1,128)S(1)} all-to-all(f32[8,1,1280]{2,1,0:T(1,128)S(1)} %broadcast_in_dim.3), channel_id=1, replica_groups=mesh['outer'=4,'ring'=8,'core'=2,'dp'=4] {'ring'}, dimensions={0} | all-to-all | bytes 81920 | tf_op jit(solution)/shard_map/all_to_all | solution.py:341
  49.8 0.7 %shard_map.104 = f32[32,1,1280]{2,1,0:T(1,128)} custom-call(f32[8,1,1280]{2,1,0:T(1,128)S(1)} %all_to_all.15.arrived), custom_call_target="tpu_custom_call" | custom-call | bytes 204800 | tf_op jit(solution)/shard_map/pallas_call | solution.py:308
  50.5 5.5 %all-to-all-start.2 = ((f32[32,1,1280]{2,1,0:T(1,128)}), f32[32,1,1280]{2,1,0:T(1,128)S(1)}, u32[]{:S(2)}, u32[]{:S(2)}) async-start(f32[32,1,1280]{2,1,0:T(1,128)} %shard_map.104), calls=%async_computation.2 | async-start | bytes 327680 | tf_op jit(solution)/shard_map/all_to_all | solution.py:350
  56.0 1.5 %shard_map.105.own = f32[2,1024,128]{2,1,0:T(8,128)S(1)} custom-call(s32[1]{0:T(128)} %bitcast.parity, bf16[1024,128]{1,0:T(8,128)(2,1)S(1)} %get-tuple-element.42.inner, bf16[1024,128]{1,0:T(8,128)(2,1)S(1)} %get-tuple-element.43.outer, bf16[27,128]{1,0:T(8,128)(2,1)S(1)} %reshape.40.d1, bf16[128,128]{1,0:T(8,128)(2,1)S(1)} %copy-done.3), custom_call_target="tpu_custom_call" | custom-call | flops 2000000000 | bytes 1612548 | tf_op jit(solution)/shard_map/pallas_call | solution.py:308
  57.5 0.0 collective-permute-done.3.far
  57.5 0.0 collective-permute-done.2.near
  57.5 2.0 %shard_map.106 = (bf16[2,1024,128]{2,1,0:T(8,128)(2,1)}, f32[8,128]{1,0:T(8,128)S(1)}) custom-call(s32[1]{0:T(128)} %bitcast.parity, f32[2,1024,128]{2,1,0:T(8,128)S(1)} %shard_map.105.own, bf16[1024,128]{1,0:T(8,128)(2,1)S(1)} %collective-permute-done.2.near, bf16[1024,128]{1,0:T(8,128)(2,1)S(1)} %collective-permute-done.3.far, ...), custom_call_target="tpu_custom_call" | custom-call | flops 2000000000 | bytes 2140932 | tf_op jit(solution)/shard_map/pallas_call | solution.py:308
  59.6 4.3 %all-to-all-done.2 = f32[32,1,1280]{2,1,0:T(1,128)S(1)} async-done(((f32[32,1,1280]{2,1,0:T(1,128)}), f32[32,1,1280]{2,1,0:T(1,128)S(1)}, u32[]{:S(2)}, u32[]{:S(2)}) %all-to-all-start.2) | async-done | bytes 163872 | tf_op jit(solution)/shard_map/all_to_all | solution.py:350
  63.9 0.7 %shard_map.107 = (f32[3,3,3,128]{3,2,1,0:T(4,128)}, f32[128,128]{1,0:T(8,128)}, f32[3,3,3,128]{3,2,1,0:T(4,128)}, f32[128,128]{1,0:T(8,128)}) custom-call(f32[320,128]{1,0:T(8,128)S(1)} %bitcast.6, f32[8,128]{1,0:T(8,128)S(1)} %get-tuple-element.46.done), custom_call_target="tpu_custom_call" | custom-call | bytes 326656 | tf_op jit(solution)/shard_map/pallas_call | solution.py:308
  (5 shorter events, 0.1 us)
Async XLA Ops:
  0.6 1.3 %copy-start.1 = (bf16[1,1,2,16,64,128]{5,4,3,2,1,0:T(8,128)(2,1)S(1)}, bf16[1,1,2,16,64,128]{5,4,3,2,1,0:T(8,128)(2,1)}, u32[]{:S(2)}) copy-start(bf16[1,1,2,16,64,128]{5,4,3,2,1,0:T(8,128)(2,1)} %param.11) | copy-start | bytes 1572868
  0.6 1.3 %copy-start = (bf16[1,1,2,16,64,128]{5,4,3,2,1,0:T(8,128)(2,1)S(1)}, bf16[1,1,2,16,64,128]{5,4,3,2,1,0:T(8,128)(2,1)}, u32[]{:S(2)}) copy-start(bf16[1,1,2,16,64,128]{5,4,3,2,1,0:T(8,128)(2,1)} %param.6) | copy-start | bytes 1572868
  1.9 5.4 %copy-start.4 = (bf16[3,3,3,128]{3,2,1,0:T(4,128)(2,1)S(1)}, bf16[3,3,3,128]{3,2,1,0:T(4,128)(2,1)}, u32[]{:S(2)}) copy-start(bf16[3,3,3,128]{3,2,1,0:T(4,128)(2,1)} %param.7) | copy-start | bytes 20740
  1.9 5.5 %copy-start.5 = (bf16[3,3,3,128]{3,2,1,0:T(4,128)(2,1)S(1)}, bf16[3,3,3,128]{3,2,1,0:T(4,128)(2,1)}, u32[]{:S(2)}) copy-start(bf16[3,3,3,128]{3,2,1,0:T(4,128)(2,1)} %param.9) | copy-start | bytes 20740
  1.9 5.5 %copy-start.2 = (bf16[128,128]{1,0:T(8,128)(2,1)S(1)}, bf16[128,128]{1,0:T(8,128)(2,1)}, u32[]{:S(2)}) copy-start(bf16[128,128]{1,0:T(8,128)(2,1)} %p2.5) | copy-start | bytes 98308
  1.9 5.5 %copy-start.3 = (bf16[128,128]{1,0:T(8,128)(2,1)S(1)}, bf16[128,128]{1,0:T(8,128)(2,1)}, u32[]{:S(2)}) copy-start(bf16[128,128]{1,0:T(8,128)(2,1)} %p1.9) | copy-start | bytes 98308
  2.1 6.2 %collective-permute-start.1 = (bf16[2,1024,128]{2,1,0:T(8,128)(2,1)S(1)}, bf16[2,1024,128]{2,1,0:T(8,128)(2,1)S(1)}, u32[]{:S(2)}, u32[]{:S(2)}) collective-permute-start(bf16[2,1024,128]{2,1,0:T(8,128)(2,1)S(1)} %pad_maximum_fusion.1), channel_id=1, source_target_pairs={{0,4},{4,0},{1,5},{5,1},{2,6},{6,2},{3,7},{7,3},{8,12},{12,8},{9,1... | collective-permute-start | bytes 1572872 | tf_op jit(solution)/shard_map/ppermute | solution.py:324
  5.4 10.5 %collective-permute-start = (bf16[2,1024,128]{2,1,0:T(8,128)(2,1)S(1)}, bf16[2,1024,128]{2,1,0:T(8,128)(2,1)S(1)}, u32[]{:S(2)}, u32[]{:S(2)}) collective-permute-start(bf16[2,1024,128]{2,1,0:T(8,128)(2,1)S(1)} %pad_maximum_fusion), channel_id=1, source_target_pairs={{4,8},{12,16},{20,24},{28,32},{36,40},{44,48},{52,56},{60,64},{68,... | collective-permute-start | bytes 1572872 | tf_op jit(solution)/shard_map/ppermute | solution.py:330
  20.2 17.7 %all-to-all-start = ((f32[32,1,1280]{2,1,0:T(1,128)}), f32[32,1,1280]{2,1,0:T(1,128)S(1)}, u32[]{:S(2)}, u32[]{:S(2)}) async-start(f32[32,1,1280]{2,1,0:T(1,128)} %bitcast.3), calls=%async_computation | async-start | bytes 327680 | tf_op jit(solution)/shard_map/all_to_all | solution.py:336
  29.9 27.6 %collective-permute-start.3 = (bf16[1024,128]{1,0:T(8,128)(2,1)S(1)}, bf16[1024,128]{1,0:T(8,128)(2,1)S(1)}, u32[]{:S(2)}, u32[]{:S(2)}) collective-permute-start(bf16[1024,128]{1,0:T(8,128)(2,1)S(1)} %get-tuple-element.43.outer), channel_id=1, source_target_pairs={{4,8},{12,16},{20,24},{28,32},{36,40},{44,48},{52,56},{60,64},{68,... | collective-permute-start | bytes 786440 | tf_op jit(solution)/shard_map/ppermute | solution.py:330
  31.8 25.7 %collective-permute-start.2 = (bf16[1024,128]{1,0:T(8,128)(2,1)S(1)}, bf16[1024,128]{1,0:T(8,128)(2,1)S(1)}, u32[]{:S(2)}, u32[]{:S(2)}) collective-permute-start(bf16[1024,128]{1,0:T(8,128)(2,1)S(1)} %get-tuple-element.42.inner), channel_id=1, source_target_pairs={{0,4},{4,0},{1,5},{5,1},{2,6},{6,2},{3,7},{7,3},{8,12},{12,8},{9,1... | collective-permute-start | bytes 786440 | tf_op jit(solution)/shard_map/ppermute | solution.py:324
  50.5 13.4 %all-to-all-start.2 = ((f32[32,1,1280]{2,1,0:T(1,128)}), f32[32,1,1280]{2,1,0:T(1,128)S(1)}, u32[]{:S(2)}, u32[]{:S(2)}) async-start(f32[32,1,1280]{2,1,0:T(1,128)} %shard_map.104), calls=%async_computation.2 | async-start | bytes 327680 | tf_op jit(solution)/shard_map/all_to_all | solution.py:350

commit v10 on v9

--- a/solution.py
+++ b/solution.py
@@ -409,7 +409,7 @@
         own_kernel,
         [slots, local_w],
         [shape((2, CELLS, CH), f32)],
-        2_000_000_000,
+        8_000_000_000,
         parity, own_inner, own_outer, d1, point_one,
     )
     grad, done = call(

time: 65 us -> 65 us (level)
  blocking collectives: 11.8 us -> 17.5 us
  waiting for transfers between devices: 11.8 us -> 8.82 us
  starting transfers between devices: 22.5 us -> 19.9 us
  Pallas kernels: 16.1 us -> 15.4 us
    all_to_all x1, blocking collectives: 11.8 us -> 17.5 us  [reduced_across(): return lax.all_to_all(tiles, ACROSS, 0, 0, tiled=True).sum(axis=0)]
    all_to_all x1, starting transfers between devices: 9.75 us -> 5.03 us  [reduced_around(): arrived = lax.all_to_all(copies, 'ring', 0, 0, tiled=True)]
    all_to_all x1, waiting for transfers between devices: 5.91 us -> 2.91 us  [reduced_around(): arrived = lax.all_to_all(copies, 'ring', 0, 0, tiled=True)]
    ppermute x2, starting transfers between devices: 3.83 us -> 5.86 us  [with_other_chip(): return lax.ppermute(v, SPACE, pairs + [(j, i) for i, j in pairs])]
    pallas_call x7, Pallas kernels: 16.1 us -> 15.4 us  [call(): pl.pallas_call(kernel, out_shape=outs, in_specs=[smem if a.dtype == jnp.i...]
where the time goes in v10:
time: 65 us; the launch traced here: 64.6 us
  starting transfers between devices  19.9 us (31%)
  blocking collectives  17.5 us (27%)
  Pallas kernels  15.4 us (24%)
  waiting for transfers between devices  8.82 us (14%)
  local copies, waits for them, and re-layouts  1.93 us (3%)
  between operations  0.84 us (1%)
    all_to_all x1, blocking collectives, reduced_across(): return lax.all_to_all(tiles, ACROSS, 0, 0, tiled=True).sum(axis=0)  17.5 us
    pallas_call x7, Pallas kernels, call(): pl.pallas_call(kernel, out_shape=outs, in_specs=[smem if a.dtype == jnp.i...  15.4 us
    ppermute x2, starting transfers between devices, with_other_chip(): return lax.ppermute(v, SPACE, pairs + [(j, i) for i, j in pairs])  5.86 us
    all_to_all x1, starting transfers between devices, gathered_across(): return lax.all_to_all(copies, ACROSS, 0, 0, tiled=True).reshape(TERMS, CH)  5.58 us
    all_to_all x1, starting transfers between devices, reduced_around(): arrived = lax.all_to_all(copies, 'ring', 0, 0, tiled=True)  5.03 us
    all_to_all x1, waiting for transfers between devices, gathered_across(): return lax.all_to_all(copies, ACROSS, 0, 0, tiled=True).reshape(TERMS, CH)  4.34 us
    ppermute x2, starting transfers between devices, with_other_core(): return lax.ppermute(v, 'core', [(0, 1), (1, 0)])  3.42 us
    all_to_all x1, waiting for transfers between devices, reduced_around(): arrived = lax.all_to_all(copies, 'ring', 0, 0, tiled=True)  2.91 us
  transfers between devices with their start and end apart: 6, of which 3 were waited for; matrix products, arithmetic and copies ran while one was open for 0% of the time, Pallas kernels for 17%

profile of v10, /device:TPU:1, one launch (start us, length us, event | category | flops | bytes accessed | tf_op | source)
XLA Modules:
  0.0 64.6 jit_solution(4365201663942545012)
XLA Ops:
  0.6 0.0 copy-start.1
  0.6 0.0 copy-start
  0.7 1.2 %constant_dynamic-slice_fusion.2 = (bf16[1,1024,128]{2,1,0:T(8,128)(2,1)S(1)}, bf16[1,1024,128]{2,1,0:T(8,128)(2,1)S(1)}) fusion(bf16[2,1024,128]{2,1,0:T(8,128)(2,1)} %bitcast.11, s32[]{:T(128)S(6)} %select_n.8, bf16[2,1024,128]{2,1,0:T(8,128)(2,1)} %bitcast.7), kind=kLoop, calls=%fused_computation.4 | loop fusion | bytes 1048580 | tf_op jit(solution)/shard_map/dynamic_slice | solution.py:366
  1.8 0.1 pad_maximum_fusion
  1.9 0.0 copy-start.4
  1.9 0.0 copy-start.5
  1.9 0.0 copy-start.2
  1.9 0.0 copy-start.3
  1.9 0.0 copy-done.1
  2.0 0.0 copy-done
  2.0 0.1 pad_maximum_fusion.1
  2.1 3.3 %collective-permute-start.1 = (bf16[2,1024,128]{2,1,0:T(8,128)(2,1)S(1)}, bf16[2,1024,128]{2,1,0:T(8,128)(2,1)S(1)}, u32[]{:S(2)}, u32[]{:S(2)}) collective-permute-start(bf16[2,1024,128]{2,1,0:T(8,128)(2,1)S(1)} %pad_maximum_fusion.1), channel_id=1, source_target_pairs={{0,4},{4,0},{1,5},{5,1},{2,6},{6,2},{3,7},{7,3},{8,12},{12,8},{9,1... | collective-permute-start | bytes 1572872 | tf_op jit(solution)/shard_map/ppermute | solution.py:324
  5.4 1.9 %collective-permute-start = (bf16[2,1024,128]{2,1,0:T(8,128)(2,1)S(1)}, bf16[2,1024,128]{2,1,0:T(8,128)(2,1)S(1)}, u32[]{:S(2)}, u32[]{:S(2)}) collective-permute-start(bf16[2,1024,128]{2,1,0:T(8,128)(2,1)S(1)} %pad_maximum_fusion), channel_id=1, source_target_pairs={{4,8},{12,16},{20,24},{28,32},{36,40},{44,48},{52,56},{60,64},{68,... | collective-permute-start | bytes 1572872 | tf_op jit(solution)/shard_map/ppermute | solution.py:330
  7.3 0.0 copy-done.4
  7.3 0.0 copy-done.5
  7.4 0.0 copy-done.2
  7.4 0.0 copy-done.3
  7.4 0.9 %shard_map.101 = (bf16[768,768]{1,0:T(8,128)(2,1)S(1)}, bf16[768,768]{1,0:T(8,128)(2,1)S(1)}, bf16[512,768]{1,0:T(8,128)(2,1)S(1)}, bf16[512,768]{1,0:T(8,128)(2...) custom-call(s32[1]{0:T(128)} %bitcast.parity, bf16[27,128]{1,0:T(8,128)(2,1)S(1)} %reshape.40.d1, ...), custom_call_target="tpu_custom_call" | custom-call | flops 1000000000 | bytes 5584388 | tf_op jit(solution)/shard_map/pallas_call | solution.py:308
  8.3 0.0 collective-permute-done.1.near
  8.3 6.0 %shard_map.102 = (bf16[1024,128]{1,0:T(8,128)(2,1)S(1)}, f32[1024,128]{1,0:T(8,128)S(1)}, f32[1024,128]{1,0:T(8,128)S(1)}, f32[320,128]{1,0:T(8,128)S(1)}) custom-call(s32[1]{0:T(128)} %bitcast.parity, bf16[2,1024,128]{2,1,0:T(8,128)(2,1)S(1)} %bitcast.9, bf16[2,1024,128]{2,1,0:T(8,128)(2,1)S(1)} %bitcast.13, ...), custom_call_target="tpu_custom_call" | custom-call | flops 6000000000 | bytes 7058948 | tf_op jit(solution)/shard_map/pallas_call | solution.py:308
  14.3 1.6 %collective-permute-done.far = bf16[2,1024,128]{2,1,0:T(8,128)(2,1)S(1)} collective-permute-done((bf16[2,1024,128]{2,1,0:T(8,128)(2,1)S(1)}, bf16[2,1024,128]{2,1,0:T(8,128)(2,1)S(1)}, u32[]{:S(2)}, u32[]{:S(2)}) %collective-permute-start) | collective-permute-done | bytes 524320 | tf_op jit(solution)/shard_map/ppermute | solution.py:330
  15.9 3.6 %shard_map.103 = (bf16[1024,128]{1,0:T(8,128)(2,1)S(1)}, f32[320,128]{1,0:T(8,128)S(1)}) custom-call(s32[1]{0:T(128)} %bitcast.parity, bf16[2,1024,128]{2,1,0:T(8,128)(2,1)S(1)} %bitcast.10, bf16[2,1024,128]{2,1,0:T(8,128)(2,1)S(1)} %bitcast.14, bf16[2,1024,128]{2,1,0:T(8,128)(2,1)S(1)} %collective-permute-done.far, f32[1024,128]{1,0:T(8,128)S(1)} %get-tuple-element.34.pre, ...), custom_call_target="tpu_custom_call" | custom-call | flops 4000000000 | bytes 4863492 | tf_op jit(solution)/shard_map/pallas_call | solution.py:308
  19.5 17.5 %all_to_all.15 = f32[32,1,1280]{2,1,0:T(1,128)S(1)} all-to-all(f32[32,1,1280]{2,1,0:T(1,128)S(1)} %bitcast.15), channel_id=1, replica_groups=mesh['outer'=4,'ring'=8,'core'=2,'dp'=4] {'outer','core','dp'}, dimensions={0} | all-to-all | bytes 327680 | tf_op jit(solution)/shard_map/all_to_all | solution.py:336
  37.0 0.1 reduce_sum.9
  37.1 0.6 broadcast_in_dim.3
  37.7 5.0 %all-to-all-start.1 = ((f32[8,1,1280]{2,1,0:T(1,128)}), f32[8,1,1280]{2,1,0:T(1,128)S(1)}, u32[]{:S(2)}, u32[]{:S(2)}) async-start(f32[8,1,1280]{2,1,0:T(1,128)} %broadcast_in_dim.3), calls=%async_computation.1 | async-start | bytes 81920 | tf_op jit(solution)/shard_map/all_to_all | solution.py:341
  42.8 4.0 %collective-permute-start.3 = (bf16[1024,128]{1,0:T(8,128)(2,1)S(1)}, bf16[1024,128]{1,0:T(8,128)(2,1)S(1)}, u32[]{:S(2)}, u32[]{:S(2)}) collective-permute-start(bf16[1024,128]{1,0:T(8,128)(2,1)S(1)} %get-tuple-element.43.outer), channel_id=1, source_target_pairs={{4,8},{12,16},{20,24},{28,32},{36,40},{44,48},{52,56},{60,64},{68,... | collective-permute-start | bytes 786440 | tf_op jit(solution)/shard_map/ppermute | solution.py:330
  46.7 0.1 collective-permute-start.2
  46.8 2.9 %all-to-all-done.1.arrived = f32[8,1,1280]{2,1,0:T(1,128)S(1)} async-done(((f32[8,1,1280]{2,1,0:T(1,128)}), f32[8,1,1280]{2,1,0:T(1,128)S(1)}, u32[]{:S(2)}, u32[]{:S(2)}) %all-to-all-start.1) | async-done | bytes 40992 | tf_op jit(solution)/shard_map/all_to_all | solution.py:341
  49.7 0.7 %shard_map.104 = f32[32,1,1280]{2,1,0:T(1,128)} custom-call(f32[8,1,1280]{2,1,0:T(1,128)S(1)} %all-to-all-done.1.arrived), custom_call_target="tpu_custom_call" | custom-call | bytes 204800 | tf_op jit(solution)/shard_map/pallas_call | solution.py:308
  50.4 5.6 %all-to-all-start.2 = ((f32[32,1,1280]{2,1,0:T(1,128)}), f32[32,1,1280]{2,1,0:T(1,128)S(1)}, u32[]{:S(2)}, u32[]{:S(2)}) async-start(f32[32,1,1280]{2,1,0:T(1,128)} %shard_map.104), calls=%async_computation.2 | async-start | bytes 327680 | tf_op jit(solution)/shard_map/all_to_all | solution.py:350
  56.0 1.5 %shard_map.105.own = f32[2,1024,128]{2,1,0:T(8,128)S(1)} custom-call(s32[1]{0:T(128)} %bitcast.parity, bf16[1024,128]{1,0:T(8,128)(2,1)S(1)} %get-tuple-element.42.inner, bf16[1024,128]{1,0:T(8,128)(2,1)S(1)} %get-tuple-element.43.outer, bf16[27,128]{1,0:T(8,128)(2,1)S(1)} %reshape.40.d1, bf16[128,128]{1,0:T(8,128)(2,1)S(1)} %copy-done.3), custom_call_target="tpu_custom_call" | custom-call | flops 8000000000 | bytes 1612548 | tf_op jit(solution)/shard_map/pallas_call | solution.py:308
  57.6 0.0 collective-permute-done.3.far
  57.6 0.0 collective-permute-done.2.near
  57.6 2.0 %shard_map.106 = (bf16[2,1024,128]{2,1,0:T(8,128)(2,1)}, f32[8,128]{1,0:T(8,128)S(1)}) custom-call(s32[1]{0:T(128)} %bitcast.parity, f32[2,1024,128]{2,1,0:T(8,128)S(1)} %shard_map.105.own, bf16[1024,128]{1,0:T(8,128)(2,1)S(1)} %collective-permute-done.2.near, bf16[1024,128]{1,0:T(8,128)(2,1)S(1)} %collective-permute-done.3.far, ...), custom_call_target="tpu_custom_call" | custom-call | flops 2000000000 | bytes 2140932 | tf_op jit(solution)/shard_map/pallas_call | solution.py:308
  59.6 4.3 %all-to-all-done.2 = f32[32,1,1280]{2,1,0:T(1,128)S(1)} async-done(((f32[32,1,1280]{2,1,0:T(1,128)}), f32[32,1,1280]{2,1,0:T(1,128)S(1)}, u32[]{:S(2)}, u32[]{:S(2)}) %all-to-all-start.2) | async-done | bytes 163872 | tf_op jit(solution)/shard_map/all_to_all | solution.py:350
  63.9 0.7 %shard_map.107 = (f32[3,3,3,128]{3,2,1,0:T(4,128)}, f32[128,128]{1,0:T(8,128)}, f32[3,3,3,128]{3,2,1,0:T(4,128)}, f32[128,128]{1,0:T(8,128)}) custom-call(f32[320,128]{1,0:T(8,128)S(1)} %bitcast.6, f32[8,128]{1,0:T(8,128)S(1)} %get-tuple-element.46.done), custom_call_target="tpu_custom_call" | custom-call | bytes 326656 | tf_op jit(solution)/shard_map/pallas_call | solution.py:308
  (4 shorter events, 0.1 us)
Async XLA Ops:
  0.6 1.3 %copy-start.1 = (bf16[1,1,2,16,64,128]{5,4,3,2,1,0:T(8,128)(2,1)S(1)}, bf16[1,1,2,16,64,128]{5,4,3,2,1,0:T(8,128)(2,1)}, u32[]{:S(2)}) copy-start(bf16[1,1,2,16,64,128]{5,4,3,2,1,0:T(8,128)(2,1)} %param.11) | copy-start | bytes 1572868
  0.6 1.3 %copy-start = (bf16[1,1,2,16,64,128]{5,4,3,2,1,0:T(8,128)(2,1)S(1)}, bf16[1,1,2,16,64,128]{5,4,3,2,1,0:T(8,128)(2,1)}, u32[]{:S(2)}) copy-start(bf16[1,1,2,16,64,128]{5,4,3,2,1,0:T(8,128)(2,1)} %param.6) | copy-start | bytes 1572868
  1.9 5.4 %copy-start.4 = (bf16[3,3,3,128]{3,2,1,0:T(4,128)(2,1)S(1)}, bf16[3,3,3,128]{3,2,1,0:T(4,128)(2,1)}, u32[]{:S(2)}) copy-start(bf16[3,3,3,128]{3,2,1,0:T(4,128)(2,1)} %param.7) | copy-start | bytes 20740
  1.9 5.5 %copy-start.5 = (bf16[3,3,3,128]{3,2,1,0:T(4,128)(2,1)S(1)}, bf16[3,3,3,128]{3,2,1,0:T(4,128)(2,1)}, u32[]{:S(2)}) copy-start(bf16[3,3,3,128]{3,2,1,0:T(4,128)(2,1)} %param.9) | copy-start | bytes 20740
  1.9 5.5 %copy-start.2 = (bf16[128,128]{1,0:T(8,128)(2,1)S(1)}, bf16[128,128]{1,0:T(8,128)(2,1)}, u32[]{:S(2)}) copy-start(bf16[128,128]{1,0:T(8,128)(2,1)} %p2.5) | copy-start | bytes 98308
  1.9 5.5 %copy-start.3 = (bf16[128,128]{1,0:T(8,128)(2,1)S(1)}, bf16[128,128]{1,0:T(8,128)(2,1)}, u32[]{:S(2)}) copy-start(bf16[128,128]{1,0:T(8,128)(2,1)} %p1.9) | copy-start | bytes 98308
  2.1 6.2 %collective-permute-start.1 = (bf16[2,1024,128]{2,1,0:T(8,128)(2,1)S(1)}, bf16[2,1024,128]{2,1,0:T(8,128)(2,1)S(1)}, u32[]{:S(2)}, u32[]{:S(2)}) collective-permute-start(bf16[2,1024,128]{2,1,0:T(8,128)(2,1)S(1)} %pad_maximum_fusion.1), channel_id=1, source_target_pairs={{0,4},{4,0},{1,5},{5,1},{2,6},{6,2},{3,7},{7,3},{8,12},{12,8},{9,1... | collective-permute-start | bytes 1572872 | tf_op jit(solution)/shard_map/ppermute | solution.py:324
  5.4 10.5 %collective-permute-start = (bf16[2,1024,128]{2,1,0:T(8,128)(2,1)S(1)}, bf16[2,1024,128]{2,1,0:T(8,128)(2,1)S(1)}, u32[]{:S(2)}, u32[]{:S(2)}) collective-permute-start(bf16[2,1024,128]{2,1,0:T(8,128)(2,1)S(1)} %pad_maximum_fusion), channel_id=1, source_target_pairs={{4,8},{12,16},{20,24},{28,32},{36,40},{44,48},{52,56},{60,64},{68,... | collective-permute-start | bytes 1572872 | tf_op jit(solution)/shard_map/ppermute | solution.py:330
  37.7 12.0 %all-to-all-start.1 = ((f32[8,1,1280]{2,1,0:T(1,128)}), f32[8,1,1280]{2,1,0:T(1,128)S(1)}, u32[]{:S(2)}, u32[]{:S(2)}) async-start(f32[8,1,1280]{2,1,0:T(1,128)} %broadcast_in_dim.3), calls=%async_computation.1 | async-start | bytes 81920 | tf_op jit(solution)/shard_map/all_to_all | solution.py:341
  42.8 14.8 %collective-permute-start.3 = (bf16[1024,128]{1,0:T(8,128)(2,1)S(1)}, bf16[1024,128]{1,0:T(8,128)(2,1)S(1)}, u32[]{:S(2)}, u32[]{:S(2)}) collective-permute-start(bf16[1024,128]{1,0:T(8,128)(2,1)S(1)} %get-tuple-element.43.outer), channel_id=1, source_target_pairs={{4,8},{12,16},{20,24},{28,32},{36,40},{44,48},{52,56},{60,64},{68,... | collective-permute-start | bytes 786440 | tf_op jit(solution)/shard_map/ppermute | solution.py:330
  46.7 10.9 %collective-permute-start.2 = (bf16[1024,128]{1,0:T(8,128)(2,1)S(1)}, bf16[1024,128]{1,0:T(8,128)(2,1)S(1)}, u32[]{:S(2)}, u32[]{:S(2)}) collective-permute-start(bf16[1024,128]{1,0:T(8,128)(2,1)S(1)} %get-tuple-element.42.inner), channel_id=1, source_target_pairs={{0,4},{4,0},{1,5},{5,1},{2,6},{6,2},{3,7},{7,3},{8,12},{12,8},{9,1... | collective-permute-start | bytes 786440 | tf_op jit(solution)/shard_map/ppermute | solution.py:324
  50.4 13.5 %all-to-all-start.2 = ((f32[32,1,1280]{2,1,0:T(1,128)}), f32[32,1,1280]{2,1,0:T(1,128)S(1)}, u32[]{:S(2)}, u32[]{:S(2)}) async-start(f32[32,1,1280]{2,1,0:T(1,128)} %shard_map.104), calls=%async_computation.2 | async-start | bytes 327680 | tf_op jit(solution)/shard_map/all_to_all | solution.py:350

commit v11 on v9

--- a/solution.py
+++ b/solution.py
@@ -12,7 +12,7 @@
 LINE = 64
 CELLS = 1024
 PADDED = CELLS + 2 * LINE
-ROWS = 256
+ROWS = 512
 TERMS = 320
 VMEM_LIMIT = 24 * 1024 * 1024
 

time: 65 us -> 65 us (level)
  no operation moved by 1% of the time
where the time goes in v11:
time: 65 us; the launch traced here: 64.6 us
  starting transfers between devices  22.4 us (34%)
  Pallas kernels  16 us (25%)
  waiting for transfers between devices  11.9 us (18%)
  blocking collectives  11.9 us (18%)
  local copies, waits for them, and re-layouts  1.32 us (2%)
  between operations  0.85 us (1%)
    pallas_call x7, Pallas kernels, call(): pl.pallas_call(kernel, out_shape=outs, in_specs=[smem if a.dtype == jnp.i...  16 us
    all_to_all x1, blocking collectives, reduced_around(): arrived = lax.all_to_all(copies, 'ring', 0, 0, tiled=True)  11.9 us
    all_to_all x1, starting transfers between devices, reduced_across(): return lax.all_to_all(tiles, ACROSS, 0, 0, tiled=True).sum(axis=0)  9.66 us
    all_to_all x1, waiting for transfers between devices, reduced_across(): return lax.all_to_all(tiles, ACROSS, 0, 0, tiled=True).sum(axis=0)  5.91 us
    all_to_all x1, starting transfers between devices, gathered_across(): return lax.all_to_all(copies, ACROSS, 0, 0, tiled=True).reshape(TERMS, CH)  5.48 us
    all_to_all x1, waiting for transfers between devices, gathered_across(): return lax.all_to_all(copies, ACROSS, 0, 0, tiled=True).reshape(TERMS, CH)  4.35 us
    ppermute x2, starting transfers between devices, with_other_chip(): return lax.ppermute(v, SPACE, pairs + [(j, i) for i, j in pairs])  3.83 us
    ppermute x2, starting transfers between devices, with_other_core(): return lax.ppermute(v, 'core', [(0, 1), (1, 0)])  3.42 us
  transfers between devices with their start and end apart: 6, of which 3 were waited for; matrix products, arithmetic and copies ran while one was open for 0% of the time, Pallas kernels for 17%

profile of v11, /device:TPU:1, one launch (start us, length us, event | category | flops | bytes accessed | tf_op | source)
XLA Modules:
  0.0 64.6 jit_solution(17644918463635661472)
XLA Ops:
  0.6 0.0 copy-start.1
  0.6 0.0 copy-start
  0.7 1.2 %constant_dynamic-slice_fusion.2 = (bf16[1,1024,128]{2,1,0:T(8,128)(2,1)S(1)}, bf16[1,1024,128]{2,1,0:T(8,128)(2,1)S(1)}) fusion(bf16[2,1024,128]{2,1,0:T(8,128)(2,1)} %bitcast.11, s32[]{:T(128)S(6)} %select_n.8, bf16[2,1024,128]{2,1,0:T(8,128)(2,1)} %bitcast.7), kind=kLoop, calls=%fused_computation.4 | loop fusion | bytes 1048580 | tf_op jit(solution)/shard_map/dynamic_slice | solution.py:366
  1.8 0.1 pad_maximum_fusion
  1.9 0.0 copy-start.4
  1.9 0.0 copy-start.5
  1.9 0.0 copy-start.2
  1.9 0.0 copy-start.3
  1.9 0.0 copy-done.1
  2.0 0.0 copy-done
  2.0 0.1 pad_maximum_fusion.1
  2.1 3.3 %collective-permute-start.1 = (bf16[2,1024,128]{2,1,0:T(8,128)(2,1)S(1)}, bf16[2,1024,128]{2,1,0:T(8,128)(2,1)S(1)}, u32[]{:S(2)}, u32[]{:S(2)}) collective-permute-start(bf16[2,1024,128]{2,1,0:T(8,128)(2,1)S(1)} %pad_maximum_fusion.1), channel_id=1, source_target_pairs={{0,4},{4,0},{1,5},{5,1},{2,6},{6,2},{3,7},{7,3},{8,12},{12,8},{9,1... | collective-permute-start | bytes 1572872 | tf_op jit(solution)/shard_map/ppermute | solution.py:324
  5.4 1.9 %collective-permute-start = (bf16[2,1024,128]{2,1,0:T(8,128)(2,1)S(1)}, bf16[2,1024,128]{2,1,0:T(8,128)(2,1)S(1)}, u32[]{:S(2)}, u32[]{:S(2)}) collective-permute-start(bf16[2,1024,128]{2,1,0:T(8,128)(2,1)S(1)} %pad_maximum_fusion), channel_id=1, source_target_pairs={{4,8},{12,16},{20,24},{28,32},{36,40},{44,48},{52,56},{60,64},{68,... | collective-permute-start | bytes 1572872 | tf_op jit(solution)/shard_map/ppermute | solution.py:330
  7.3 0.0 copy-done.4
  7.3 0.0 copy-done.5
  7.4 0.0 copy-done.2
  7.4 0.0 copy-done.3
  7.4 0.9 %shard_map.101 = (bf16[768,768]{1,0:T(8,128)(2,1)S(1)}, bf16[768,768]{1,0:T(8,128)(2,1)S(1)}, bf16[512,768]{1,0:T(8,128)(2,1)S(1)}, bf16[512,768]{1,0:T(8,128)(2...) custom-call(s32[1]{0:T(128)} %bitcast.parity, bf16[27,128]{1,0:T(8,128)(2,1)S(1)} %reshape.40.d1, ...), custom_call_target="tpu_custom_call" | custom-call | flops 1000000000 | bytes 5584388 | tf_op jit(solution)/shard_map/pallas_call | solution.py:308
  8.3 0.0 collective-permute-done.1.near
  8.3 5.9 %shard_map.102 = (bf16[1024,128]{1,0:T(8,128)(2,1)S(1)}, f32[1024,128]{1,0:T(8,128)S(1)}, f32[1024,128]{1,0:T(8,128)S(1)}, f32[320,128]{1,0:T(8,128)S(1)}) custom-call(s32[1]{0:T(128)} %bitcast.parity, bf16[2,1024,128]{2,1,0:T(8,128)(2,1)S(1)} %bitcast.9, bf16[2,1024,128]{2,1,0:T(8,128)(2,1)S(1)} %bitcast.13, ...), custom_call_target="tpu_custom_call" | custom-call | flops 6000000000 | bytes 7058948 | tf_op jit(solution)/shard_map/pallas_call | solution.py:308
  14.2 1.7 %collective-permute-done.far = bf16[2,1024,128]{2,1,0:T(8,128)(2,1)S(1)} collective-permute-done((bf16[2,1024,128]{2,1,0:T(8,128)(2,1)S(1)}, bf16[2,1024,128]{2,1,0:T(8,128)(2,1)S(1)}, u32[]{:S(2)}, u32[]{:S(2)}) %collective-permute-start) | collective-permute-done | bytes 524320 | tf_op jit(solution)/shard_map/ppermute | solution.py:330
  15.9 4.3 %shard_map.103 = (bf16[1024,128]{1,0:T(8,128)(2,1)S(1)}, f32[320,128]{1,0:T(8,128)}) custom-call(s32[1]{0:T(128)} %bitcast.parity, bf16[2,1024,128]{2,1,0:T(8,128)(2,1)S(1)} %bitcast.10, bf16[2,1024,128]{2,1,0:T(8,128)(2,1)S(1)} %bitcast.14, bf16[2,1024,128]{2,1,0:T(8,128)(2,1)S(1)} %collective-permute-done.far, f32[1024,128]{1,0:T(8,128)S(1)} %get-tuple-element.34.pre, ...), custom_call_target="tpu_custom_call" | custom-call | flops 4000000000 | bytes 4863492 | tf_op jit(solution)/shard_map/pallas_call | solution.py:308
  20.2 9.7 %all-to-all-start = ((f32[32,1,1280]{2,1,0:T(1,128)}), f32[32,1,1280]{2,1,0:T(1,128)S(1)}, u32[]{:S(2)}, u32[]{:S(2)}) async-start(f32[32,1,1280]{2,1,0:T(1,128)} %bitcast.3), calls=%async_computation | async-start | bytes 327680 | tf_op jit(solution)/shard_map/all_to_all | solution.py:336
  29.9 1.9 %collective-permute-start.3 = (bf16[1024,128]{1,0:T(8,128)(2,1)S(1)}, bf16[1024,128]{1,0:T(8,128)(2,1)S(1)}, u32[]{:S(2)}, u32[]{:S(2)}) collective-permute-start(bf16[1024,128]{1,0:T(8,128)(2,1)S(1)} %get-tuple-element.43.outer), channel_id=1, source_target_pairs={{4,8},{12,16},{20,24},{28,32},{36,40},{44,48},{52,56},{60,64},{68,... | collective-permute-start | bytes 786440 | tf_op jit(solution)/shard_map/ppermute | solution.py:330
  31.8 0.1 collective-permute-start.2
  31.9 5.9 %all-to-all-done = f32[32,1,1280]{2,1,0:T(1,128)S(1)} async-done(((f32[32,1,1280]{2,1,0:T(1,128)}), f32[32,1,1280]{2,1,0:T(1,128)S(1)}, u32[]{:S(2)}, u32[]{:S(2)}) %all-to-all-start) | async-done | bytes 163872 | tf_op jit(solution)/shard_map/all_to_all | solution.py:336
  37.8 0.1 reduce_sum.9
  37.9 11.9 %all_to_all.15.arrived = f32[8,1,1280]{2,1,0:T(1,128)S(1)} all-to-all(f32[8,1,1280]{2,1,0:T(1,128)S(1)} %broadcast_in_dim.3), channel_id=1, replica_groups=mesh['outer'=4,'ring'=8,'core'=2,'dp'=4] {'ring'}, dimensions={0} | all-to-all | bytes 81920 | tf_op jit(solution)/shard_map/all_to_all | solution.py:341
  49.8 0.7 %shard_map.104 = f32[32,1,1280]{2,1,0:T(1,128)} custom-call(f32[8,1,1280]{2,1,0:T(1,128)S(1)} %all_to_all.15.arrived), custom_call_target="tpu_custom_call" | custom-call | bytes 204800 | tf_op jit(solution)/shard_map/pallas_call | solution.py:308
  50.5 5.5 %all-to-all-start.2 = ((f32[32,1,1280]{2,1,0:T(1,128)}), f32[32,1,1280]{2,1,0:T(1,128)S(1)}, u32[]{:S(2)}, u32[]{:S(2)}) async-start(f32[32,1,1280]{2,1,0:T(1,128)} %shard_map.104), calls=%async_computation.2 | async-start | bytes 327680 | tf_op jit(solution)/shard_map/all_to_all | solution.py:350
  56.0 1.5 %shard_map.105.own = f32[2,1024,128]{2,1,0:T(8,128)S(1)} custom-call(s32[1]{0:T(128)} %bitcast.parity, bf16[1024,128]{1,0:T(8,128)(2,1)S(1)} %get-tuple-element.42.inner, bf16[1024,128]{1,0:T(8,128)(2,1)S(1)} %get-tuple-element.43.outer, bf16[27,128]{1,0:T(8,128)(2,1)S(1)} %reshape.40.d1, bf16[128,128]{1,0:T(8,128)(2,1)S(1)} %copy-done.3), custom_call_target="tpu_custom_call" | custom-call | flops 2000000000 | bytes 1612548 | tf_op jit(solution)/shard_map/pallas_call | solution.py:308
  57.5 0.0 collective-permute-done.3.far
  57.6 0.0 collective-permute-done.2.near
  57.6 2.0 %shard_map.106 = (bf16[2,1024,128]{2,1,0:T(8,128)(2,1)}, f32[8,128]{1,0:T(8,128)S(1)}) custom-call(s32[1]{0:T(128)} %bitcast.parity, f32[2,1024,128]{2,1,0:T(8,128)S(1)} %shard_map.105.own, bf16[1024,128]{1,0:T(8,128)(2,1)S(1)} %collective-permute-done.2.near, bf16[1024,128]{1,0:T(8,128)(2,1)S(1)} %collective-permute-done.3.far, ...), custom_call_target="tpu_custom_call" | custom-call | flops 2000000000 | bytes 2140932 | tf_op jit(solution)/shard_map/pallas_call | solution.py:308
  59.6 4.4 %all-to-all-done.2 = f32[32,1,1280]{2,1,0:T(1,128)S(1)} async-done(((f32[32,1,1280]{2,1,0:T(1,128)}), f32[32,1,1280]{2,1,0:T(1,128)S(1)}, u32[]{:S(2)}, u32[]{:S(2)}) %all-to-all-start.2) | async-done | bytes 163872 | tf_op jit(solution)/shard_map/all_to_all | solution.py:350
  63.9 0.7 %shard_map.107 = (f32[3,3,3,128]{3,2,1,0:T(4,128)}, f32[128,128]{1,0:T(8,128)}, f32[3,3,3,128]{3,2,1,0:T(4,128)}, f32[128,128]{1,0:T(8,128)}) custom-call(f32[320,128]{1,0:T(8,128)S(1)} %bitcast.6, f32[8,128]{1,0:T(8,128)S(1)} %get-tuple-element.46.done), custom_call_target="tpu_custom_call" | custom-call | bytes 326656 | tf_op jit(solution)/shard_map/pallas_call | solution.py:308
  (5 shorter events, 0.1 us)
Async XLA Ops:
  0.6 1.3 %copy-start.1 = (bf16[1,1,2,16,64,128]{5,4,3,2,1,0:T(8,128)(2,1)S(1)}, bf16[1,1,2,16,64,128]{5,4,3,2,1,0:T(8,128)(2,1)}, u32[]{:S(2)}) copy-start(bf16[1,1,2,16,64,128]{5,4,3,2,1,0:T(8,128)(2,1)} %param.11) | copy-start | bytes 1572868
  0.6 1.3 %copy-start = (bf16[1,1,2,16,64,128]{5,4,3,2,1,0:T(8,128)(2,1)S(1)}, bf16[1,1,2,16,64,128]{5,4,3,2,1,0:T(8,128)(2,1)}, u32[]{:S(2)}) copy-start(bf16[1,1,2,16,64,128]{5,4,3,2,1,0:T(8,128)(2,1)} %param.6) | copy-start | bytes 1572868
  1.9 5.4 %copy-start.4 = (bf16[3,3,3,128]{3,2,1,0:T(4,128)(2,1)S(1)}, bf16[3,3,3,128]{3,2,1,0:T(4,128)(2,1)}, u32[]{:S(2)}) copy-start(bf16[3,3,3,128]{3,2,1,0:T(4,128)(2,1)} %param.7) | copy-start | bytes 20740
  1.9 5.5 %copy-start.5 = (bf16[3,3,3,128]{3,2,1,0:T(4,128)(2,1)S(1)}, bf16[3,3,3,128]{3,2,1,0:T(4,128)(2,1)}, u32[]{:S(2)}) copy-start(bf16[3,3,3,128]{3,2,1,0:T(4,128)(2,1)} %param.9) | copy-start | bytes 20740
  1.9 5.5 %copy-start.2 = (bf16[128,128]{1,0:T(8,128)(2,1)S(1)}, bf16[128,128]{1,0:T(8,128)(2,1)}, u32[]{:S(2)}) copy-start(bf16[128,128]{1,0:T(8,128)(2,1)} %p2.5) | copy-start | bytes 98308
  1.9 5.5 %copy-start.3 = (bf16[128,128]{1,0:T(8,128)(2,1)S(1)}, bf16[128,128]{1,0:T(8,128)(2,1)}, u32[]{:S(2)}) copy-start(bf16[128,128]{1,0:T(8,128)(2,1)} %p1.9) | copy-start | bytes 98308
  2.1 6.2 %collective-permute-start.1 = (bf16[2,1024,128]{2,1,0:T(8,128)(2,1)S(1)}, bf16[2,1024,128]{2,1,0:T(8,128)(2,1)S(1)}, u32[]{:S(2)}, u32[]{:S(2)}) collective-permute-start(bf16[2,1024,128]{2,1,0:T(8,128)(2,1)S(1)} %pad_maximum_fusion.1), channel_id=1, source_target_pairs={{0,4},{4,0},{1,5},{5,1},{2,6},{6,2},{3,7},{7,3},{8,12},{12,8},{9,1... | collective-permute-start | bytes 1572872 | tf_op jit(solution)/shard_map/ppermute | solution.py:324
  5.4 10.5 %collective-permute-start = (bf16[2,1024,128]{2,1,0:T(8,128)(2,1)S(1)}, bf16[2,1024,128]{2,1,0:T(8,128)(2,1)S(1)}, u32[]{:S(2)}, u32[]{:S(2)}) collective-permute-start(bf16[2,1024,128]{2,1,0:T(8,128)(2,1)S(1)} %pad_maximum_fusion), channel_id=1, source_target_pairs={{4,8},{12,16},{20,24},{28,32},{36,40},{44,48},{52,56},{60,64},{68,... | collective-permute-start | bytes 1572872 | tf_op jit(solution)/shard_map/ppermute | solution.py:330
  20.2 17.6 %all-to-all-start = ((f32[32,1,1280]{2,1,0:T(1,128)}), f32[32,1,1280]{2,1,0:T(1,128)S(1)}, u32[]{:S(2)}, u32[]{:S(2)}) async-start(f32[32,1,1280]{2,1,0:T(1,128)} %bitcast.3), calls=%async_computation | async-start | bytes 327680 | tf_op jit(solution)/shard_map/all_to_all | solution.py:336
  29.9 27.7 %collective-permute-start.3 = (bf16[1024,128]{1,0:T(8,128)(2,1)S(1)}, bf16[1024,128]{1,0:T(8,128)(2,1)S(1)}, u32[]{:S(2)}, u32[]{:S(2)}) collective-permute-start(bf16[1024,128]{1,0:T(8,128)(2,1)S(1)} %get-tuple-element.43.outer), channel_id=1, source_target_pairs={{4,8},{12,16},{20,24},{28,32},{36,40},{44,48},{52,56},{60,64},{68,... | collective-permute-start | bytes 786440 | tf_op jit(solution)/shard_map/ppermute | solution.py:330
  31.8 25.8 %collective-permute-start.2 = (bf16[1024,128]{1,0:T(8,128)(2,1)S(1)}, bf16[1024,128]{1,0:T(8,128)(2,1)S(1)}, u32[]{:S(2)}, u32[]{:S(2)}) collective-permute-start(bf16[1024,128]{1,0:T(8,128)(2,1)S(1)} %get-tuple-element.42.inner), channel_id=1, source_target_pairs={{0,4},{4,0},{1,5},{5,1},{2,6},{6,2},{3,7},{7,3},{8,12},{12,8},{9,1... | collective-permute-start | bytes 786440 | tf_op jit(solution)/shard_map/ppermute | solution.py:324
  50.5 13.4 %all-to-all-start.2 = ((f32[32,1,1280]{2,1,0:T(1,128)}), f32[32,1,1280]{2,1,0:T(1,128)S(1)}, u32[]{:S(2)}, u32[]{:S(2)}) async-start(f32[32,1,1280]{2,1,0:T(1,128)} %shard_map.104), calls=%async_computation.2 | async-start | bytes 327680 | tf_op jit(solution)/shard_map/all_to_all | solution.py:350
